TPU v7x, 32 devices: a whole 2x2x4 slice. The times are simulated.
32 devices in a mesh: sp: 4 (over z), dp: 8 (over y, x, core).
Axes of the slice: x: 2, y: 2, z: 4, core: 2. Of those that a mesh axis runs over, the one named last changes fastest.
Arguments:
- tokens: bfloat16 [128, 32, 32, 384], P('dp', 'sp'), may hold values from -6 to 6
- extents: int32 [128, 2], P('dp'), may hold values from 16 to 32, as said below
- keep_mask: int32 [128], P('dp'), may hold values 0 or 1
- cotangent: bfloat16 [128, 16, 16, 768], P('dp', 'sp'), may hold values from -6 to 6
- dw_kernel: float32 [7, 7, 384], replicated, may hold values from -0.875 to 0.875
- dw_bias: float32 [384], replicated, may hold values from -3 to 3
- norm_gain: float32 [384], replicated, may hold values from 0.25 to 1.75
- norm_bias: float32 [384], replicated, may hold values from -2 to 2
- expand_weight: bfloat16 [384, 1536], replicated, may hold values from -0.3125 to 0.3125
- expand_bias: float32 [1536], replicated, may hold values from -2 to 2
- project_weight: bfloat16 [1536, 384], replicated, may hold values from -0.15625 to 0.15625
- project_bias: float32 [384], replicated, may hold values from -2 to 2
- layer_scale: float32 [384], replicated, may hold values from 0.5 to 2
- down_gain: float32 [384], replicated, may hold values from 0.25 to 1.75
- down_shift: float32 [384], replicated, may hold values from -2 to 2
- down_weight: bfloat16 [2, 2, 384, 768], replicated, may hold values from -0.15625 to 0.15625
- down_bias: float32 [768], replicated, may hold values from -2 to 2
Outputs:
- downsampled: bfloat16 [128, 16, 16, 768], P('dp', 'sp')
- input_grad: bfloat16 [128, 32, 32, 384], P('dp', 'sp')
- grad_dw_kernel: float32 [7, 7, 384], replicated
- grad_dw_bias: float32 [384], replicated
- grad_norm_gain: float32 [384], replicated
- grad_norm_bias: float32 [384], replicated
- grad_expand_weight: float32 [384, 1536], replicated
- grad_expand_bias: float32 [1536], replicated
- grad_project_weight: float32 [1536, 384], replicated
- grad_project_bias: float32 [384], replicated
- grad_layer_scale: float32 [384], replicated
- grad_down_gain: float32 [384], replicated
- grad_down_shift: float32 [384], replicated
- grad_down_weight: float32 [2, 2, 384, 768], replicated
- grad_down_bias: float32 [768], replicated
Inputs may be any that keep to these rules, and one draw needn't show every extreme that they name: extents[b] holds the valid rows (at least 16) and valid columns (at least 16) of image b; among the 16 images of each index of dp, one chosen by the seed has all 32 rows valid.
All inputs are finite; a program needn't handle non-finite values. No bound on the sum of `keep_mask` on one device may be relied on, other than what follows from the above.
Results may differ from a plain program's by a relative error of at most 0.0072.
Values may be sent and summed in bfloat16 or wider, within the bound.
A program may use at most 192 MiB of HBM per device.

v0:
```python
import jax
import jax.numpy as jnp
from jax import lax
from jax.sharding import PartitionSpec as P

epsilon = 1e-06
survival = 0.875


def inside(extents, row_total, col_total, stride):
    row_index = stride * jnp.arange(row_total, dtype=jnp.int32)
    col_index = stride * jnp.arange(col_total, dtype=jnp.int32)
    inside_mask = (row_index[None, :, None] < extents[:, 0][:, None, None]) & (
        col_index[None, None, :] < extents[:, 1][:, None, None]
    )
    return inside_mask.astype(jnp.float32)[..., None]


def depthwise(padded, kernel):
    row_total = padded.shape[1] - 6
    col_total = padded.shape[2]
    widened = jnp.pad(padded, ((0, 0), (0, 0), (3, 3), (0, 0)))
    running = jnp.zeros((padded.shape[0], row_total, col_total, padded.shape[3]), jnp.float32)
    for row_tap in range(7):
        for col_tap in range(7):
            running = (
                running
                + widened[:, row_tap : row_tap + row_total, col_tap : col_tap + col_total, :]
                * kernel[row_tap, col_tap]
            )
    return running


def kernel_grad(padded, gradient):
    row_total, col_total = (gradient.shape[1], gradient.shape[2])
    widened = jnp.pad(padded, ((0, 0), (0, 0), (3, 3), (0, 0)))
    tap_sums = [
        jnp.sum(
            widened[:, row_tap : row_tap + row_total, col_tap : col_tap + col_total, :] * gradient,
            axis=(0, 1, 2),
        )
        for row_tap in range(7)
        for col_tap in range(7)
    ]
    return jnp.stack(tap_sums).reshape(7, 7, gradient.shape[3])


def normalize(values):
    average = jnp.mean(values, axis=-1, keepdims=True)
    centred = values - average
    inverse = lax.rsqrt(jnp.mean(centred * centred, axis=-1, keepdims=True) + epsilon)
    return (centred * inverse, inverse)


def normalize_back(grad_hat, normed_hat, inverse):
    return inverse * (
        grad_hat
        - jnp.mean(grad_hat, axis=-1, keepdims=True)
        - normed_hat * jnp.mean(grad_hat * normed_hat, axis=-1, keepdims=True)
    )


def gelu_slope(values):
    return (
        0.5 * (1.0 + lax.erf(values * 0.7071067811865476))
        + values * jnp.exp(-0.5 * values * values) * 0.3989422804014327
    )


def per_device(
    tokens,
    extents,
    keep_mask,
    cotangent,
    dw_kernel,
    dw_bias,
    norm_gain,
    norm_bias,
    expand_weight,
    expand_bias,
    project_weight,
    project_bias,
    layer_scale,
    down_gain,
    down_shift,
    down_weight,
    down_bias,
):
    field, upstream = (
        lax.all_to_all(tokens, "sp", split_axis=0, concat_axis=1, tiled=True),
        lax.all_to_all(cotangent, "sp", split_axis=0, concat_axis=1, tiled=True),
    )
    own_count = field.shape[0]
    offset = lax.axis_index("sp") * own_count
    own_extents = lax.dynamic_slice_in_dim(extents, offset, own_count, 0)
    own_keep = lax.dynamic_slice_in_dim(keep_mask, offset, own_count, 0)
    img_count, height, across, channels = field.shape
    pixel_mask = inside(own_extents, height, across, 1)
    coarse_mask = inside(own_extents, height // 2, across // 2, 2)
    flat_pixel = pixel_mask.reshape(-1, 1)
    coarse_flat = coarse_mask.reshape(-1, 1)
    masked = field * pixel_mask.astype(jnp.bfloat16)
    padded = jnp.pad(masked, ((0, 0), (3, 3), (0, 0), (0, 0)))
    padded = padded.astype(jnp.float32)
    mixed = (depthwise(padded, dw_kernel) + dw_bias).reshape(-1, channels)
    first_hat, first_inv = normalize(mixed)
    normed = (first_hat * norm_gain + norm_bias).astype(jnp.bfloat16)
    hidden = jnp.dot(normed, expand_weight, preferred_element_type=jnp.float32) + expand_bias
    activated = jax.nn.gelu(hidden, approximate=False).astype(jnp.bfloat16)
    branch = jnp.dot(activated, project_weight, preferred_element_type=jnp.float32) + project_bias
    factor = (pixel_mask * (own_keep.astype(jnp.float32) / survival)[:, None, None, None]).reshape(
        -1, 1
    )
    residual = masked.astype(jnp.float32).reshape(-1, channels) + factor * layer_scale * branch
    second_hat, second_inv = normalize(residual)
    reduced = ((second_hat * down_gain + down_shift) * flat_pixel).astype(jnp.bfloat16)
    patches = (
        reduced.reshape(img_count, height // 2, 2, across // 2, 2, channels)
        .transpose(0, 1, 3, 2, 4, 5)
        .reshape(-1, 4 * channels)
    )
    kernel_flat = down_weight.reshape(4 * channels, -1)
    outward = (
        jnp.dot(patches, kernel_flat, preferred_element_type=jnp.float32) + down_bias
    ) * coarse_flat
    result = outward.astype(jnp.bfloat16).reshape(img_count, height // 2, across // 2, -1)
    upward = upstream.reshape(-1, upstream.shape[-1]) * coarse_flat.astype(jnp.bfloat16)
    grad_down_weight = jnp.dot(patches.T, upward, preferred_element_type=jnp.float32).reshape(
        down_weight.shape
    )
    grad_down_bias = jnp.sum(upward.astype(jnp.float32), axis=0)
    grad_patches = jnp.dot(upward, kernel_flat.T, preferred_element_type=jnp.float32)
    grad_reduced = (
        grad_patches.reshape(img_count, height // 2, across // 2, 2, 2, channels)
        .transpose(0, 1, 3, 2, 4, 5)
        .reshape(-1, channels)
        * flat_pixel
    )
    grad_down_gain = jnp.sum(grad_reduced * second_hat, axis=0)
    grad_down_shift = jnp.sum(grad_reduced, axis=0)
    grad_residual = normalize_back(grad_reduced * down_gain, second_hat, second_inv)
    grad_layer_scale = jnp.sum(grad_residual * factor * branch, axis=0)
    grad_branch = (grad_residual * factor * layer_scale).astype(jnp.bfloat16)
    grad_project_weight = jnp.dot(activated.T, grad_branch, preferred_element_type=jnp.float32)
    grad_project_bias = jnp.sum(grad_branch.astype(jnp.float32), axis=0)
    grad_activated = jnp.dot(grad_branch, project_weight.T, preferred_element_type=jnp.float32)
    grad_hidden = (grad_activated * gelu_slope(hidden)).astype(jnp.bfloat16)
    grad_expand_weight = jnp.dot(normed.T, grad_hidden, preferred_element_type=jnp.float32)
    grad_expand_bias = jnp.sum(grad_hidden.astype(jnp.float32), axis=0)
    grad_normed = jnp.dot(grad_hidden, expand_weight.T, preferred_element_type=jnp.float32)
    grad_norm_gain = jnp.sum(grad_normed * first_hat, axis=0)
    grad_norm_bias = jnp.sum(grad_normed, axis=0)
    grad_mixed = normalize_back(grad_normed * norm_gain, first_hat, first_inv)
    grad_dw_bias = jnp.sum(grad_mixed, axis=0)
    grad_field = grad_mixed.reshape(field.shape)
    grad_padded = jnp.pad(grad_field, ((0, 0), (3, 3), (0, 0), (0, 0)))
    grad_dw_kernel = kernel_grad(padded, grad_field)
    grad_masked = depthwise(grad_padded, dw_kernel[::-1, ::-1])
    input_grad = ((grad_residual.reshape(field.shape) + grad_masked) * pixel_mask).astype(
        jnp.bfloat16
    )
    all_sums = lax.psum(
        (
            grad_dw_kernel,
            grad_dw_bias,
            grad_norm_gain,
            grad_norm_bias,
            grad_expand_weight,
            grad_expand_bias,
            grad_project_weight,
            grad_project_bias,
            grad_layer_scale,
            grad_down_gain,
            grad_down_shift,
            grad_down_weight,
            grad_down_bias,
        ),
        ("sp", "dp"),
    )
    result_out, grad_out = (
        lax.all_to_all(result, "sp", split_axis=1, concat_axis=0, tiled=True),
        lax.all_to_all(input_grad, "sp", split_axis=1, concat_axis=0, tiled=True),
    )
    return (result_out, grad_out) + tuple(all_sums)


def solution(mesh):
    placed = (
        P("dp", "sp", None, None),
        P("dp", None),
        P("dp"),
        P("dp", "sp", None, None),
        P(),
        P(),
        P(),
        P(),
        P(),
        P(),
        P(),
        P(),
        P(),
        P(),
        P(),
        P(),
        P(),
    )
    return jax.shard_map(
        per_device,
        mesh=mesh,
        in_specs=placed,
        out_specs=(
            P("dp", "sp", None, None),
            P("dp", "sp", None, None),
            P(),
            P(),
            P(),
            P(),
            P(),
            P(),
            P(),
            P(),
            P(),
            P(),
            P(),
            P(),
            P(),
        ),
        check_vma=False,
    )
```

profile of v0, /device:TPU:0, one launch (start us, length us, event | category | flops | bytes accessed | tf_op | source)
XLA Modules:
  0.0 934.1 jit_solution(5302992230647694243)
XLA Ops:
  7.2 43.5 %all_to_all.72 = bf16[16,4,16,768]{3,2,1,0:T(8,128)(2,1)} all-to-all(bf16[16,4,16,768]{3,2,1,0:T(8,128)(2,1)} %param.20), channel_id=1, replica_groups=mesh['sp'=4,'dp'=8] {'sp'}, dimensions={0} | all-to-all | bytes 3145728 | tf_op jit(solution)/shard_map/all_to_all | solution.py:91
  50.8 4.8 all-to-all-start
  55.9 0.7 copy.269
  56.7 0.1 copy.262
  57.0 0.7 reshape.518
  57.8 0.7 mul.1201
  58.5 0.6 copy.252
  59.1 0.6 convert_element_type.111
  59.7 0.6 slice_reduce_fusion.46
  60.4 0.7 slice_reduce_fusion.48
  61.1 0.7 slice_reduce_fusion.47
  62.0 0.2 and_convert_fusion
  62.2 2.4 convert_reduce_fusion.2
  64.6 0.1 copy.260
  64.7 5.6 multiply_reduce_fusion.57
  70.3 0.8 copy.265
  71.2 1.1 div.38
  72.2 8.9 copy.261
  81.1 8.5 reshape.513
  89.6 35.8 %all-to-all-done = bf16[16,8,32,384]{3,2,1,0:T(8,128)(2,1)} async-done(((bf16[16,8,32,384]{3,2,1,0:T(8,128)(2,1)}), bf16[16,8,32,384]{3,2,1,0:T(8,128)(2,1)}, u32[]{:S(2)}, u32[]{:S(2)}) %all-to-all-start) | async-done | bytes 3145760 | tf_op jit(solution)/shard_map/all_to_all | solution.py:90
  125.5 2.5 copy.251
  127.9 1.1 bitcast_multiply_fusion.1
  129.4 4.0 pad_convert_fusion
  133.8 155.1 %fusion.115 = (f32[4,32,32]{2,0,1:T(4,128)S(1)}, f32[4,32,32,384]{3,2,0,1:T(8,128)}) fusion(f32[384]{0:T(512)} %param.22, f32[384]{0:T(512)S(1)} %copy-done.35, f32[384]{0:T(512)S(1)} %copy-done.37, f32[384]{0:T(512)S(1)} %copy-done.41, f32[384]{0:T(512)S(1)} %copy-done.43, f32[4,38,32,384]{3,2,0,1:T(8,128)} %pad_convert_fusion, f32[384]{0:T(512)S(1)} %copy-done.45, ...), kind=kLoop, calls=%fused_computation.363 | loop fusion | flops 155709440 | bytes 57899520 | tf_op jit(solution)/shard_map/reduce_sum | solution.py:49
  289.1 4.1 copy.250
  293.3 3.1 copy.253
  296.4 1.4 multiply_reduce_fusion.56
  298.0 3.6 add_convert_fusion
  301.7 61.4 %fusion.2 = (bf16[4096,1536]{1,0:T(8,128)(2,1)}, f32[4096,1536]{1,0:T(8,128)}) fusion(f32[1536]{0:T(1024)S(1)} %copy-done.115, bf16[4096,384]{1,0:T(8,128)(2,1)S(1)} %add_convert_fusion, bf16[384,1536]{1,0:T(8,128)(2,1)S(1)} %copy-done.113), kind=kOutput, calls=%fused_computation.4 | convolution fusion | flops 5247074304 | bytes 42080256 | tf_op jit(solution)/shard_map/dot_general | solution.py:108
  363.1 12.3 %fusion.114 = (f32[4096]{0:T(1024)S(1)}, f32[4096,384]{1,0:T(8,128)S(1)}, f32[4096,384]{1,0:T(8,128)S(1)}) fusion(f32[384]{0:T(512)S(1)} %copy-done.107, f32[384]{0:T(512)S(1)} %copy-done.109, f32[4096]{0:T(1024)S(1)} %copy-done.9, bf16[4096]{0:T(1024)(128)(2,1)S(1)} %copy-done.102, bf16[4,4,8,32,384]{4,3,2,0,1:T(8,128)(2,1)} %copy.250, ...), kind=kOutput, calls=%fused_computation.362 | convolution fusion | flops 4842844160 | bytes 29535232 | tf_op jit(solution)/shard_map/dot_general | solution.py:110
  375.4 1.4 multiply_reduce_fusion.55
  376.9 2.6 multiply_reduce_fusion
  379.5 5.7 multiply_reduce_fusion.1
  385.2 2.6 copy-done.2
  387.8 1.0 convert_reduce_fusion.1
  388.8 10.8 %fusion.117 = f32[1536,384]{1,0:T(8,128)} fusion(bf16[4096,1536]{1,0:T(8,128)(2,1)} %get-tuple-element.156, bf16[4096,384]{1,0:T(8,128)(2,1)S(1)} %get-tuple-element.139), kind=kOutput, calls=%fused_computation.365 | convolution fusion | flops 4831838208 | bytes 18087936 | tf_op jit(solution)/shard_map/dot_general | solution.py:144
  399.7 17.5 %convert_reduce_fusion = (f32[1536]{0:T(1024)S(1)}, bf16[4096,1536]{1,0:T(8,128)(2,1)}) fusion(f32[4096,1536]{1,0:T(8,128)} %get-tuple-element.157, f32[1536]{0:T(1024)S(1)} %copy-done.115, bf16[4096,384]{1,0:T(8,128)(2,1)S(1)} %get-tuple-element.139, bf16[1536,384]{1,0:T(8,128)(2,1)S(1)} %copy-done.112), kind=kOutput, calls=%fused_computation.11 | convolution fusion | flops 4913625600 | bytes 42086400 | tf_op jit(solution)/shard_map/dot_general | solution.py:146
  417.3 9.6 %fusion.116 = f32[384,1536]{1,0:T(8,128)} fusion(bf16[4096,384]{1,0:T(8,128)(2,1)S(1)} %copy-done.4, bf16[4096,1536]{1,0:T(8,128)(2,1)} %get-tuple-element.162), kind=kOutput, calls=%fused_computation.364 | convolution fusion | flops 4831838208 | bytes 18087936 | tf_op jit(solution)/shard_map/dot_general | solution.py:148
  426.9 10.8 %multiply_reduce_fusion.2 = (f32[384]{0:T(512)S(1)}, f32[4096]{0:T(1024)S(1)}, f32[4096]{0:T(1024)S(1)}, f32[384]{0:T(512)S(1)}, f32[4096,384]{1,0:T(8,128)S(1)}) fusion(f32[4,32,32,384]{3,2,1,0:T(8,128)S(1)} %bitcast.95, f32[4096]{0:T(1024)S(1)} %copy-done.13, f32[4096]{0:T(1024)S(1)} %copy-done.11, f32[384]{0:T(512)S(1)} %copy-done.104, ...), kind=kOutput, calls=%fused_computation.208 | convolution fusion | flops 4845984768 | bytes 26415616 | tf_op jit(solution)/shard_map/dot_general | solution.py:150
  437.7 5.6 fusion.113
  443.3 38.4 %multiply_reduce_fusion.5 = (f32[384]{0:T(512)S(1)}, f32[384]{0:T(512)S(1)}, f32[384]{0:T(512)S(1)}, f32[384]{0:T(512)S(1)}, f32[384]{0:T(512)S(1)}, /*index=5*/...) fusion(f32[4,38,32,384]{3,2,0,1:T(8,128)} %pad_convert_fusion, ...), kind=kLoop, calls=%fused_computation.211 | loop fusion | flops 40889472 | bytes 51531264 | tf_op jit(solution)/shard_map/reduce_sum | solution.py:38
  481.7 50.2 %multiply_reduce_fusion.3 = (f32[384]{0:T(512)S(1)}, f32[384]{0:T(512)S(1)}, f32[384]{0:T(512)S(1)}, f32[384]{0:T(512)S(1)}, f32[384]{0:T(512)S(1)}, /*index=5*/...) fusion(f32[4,38,32,384]{3,2,0,1:T(8,128)} %pad_convert_fusion, ...), kind=kLoop, calls=%fused_computation.209 | loop fusion | flops 56616192 | bytes 20081664 | tf_op jit(solution)/shard_map/reduce_sum | solution.py:38
  532.0 51.2 %multiply_reduce_fusion.4 = (f32[384]{0:T(512)S(1)}, f32[384]{0:T(512)S(1)}, f32[384]{0:T(512)S(1)}, f32[384]{0:T(512)S(1)}, f32[384]{0:T(512)S(1)}, /*index=5*/...) fusion(f32[4,38,32,384]{3,2,0,1:T(8,128)} %pad_convert_fusion, ...), kind=kLoop, calls=%fused_computation.210 | loop fusion | flops 56616192 | bytes 20081664 | tf_op jit(solution)/shard_map/reduce_sum | solution.py:38
  583.2 7.5 reshape.509
  590.6 6.3 copy.387
  596.9 8.0 reshape.510
  604.9 4.5 multiply_convert_fusion.2
  609.4 1.3 copy.258
  610.7 4.3 all-to-all-start.1
  615.1 4.9 copy.326
  620.5 0.2 stack.199
  620.7 0.7 reshape.516
  621.4 7.2 fusion.118
  628.5 6.7 pad.18
  635.7 0.4 copy-done.8
  636.5 143.6 %fusion.105 = bf16[4,32,32,384]{3,2,0,1:T(8,128)(2,1)} fusion(f32[4,38,32,384]{3,2,0,1:T(8,128)} %pad.18, f32[4,32,32,384]{3,2,1,0:T(8,128)} %bitcast.93, f32[4,32,32]{2,0,1:T(4,128)S(1)} %copy-done.8, f32[384]{0:T(512)S(1)} %copy-done.36, f32[384]{0:T(512)S(1)} %copy-done.38, f32[384]{0:T(512)S(1)} %copy-done.42, f32[384]{0:T(512)S(1)} %copy-done.44, ...), kind=kLoop, calls=%fused_computation.200 | loop fusion | flops 157286400 | bytes 61045248 | tf_op jit(solution)/shard_map/convert_element_type | solution.py:159
  780.1 5.0 all-to-all-start.3
  785.1 124.5 %all-reduce.4 = (f32[384]{0:T(512)}, f32[384]{0:T(512)}, f32[384]{0:T(512)}, f32[1536]{0:T(1024)}, f32[384]{0:T(512)}, /*index=5*/f32[384]{0:T(512)}, f32[384]{0:T(512)}, f32[384]{0:T(512)}, f32[768]{0:T(1024)}) all-reduce(f32[384]{0:T(512)S(1)} %get-tuple-element.140, ...), channel_id=1, replica_groups=mesh['sp'=4,'dp'=8] {'sp','dp'}, use_global_device_ids=true, to_apply=%region_59.60 | all-reduce | flops 4992 | bytes 39936 | tf_op jit(solution)/shard_map/psum | solution.py:162
  909.7 2.7 copy.259
  912.4 4.1 copy.270
  916.5 1.7 copy.392
  918.2 3.3 copy.393
  921.4 3.2 copy.394
  924.7 2.2 copy.395
  (330 shorter events, 2.0 us)
Async XLA Ops:
  7.2 57.5 %copy-start = (bf16[2,2,384,768]{3,2,1,0:T(8,128)(2,1)S(1)}, bf16[2,2,384,768]{3,2,1,0:T(8,128)(2,1)}, u32[]{:S(2)}) copy-start(bf16[2,2,384,768]{3,2,1,0:T(8,128)(2,1)} %param.32) | copy-start | bytes 7077892
  7.2 48.4 %copy-start.111 = (s32[16,2]{0,1:T(2,128)S(1)}, s32[16,2]{0,1:T(2,128)}, u32[]{:S(2)}) copy-start(s32[16,2]{0,1:T(2,128)} %param.18) | copy-start | bytes 388
  7.2 50.4 %copy-start.117 = (s32[16]{0:T(128)S(1)}, s32[16]{0:T(128)}, u32[]{:S(2)}) copy-start(s32[16]{0:T(128)} %param.19) | copy-start | bytes 196
  7.2 52.5 %copy-start.15 = (f32[7,7,384]{2,1,0:T(8,128)S(1)}, f32[7,7,384]{2,1,0:T(8,128)}, u32[]{:S(2)}) copy-start(f32[7,7,384]{2,1,0:T(8,128)} %param.21) | copy-start | bytes 225796
  50.8 14.0 %copy-start.100 = (f32[384]{0:T(512)S(1)}, f32[384]{0:T(512)}, u32[]{:S(2)}) copy-start(f32[384]{0:T(512)} %param.30) | copy-start | bytes 4612
  50.8 74.7 %all-to-all-start = ((bf16[16,8,32,384]{3,2,1,0:T(8,128)(2,1)}), bf16[16,8,32,384]{3,2,1,0:T(8,128)(2,1)}, u32[]{:S(2)}, u32[]{:S(2)}) async-start(bf16[16,8,32,384]{3,2,1,0:T(8,128)(2,1)} %param.17), calls=%async_computation | async-start | bytes 6291456 | tf_op jit(solution)/shard_map/all_to_all | solution.py:90
  55.9 14.4 %copy-start.6 = (f32[4096]{0:T(1024)}, f32[4096]{0:T(1024)S(1)}, u32[]{:S(2)}) copy-start(f32[4096]{0:T(1024)S(1)} %reshape.517) | copy-start | bytes 49156
  60.4 73.0 %copy-start.17 = (f32[384]{0:T(512)}, f32[384]{0:T(512)S(1)}, u32[]{:S(2)}) copy-start(f32[384]{0:T(512)S(1)} %get-tuple-element.110) | copy-start | bytes 4612
  60.4 73.0 %copy-start.19 = (f32[384]{0:T(512)}, f32[384]{0:T(512)S(1)}, u32[]{:S(2)}) copy-start(f32[384]{0:T(512)S(1)} %get-tuple-element.111) | copy-start | bytes 4612
  60.4 73.0 %copy-start.21 = (f32[384]{0:T(512)}, f32[384]{0:T(512)S(1)}, u32[]{:S(2)}) copy-start(f32[384]{0:T(512)S(1)} %get-tuple-element.112) | copy-start | bytes 4612
  60.4 73.0 %copy-start.23 = (f32[384]{0:T(512)}, f32[384]{0:T(512)S(1)}, u32[]{:S(2)}) copy-start(f32[384]{0:T(512)S(1)} %get-tuple-element.113) | copy-start | bytes 4612
  64.7 5.6 copy-start.5
  89.6 38.3 %copy-start.14 = (bf16[4,32,32]{2,0,1:T(4,128)(2,1)S(1)}, bf16[4,32,32]{2,0,1:T(4,128)(2,1)}, u32[]{:S(2)}) copy-start(bf16[4,32,32]{2,0,1:T(4,128)(2,1)} %copy.252) | copy-start | bytes 24580
  129.0 4.4 copy-start.25
  129.0 4.4 copy-start.27
  129.0 4.4 copy-start.29
  129.0 4.4 copy-start.31
  129.1 4.4 copy-start.33
  129.1 4.4 copy-start.35
  129.1 4.4 copy-start.37
  129.1 4.4 copy-start.39
  129.1 4.4 copy-start.41
  129.1 4.4 copy-start.43
  129.1 4.4 copy-start.45
  129.1 4.4 copy-start.47
  129.1 4.4 copy-start.49
  129.2 4.4 copy-start.51
  129.2 4.4 copy-start.53
  129.2 4.4 copy-start.55
  129.2 4.4 copy-start.57
  129.2 4.4 copy-start.59
  129.2 4.4 copy-start.61
  129.2 4.4 copy-start.63
  129.2 4.4 copy-start.65
  129.2 4.4 copy-start.67
  129.2 4.4 copy-start.69
  129.3 4.4 copy-start.71
  129.3 4.4 copy-start.73
  289.0 8.9 copy-start.10
  298.0 65.1 %copy-start.12 = (f32[4096]{0:T(1024)}, f32[4096]{0:T(1024)S(1)}, u32[]{:S(2)}) copy-start(f32[4096]{0:T(1024)S(1)} %rsqrt.20) | copy-start | bytes 49156
  301.6 61.4 %copy-start.3 = (bf16[4096,384]{1,0:T(8,128)(2,1)}, bf16[4096,384]{1,0:T(8,128)(2,1)S(1)}, u32[]{:S(2)}) copy-start(bf16[4096,384]{1,0:T(8,128)(2,1)S(1)} %add_convert_fusion) | copy-start | bytes 9437188
  301.6 61.4 %copy-start.9 = (f32[4096]{0:T(1024)S(1)}, f32[4096]{0:T(1024)}, u32[]{:S(2)}) copy-start(f32[4096]{0:T(1024)} %mul.1201) | copy-start | bytes 49156
  301.6 61.4 %copy-start.102 = (bf16[4096]{0:T(1024)(128)(2,1)S(1)}, bf16[4096]{0:T(1024)(128)(2,1)}, u32[]{:S(2)}) copy-start(bf16[4096]{0:T(1024)(128)(2,1)} %convert_element_type.111) | copy-start | bytes 24580
  301.6 61.4 %copy-start.107 = (f32[384]{0:T(512)S(1)}, f32[384]{0:T(512)}, u32[]{:S(2)}) copy-start(f32[384]{0:T(512)} %param.28) | copy-start | bytes 4612
  301.6 61.4 %copy-start.109 = (f32[384]{0:T(512)S(1)}, f32[384]{0:T(512)}, u32[]{:S(2)}) copy-start(f32[384]{0:T(512)} %param.29) | copy-start | bytes 4612
  363.0 13.8 %slice-start.2 = ((s8[6291456]{0:T(1024)(128)(4,1)}), s8[4194304]{0:T(1024)(128)(4,1)S(1)}, s32[]{:S(2)}) async-start(s8[6291456]{0:T(1024)(128)(4,1)} %bitcast.96), calls=%async_computation.7 | async-start | bytes 8388608
  363.1 13.7 %slice-start.3 = ((s8[6291456]{0:T(1024)(128)(4,1)}), s8[2097152]{0:T(1024)(128)(4,1)S(1)}, s32[]{:S(2)}) async-start(s8[6291456]{0:T(1024)(128)(4,1)} %bitcast.96), calls=%async_computation.8 | async-start | bytes 4194304
  388.8 10.9 %copy-start.112 = (bf16[1536,384]{1,0:T(8,128)(2,1)S(1)}, bf16[1536,384]{1,0:T(8,128)(2,1)}, u32[]{:S(2)}) copy-start(bf16[1536,384]{1,0:T(8,128)(2,1)} %param.27) | copy-start | bytes 3538948
  388.8 38.1 %slice-start = ((s8[6291456]{0:T(1024)(128)(4,1)}), s8[4194304]{0:T(1024)(128)(4,1)S(1)}, s32[]{:S(2)}) async-start(s8[6291456]{0:T(1024)(128)(4,1)} %bitcast.94), calls=%async_computation.5 | async-start | bytes 8388608
  399.7 17.6 %copy-start.4 = (bf16[4096,384]{1,0:T(8,128)(2,1)S(1)}, bf16[4096,384]{1,0:T(8,128)(2,1)}, u32[]{:S(2)}) copy-start(bf16[4096,384]{1,0:T(8,128)(2,1)} %copy-done.3) | copy-start | bytes 9437188
  399.7 27.2 %slice-start.1 = ((s8[6291456]{0:T(1024)(128)(4,1)}), s8[2097152]{0:T(1024)(128)(4,1)S(1)}, s32[]{:S(2)}) async-start(s8[6291456]{0:T(1024)(128)(4,1)} %bitcast.94), calls=%async_computation.6 | async-start | bytes 4194304
  417.2 9.7 %copy-start.11 = (f32[4096]{0:T(1024)S(1)}, f32[4096]{0:T(1024)}, u32[]{:S(2)}) copy-start(f32[4096]{0:T(1024)} %copy-done.10) | copy-start | bytes 49156
  417.2 9.7 %copy-start.13 = (f32[4096]{0:T(1024)S(1)}, f32[4096]{0:T(1024)}, u32[]{:S(2)}) copy-start(f32[4096]{0:T(1024)} %copy-done.12) | copy-start | bytes 49156
  417.2 9.7 %copy-start.104 = (f32[384]{0:T(512)S(1)}, f32[384]{0:T(512)}, u32[]{:S(2)}) copy-start(f32[384]{0:T(512)} %param.23) | copy-start | bytes 4612
  417.3 9.7 %copy-start.114 = (bf16[384,1536]{1,0:T(8,128)(2,1)S(1)}, bf16[384,1536]{1,0:T(8,128)(2,1)}, u32[]{:S(2)}) copy-start(bf16[384,1536]{1,0:T(8,128)(2,1)} %param.25) | copy-start | bytes 3538948
  590.6 14.3 %copy-start.105 = (f32[1024]{0:T(1024)S(1)}, f32[1024]{0:T(1024)}, u32[]{:S(2)}) copy-start(f32[1024]{0:T(1024)} %reshape.518) | copy-start | bytes 12292
  590.6 14.3 %copy-start.116 = (f32[768]{0:T(1024)S(1)}, f32[768]{0:T(1024)}, u32[]{:S(2)}) copy-start(f32[768]{0:T(1024)} %param.33) | copy-start | bytes 9220
  610.7 169.4 %all-to-all-start.1 = ((bf16[4,16,16,768]{3,2,0,1:T(8,128)(2,1)}), bf16[4,16,16,768]{3,2,0,1:T(8,128)(2,1)}, u32[]{:S(2)}, u32[]{:S(2)}) async-start(bf16[4,16,16,768]{3,2,0,1:T(8,128)(2,1)} %copy.258), calls=%async_computation.1 | async-start | bytes 3145728 | tf_op jit(solution)/shard_map/all_to_all | solution.py:181
  615.1 301.4 %all-reduce.8.cloned.1.call-start = ((), (), s32[]{:S(2)}) async-start(), calls=%async_computation.4 | async-start | bytes 19046400 | tf_op jit(solution)/shard_map/psum | solution.py:162
  780.1 5.0 copy-start.99
  780.1 5.0 copy-start.110
  780.1 132.3 %all-to-all-start.3 = ((bf16[4,32,32,384]{3,2,0,1:T(8,128)(2,1)}), bf16[4,32,32,384]{3,2,0,1:T(8,128)(2,1)}, u32[]{:S(2)}, u32[]{:S(2)}) async-start(bf16[4,32,32,384]{3,2,0,1:T(8,128)(2,1)} %fusion.105), calls=%async_computation.3 | async-start | bytes 6291456 | tf_op jit(solution)/shard_map/all_to_all | solution.py:182
  916.5 8.2 slice-start.4
  918.2 6.5 slice-start.5
  (64 other events, 119.8 us)
Sparse Core Ops, SparseCore 0:
  635.8 263.4 all-reduce.7
where the time goes:
time: 943 us; the launch traced here: 934 us
  other arithmetic  469 us (50%)
  blocking collectives  168 us (18%)
  matrix products  140 us (15%)
  local copies, waits for them, and re-layouts  90.8 us (10%)
  waiting for transfers between devices  35.8 us (4%)
  between operations  16.8 us (2%)
  starting transfers between devices  14.2 us (2%)
    reduce_sum x1, other arithmetic, normalize(): average = jnp.mean(values, axis=-1, keepdims=True)  155 us
    convert_element_type x1, other arithmetic, per_device(): ((grad_residual.reshape(field.shape) + grad_masked) * pixel_mask).astype(...  144 us
    reduce_sum x3, other arithmetic, kernel_grad(): jnp.sum(widened[:, row_tap:row_tap + row_total, col_tap:col_tap + col_tot...  140 us
    psum x1, blocking collectives, per_device(): lax.psum((grad_dw_kernel, grad_dw_bias, grad_norm_gain, grad_norm_bias, g...  125 us
    dot_general x1, matrix products, per_device(): jnp.dot(normed, expand_weight, preferred_element_type=jnp.float32)  61.4 us
    all_to_all x1, blocking collectives, per_device(): lax.all_to_all(cotangent, 'sp', split_axis=0, concat_axis=1, tiled=True)  43.5 us
    all_to_all x1, waiting for transfers between devices, per_device(): lax.all_to_all(tokens, 'sp', split_axis=0, concat_axis=1, tiled=True)  35.8 us
  transfers between devices with their start and end apart: 4, of which 1 were waited for; matrix products, arithmetic and copies ran while one was open for 22% of the time, Pallas kernels for 0%

commit v1 on v0

v1 whole, which is shorter than its diff:
```python
import functools

import jax
import jax.numpy as jnp
import numpy as np
from jax import lax
from jax.experimental import pallas as pl
from jax.experimental.pallas import tpu as pltpu
from jax.sharding import PartitionSpec as P

bf16 = jnp.bfloat16
f32 = jnp.float32
epsilon = 1e-06
survival = 0.875
VMEM = 60 * 1024 * 1024


def tables(h, across):
    nr, nc = h + 6, across + 3
    us, vs, ms = [], [], []
    for v in range(nc // 2 + 1):
        for u in range(nr):
            mu, mv = (-u) % nr, (-v) % nc
            if (mv, mu) < (v, u):
                continue
            us.append(u)
            vs.append(v)
            ms.append(1.0 if (mu, mv) == (u, v) else 2.0)
    n = len(us)
    nf = -(-n // 128) * 128
    us, vs, ms = (np.array(a + [0] * (nf - n), np.float64) for a in (us, vs, ms))
    live = (np.arange(nf) < n)[:, None]

    def angle(r, c):
        turns = (np.outer(us, r.ravel()) * nc + np.outer(vs, c.ravel()) * nr) % (nr * nc)
        return 2 * np.pi * turns / (nr * nc)

    def waves(a):
        return np.concatenate([np.cos(a) * live, -np.sin(a) * live])

    r_all, c_all = np.meshgrid(np.arange(h + 6), np.arange(across), indexing="ij")
    p, q, i, j = np.meshgrid(
        np.arange(2), np.arange(2), np.arange(h // 2), np.arange(across // 2), indexing="ij"
    )
    r_own, c_own = (2 * i + p).ravel(), (2 * j + q).ravel()
    pick = np.zeros((h * across, (h + 6) * across))
    pick[np.arange(h * across), (r_own + 3) * across + c_own] = 1.0
    every, own = waves(angle(r_all, c_all)), waves(angle(r_own, c_own))
    ki, kj = np.meshgrid(np.arange(7), np.arange(7) - 3, indexing="ij")
    taps = angle(ki, kj)
    weight = (ms / (nr * nc))[:, None]
    spectrum = np.concatenate([np.cos(taps) * weight, np.sin(taps) * weight])
    back = np.concatenate([np.cos(taps) * weight, -np.sin(taps) * weight]).T
    back = np.pad(back, ((0, 7), (0, 0)))
    return (
        nf,
        np.concatenate([every, pick]),
        own.T,
        own,
        np.concatenate([every, pick]).T,
        spectrum,
        back,
    )


def dot(a, b):
    return jnp.dot(a, b, preferred_element_type=f32)


def dot_nt(a, b):
    return lax.dot_general(a, b, (((1,), (1,)), ((), ())), preferred_element_type=f32)


def dot_tn(a, b):
    return lax.dot_general(a, b, (((0,), (0,)), ((), ())), preferred_element_type=f32)


def mean(x):
    return jnp.sum(x, axis=-1, keepdims=True) * (1.0 / x.shape[-1])


def total(x):
    return jnp.sum(x, axis=0, keepdims=True)


def lanes(x, width):
    return jnp.concatenate([x] * (width // 128), axis=1)


def gelu_parts(v):
    e = jnp.exp(v * v * -0.5)
    t = 1.0 / (1.0 + jnp.abs(v) * (0.3275911 * 0.7071067811865476))
    q = (
        t
        * (
            0.127414796
            + t * (-0.142248368 + t * (0.7107068705 + t * (-0.7265760135 + t * 0.5307027145)))
        )
        * e
    )
    phi = jnp.where(v < 0.0, q, 1.0 - q)
    return v * phi, phi + v * e * 0.3989422804014327


class Masks:
    def __init__(self, h, across):
        n = lax.broadcasted_iota(jnp.int32, ((h + 6) * across, 128), 0)
        shift, low = across.bit_length() - 1, across - 1
        self.row, self.col = (n >> shift) - 3, n & low
        quarter = h * across // 4
        m = lax.broadcasted_iota(jnp.int32, (h * across, 128), 0)
        part, at = m >> (quarter.bit_length() - 1), m & (quarter - 1)
        self.own_row = 2 * (at >> (shift - 1)) + (part >> 1)
        self.own_col = 2 * (at & (across // 2 - 1)) + (part & 1)
        self.quarter = quarter

    def every(self, rows, cols):
        return ((self.row < rows) & (self.col < cols)).astype(f32)

    def own(self, rows, cols):
        return ((self.own_row < rows) & (self.own_col < cols)).astype(f32)


def forward_kernel(
    G, h, across, nf,
    ext, keep, top, own, bot, cot, fwd, inv, spec, dwb, ng, nb, ew, eb, pw, pb, ls, dg, ds, dw, db,
    out, act, slope, xhat, fh_out, nm, inv1_out, sh_out, inv2_out, gdw,
    mix, field, fac,
):
    g = pl.program_id(0)
    pixels = h * across
    C = own.shape[-1]
    masks = Masks(h, across)
    Q = masks.quarter
    kr, ki = spec[:nf], spec[nf:]
    for b in range(G):
        rows, cols = ext[g * G + b, 0], ext[g * G + b, 1]
        here = pl.ds(b * pixels, pixels)
        x = jnp.concatenate([top[b], own[b], bot[b]], axis=0)
        x = x * lanes(masks.every(rows, cols).astype(bf16), C)
        hat = dot(fwd[...], x)
        xr, xi = hat[:nf], hat[nf : 2 * nf]
        field[here, :] = hat[2 * nf :]
        xhat[b] = hat[: 2 * nf].astype(bf16)
        product = jnp.concatenate(
            [(xr * kr - xi * ki).astype(bf16), (xr * ki + xi * kr).astype(bf16)], axis=0
        )
        mix[here, :] = dot(inv[...], product)
        fac[here, :] = masks.own(rows, cols) * (
            keep[g * G + b].astype(f32) * (1.0 / survival)
        )
    mixed = mix[...] + dwb[...]
    d = mixed - mean(mixed)
    inv1 = lax.rsqrt(mean(d * d) + epsilon)
    fh = d * inv1
    fh_out[...] = fh.astype(bf16)
    inv1_out[...] = jnp.broadcast_to(inv1, inv1_out.shape)
    nm[...] = (fh * ng[...] + nb[...]).astype(bf16)
    HC = 512
    for k in range(ew.shape[1] // HC):
        part = pl.ds(k * HC, HC)
        hidden = dot(nm[...], ew[:, part]) + eb[:, part]
        a, s = gelu_parts(hidden)
        act[:, part] = a.astype(bf16)
        slope[:, part] = s.astype(bf16)
    branch = dot(act[...], pw[...]) + pb[...]
    res = field[...] + lanes(fac[...], C) * ls[...] * branch
    d = res - mean(res)
    inv2 = lax.rsqrt(mean(d * d) + epsilon)
    sh = d * inv2
    sh_out[...] = sh.astype(bf16)
    inv2_out[...] = jnp.broadcast_to(inv2, inv2_out.shape)
    reduced = sh * dg[...] + ds[...]
    patches, ups = [], []
    for b in range(G):
        rows, cols = ext[g * G + b, 0], ext[g * G + b, 1]
        valid = masks.own(rows, cols)
        rb = (reduced[b * pixels : (b + 1) * pixels] * lanes(valid, C)).astype(bf16)
        patches.append(jnp.concatenate([rb[k * Q : (k + 1) * Q] for k in range(4)], axis=1))
        coarse = lanes(valid[:Q], cot.shape[-1])
        ups.append(cot[b] * coarse.astype(bf16))
        out[b] = ((dot(patches[-1], dw[...]) + db[...]) * coarse).astype(bf16)
    term = dot_tn(jnp.concatenate(patches, axis=0), jnp.concatenate(ups, axis=0))

    @pl.when(g == 0)
    def _():
        gdw[...] = term

    @pl.when(g != 0)
    def _():
        gdw[...] += term


def forward(G, h, across, nf, n_img, ext, keep, top, own, bot, cot, *consts):
    pixels, C, CO = h * across, own.shape[-1], cot.shape[-1]
    HID = consts[6].shape[1]
    Q, NP = pixels // 4, n_img * pixels

    def whole(a):
        return pl.BlockSpec(a.shape, lambda g: (0,) * a.ndim)

    def img(*s):
        return pl.BlockSpec((G,) + s, lambda g: (g,) + (0,) * len(s))

    def pix(c):
        return pl.BlockSpec((G * pixels, c), lambda g: (g, 0))

    smem = pl.BlockSpec(memory_space=pltpu.SMEM)
    sds = jax.ShapeDtypeStruct
    return pl.pallas_call(
        functools.partial(forward_kernel, G, h, across, nf),
        grid=(n_img // G,),
        in_specs=[smem, smem, img(3 * across, C), img(pixels, C), img(3 * across, C), img(Q, CO)]
        + [whole(a) for a in consts],
        out_specs=[
            img(Q, CO), pix(HID), pix(HID), img(2 * nf, C), pix(C), pix(C), pix(128), pix(C), pix(128),
            pl.BlockSpec((4 * C, CO), lambda g: (0, 0)),
        ],
        out_shape=[
            sds((n_img, Q, CO), bf16), sds((NP, HID), bf16), sds((NP, HID), bf16), sds((n_img, 2 * nf, C), bf16),
            sds((NP, C), bf16), sds((NP, C), bf16), sds((NP, 128), f32), sds((NP, C), bf16), sds((NP, 128), f32),
            sds((4 * C, CO), f32),
        ],
        scratch_shapes=[
            pltpu.VMEM((G * pixels, C), f32), pltpu.VMEM((G * pixels, C), f32), pltpu.VMEM((G * pixels, 128), f32),
        ],
        compiler_params=pltpu.CompilerParams(vmem_limit_bytes=VMEM),
        name="forward",
    )(ext, keep, top, own, bot, cot, *consts)


def backward_kernel(
    G, h, across, nf,
    ext, keep, cot, sh_in, inv2, act, slope, nm, fh_in, inv1, xhat,
    dw, dg, ls, pw, ew, ng, fwd_own, inv_all, spec, back,
    own_out, top_out, bot_out, gpw, gew, gdk, vecs, geb, gdb,
    gb_s, gres_s, gm_s, acc,
):
    phase, g = pl.program_id(0), pl.program_id(1)
    pixels = h * across
    C = sh_in.shape[-1]
    masks = Masks(h, across)
    Q = masks.quarter
    rows_here = pl.ds(pl.multiple_of(g * (G * pixels), G * pixels), G * pixels)

    @pl.when((phase == 0) & (g == 0))
    def _():
        for ref in (gpw, gew, vecs, geb, gdb, acc):
            ref[...] = jnp.zeros_like(ref)

    @pl.when(phase == 0)
    def _():
        ups, valids = [], []
        for b in range(G):
            valid = masks.own(ext[g * G + b, 0], ext[g * G + b, 1])
            valids.append(valid)
            ups.append(cot[b] * lanes(valid[:Q].astype(bf16), cot.shape[-1]))
        up = jnp.concatenate(ups, axis=0)
        gdb[...] += total(up.astype(f32))
        gp = dot_nt(up, dw[...])
        slabs = []
        for b in range(G):
            for k in range(4):
                slabs.append(gp[b * Q : (b + 1) * Q, k * C : (k + 1) * C])
        valid = jnp.concatenate(valids, axis=0)
        gr = jnp.concatenate(slabs, axis=0) * lanes(valid, C)
        sh = sh_in[...].astype(f32)
        vecs[0:1, :] += total(gr * sh)
        vecs[1:2, :] += total(gr)
        u = gr * dg[...]
        gres = lanes(inv2[...], C) * (u - mean(u) - sh * mean(u * sh))
        gres_s[rows_here, :] = gres.astype(bf16)
        fac = jnp.concatenate(
            [valids[b] * (keep[g * G + b].astype(f32) * (1.0 / survival)) for b in range(G)], axis=0
        )
        gb = (gres * lanes(fac, C) * ls[...]).astype(bf16)
        gb_s[rows_here, :] = gb
        vecs[2:3, :] += total(gb.astype(f32))
        gpw[...] += dot_tn(gb, act[...])

    @pl.when(phase == 1)
    def _():
        gb = gb_s[rows_here, :]
        HC = 512
        gn = None
        for k in range(ew.shape[1] // HC):
            part = pl.ds(k * HC, HC)
            ga = dot_nt(gb, pw[part, :])
            gh = (ga * slope[:, part].astype(f32)).astype(bf16)
            geb[:, part] += total(gh.astype(f32))
            gew[:, part] += dot_tn(nm[...], gh)
            term = dot_nt(gh, ew[:, part])
            gn = term if gn is None else gn + term
        fh = fh_in[...].astype(f32)
        vecs[3:4, :] += total(gn * fh)
        vecs[4:5, :] += total(gn)
        w = gn * ng[...]
        gm = lanes(inv1[...], C) * (w - mean(w) - fh * mean(w * fh))
        vecs[5:6, :] += total(gm)
        gm_s[rows_here, :] = gm.astype(bf16)

    @pl.when(phase == 2)
    def _():
        kr, ki = spec[:nf], spec[nf:]
        sr, si = acc[:nf], acc[nf:]
        for b in range(G):
            here = pl.ds(pl.multiple_of((g * G + b) * pixels, pixels), pixels)
            hat = dot(fwd_own[...], gm_s[here, :])
            gr, gi = hat[:nf], hat[nf:]
            xr, xi = xhat[b, :nf].astype(f32), xhat[b, nf:].astype(f32)
            sr = sr + gr * xr + gi * xi
            si = si + gr * xi - gi * xr
            q = jnp.concatenate(
                [
                    (gr * kr + gi * ki).astype(bf16),
                    (gi * kr - gr * ki).astype(bf16),
                    gres_s[here, :],
                ],
                axis=0,
            )
            o = dot(inv_all[...], q)
            o = (o * lanes(masks.every(ext[g * G + b, 0], ext[g * G + b, 1]), C)).astype(bf16)
            top_out[b] = o[: 3 * across]
            own_out[b] = o[3 * across : 3 * across + pixels]
            bot_out[b] = o[3 * across + pixels :]
        acc[:nf] = sr
        acc[nf:] = si

    @pl.when((phase == 2) & (g == pl.num_programs(1) - 1))
    def _():
        gdk[...] = jnp.dot(
            back[...], acc[...], preferred_element_type=f32, precision=lax.Precision.HIGHEST
        )


def backward(G, h, across, nf, n_img, ext, keep, cot, sh, inv2, act, slope, nm, fh, inv1, xhat, *consts):
    pixels, C, CO = h * across, sh.shape[-1], cot.shape[-1]
    HID = act.shape[1]
    Q, NP, steps = pixels // 4, n_img * pixels, n_img // G

    def whole(a):
        return pl.BlockSpec(a.shape, lambda t, g: (0,) * a.ndim)

    def at(phase):
        def index(t, g):
            return jnp.where(t < phase, 0, jnp.where(t > phase, steps - 1, g))

        return index

    def img(phase, *s):
        index = at(phase)
        return pl.BlockSpec((G,) + s, lambda t, g: (index(t, g),) + (0,) * len(s))

    def pix(phase, c):
        index = at(phase)
        return pl.BlockSpec((G * pixels, c), lambda t, g: (index(t, g), 0))

    def result(*s):
        return pl.BlockSpec(s, lambda t, g: (0,) * len(s))

    smem = pl.BlockSpec(memory_space=pltpu.SMEM)
    sds = jax.ShapeDtypeStruct
    return pl.pallas_call(
        functools.partial(backward_kernel, G, h, across, nf),
        grid=(3, steps),
        in_specs=[
            smem, smem, img(0, Q, CO), pix(0, C), pix(0, 128), pix(0, HID), pix(1, HID), pix(1, C), pix(1, C), pix(1, 128),
            img(2, 2 * nf, C),
        ]
        + [whole(a) for a in consts],
        out_specs=[
            img(2, pixels, C), img(2, 3 * across, C), img(2, 3 * across, C),
            result(C, HID), result(C, HID), result(56, C), result(8, C), result(1, HID), result(1, CO),
        ],
        out_shape=[
            sds((n_img, pixels, C), bf16), sds((n_img, 3 * across, C), bf16), sds((n_img, 3 * across, C), bf16),
            sds((C, HID), f32), sds((C, HID), f32), sds((56, C), f32), sds((8, C), f32), sds((1, HID), f32), sds((1, CO), f32),
        ],
        scratch_shapes=[
            pltpu.VMEM((NP, C), bf16), pltpu.VMEM((NP, C), bf16), pltpu.VMEM((NP, C), bf16), pltpu.VMEM((2 * nf, C), f32),
        ],
        compiler_params=pltpu.CompilerParams(vmem_limit_bytes=VMEM),
        name="backward",
    )(ext, keep, cot, sh, inv2, act, slope, nm, fh, inv1, xhat, *consts)


def per_device(n_sp, *arrays):
    (
        tokens, extents, keep_mask, cotangent, dw_kernel, dw_bias, norm_gain, norm_bias, expand_weight, expand_bias,
        project_weight, project_bias, layer_scale, down_gain, down_shift, down_weight, down_bias,
    ) = arrays
    n_img, h, across, C = tokens.shape
    CO = cotangent.shape[-1]
    pixels = h * across
    G = 1024 // pixels
    nf, fwd, inv, fwd_own, inv_all, spectrum, back = tables(h, across)
    fwd, inv, fwd_own, inv_all = (jnp.asarray(a, bf16) for a in (fwd, inv, fwd_own, inv_all))
    back = jnp.asarray(back, f32)
    down = [(i, i + 1) for i in range(n_sp - 1)]
    up = [(i + 1, i) for i in range(n_sp - 1)]
    top = lax.ppermute(tokens[:, h - 3 :], "sp", down).reshape(n_img, 3 * across, C)
    bot = lax.ppermute(tokens[:, :3], "sp", up).reshape(n_img, 3 * across, C)
    first = lax.axis_index("sp") * h
    ext = extents - jnp.stack([first, jnp.zeros_like(first)])[None, :]
    spec = jnp.dot(
        jnp.asarray(spectrum, f32), dw_kernel.reshape(49, C), preferred_element_type=f32, precision=lax.Precision.HIGHEST
    )
    own = tokens.reshape(n_img, pixels, C)
    cot = cotangent.reshape(n_img, pixels // 4, CO)
    row = lambda v: v.reshape(1, -1)
    dw = down_weight.reshape(4 * C, CO)
    out, act, slope, xhat, fh, nm, inv1, sh, inv2, gdw = forward(
        G, h, across, nf, n_img, ext, keep_mask, top, own, bot, cot, fwd, inv, spec, row(dw_bias), row(norm_gain),
        row(norm_bias), expand_weight, row(expand_bias), project_weight, row(project_bias), row(layer_scale),
        row(down_gain), row(down_shift), dw, row(down_bias),
    )
    grad, top_g, bot_g, gpw, gew, gdk, vecs, geb, gdb = backward(
        G, h, across, nf, n_img, ext, keep_mask, cot, sh, inv2, act, slope, nm, fh, inv1, xhat, dw, row(down_gain),
        row(layer_scale), project_weight, expand_weight, row(norm_gain), fwd_own, inv_all, spec, back,
    )
    from_above = lax.ppermute(bot_g, "sp", down).reshape(n_img, 3, across, C)
    from_below = lax.ppermute(top_g, "sp", up).reshape(n_img, 3, across, C)
    grad = grad.reshape(n_img, h, across, C)
    gap = ((0, 0), (0, h - 3), (0, 0), (0, 0))
    pog = ((0, 0), (h - 3, 0), (0, 0), (0, 0))
    grad = (
        grad.astype(f32) + jnp.pad(from_above, gap).astype(f32) + jnp.pad(from_below, pog).astype(f32)
    ).astype(bf16)
    gdw, gpw, gew, gdk, vecs, geb, gdb = lax.psum((gdw, gpw, gew, gdk, vecs, geb, gdb), ("sp", "dp"))
    gpw = gpw.T
    gls = (jnp.sum(project_weight.astype(f32) * gpw, axis=0) + project_bias * vecs[2]) / layer_scale
    return (
        out.reshape(n_img, h // 2, across // 2, CO), grad, gdk[:49].reshape(7, 7, C), vecs[5], vecs[3], vecs[4], gew,
        geb[0], gpw, vecs[2], gls, vecs[0], vecs[1], gdw.reshape(down_weight.shape), gdb[0],
    )


def solution(mesh):
    maps = P("dp", "sp", None, None)
    return jax.shard_map(
        functools.partial(per_device, mesh.shape["sp"]),
        mesh=mesh,
        in_specs=(maps, P("dp", None), P("dp"), maps) + (P(),) * 13,
        out_specs=(maps, maps) + (P(),) * 13,
        check_vma=False,
    )
```

time: 943 us -> 407 us (0.43)
  other arithmetic: 469 us -> 7.76 us
  matrix products: 140 us -> 2.65 us
  Pallas kernels: 0 us -> 124 us
  waiting for transfers between devices: 35.8 us -> 145 us
  blocking collectives: 168 us -> 73.5 us
  local copies, waits for them, and re-layouts: 90.8 us -> 27.8 us
    reduce_sum x11 -> x1, other arithmetic: 315 us -> 0.31 us  [per_device(): jnp.sum(project_weight.astype(f32) * gpw, axis=0) + project_bias * vecs[2]]
    convert_element_type x8 -> x1, other arithmetic: 152 us -> 4.74 us  [per_device(): grad = (grad.astype(f32) + jnp.pad(from_above, gap).astype(f32) + jnp.pad...]
    dot_general x9 -> x1, matrix products: 140 us -> 2.65 us  [per_device(): jnp.dot(jnp.asarray(spectrum, f32), dw_kernel.reshape(49, C), preferred_e...]
    psum x1, waiting for transfers between devices: 0.01 us -> 133 us  [per_device(): lax.psum((gdw, gpw, gew, gdk, vecs, geb, gdb), ('sp', 'dp'))]
    pallas_call x0 -> x2, Pallas kernels: none -> 124 us  [the longest x1 64.3 us: forward(): pl.pallas_call(functools.partial(forward_kernel, G, h, across, nf), grid=...]
    psum x1, blocking collectives: 125 us -> 73.5 us  [per_device(): lax.psum((gdw, gpw, gew, gdk, vecs, geb, gdb), ('sp', 'dp'))]
    all_to_all x1 -> x0, blocking collectives: 43.5 us -> none  [per_device(): lax.all_to_all(cotangent, 'sp', split_axis=0, concat_axis=1, tiled=True)]
    all_to_all x3 -> x0, waiting for transfers between devices: 35.8 us -> none  [the longest x1 35.8 us: per_device(): lax.all_to_all(tokens, 'sp', split_axis=0, concat_axis=1, tiled=True)]
  transfers between devices with their start and end apart: 4 -> 5, of which waited for: 1 -> 3; matrix products, arithmetic and copies ran while one was open for 22% -> 6% of each run, Pallas kernels for 0% -> 0%
where the time goes in v1:
time: 407 us; the launch traced here: 406 us
  waiting for transfers between devices  145 us (36%)
  Pallas kernels  124 us (30%)
  blocking collectives  73.5 us (18%)
  local copies, waits for them, and re-layouts  27.8 us (7%)
  between operations  14.2 us (3%)
  starting transfers between devices  11.2 us (3%)
  other arithmetic  7.76 us (2%)
    psum x1, waiting for transfers between devices, per_device(): lax.psum((gdw, gpw, gew, gdk, vecs, geb, gdb), ('sp', 'dp'))  133 us
    psum x1, blocking collectives, per_device(): lax.psum((gdw, gpw, gew, gdk, vecs, geb, gdb), ('sp', 'dp'))  73.5 us
    pallas_call x1, Pallas kernels, forward(): pl.pallas_call(functools.partial(forward_kernel, G, h, across, nf), grid=...  64.3 us
    pallas_call x1, Pallas kernels, backward(): pl.pallas_call(functools.partial(backward_kernel, G, h, across, nf), grid...  59.2 us
    unnamed x25, local copies, waits for them, and re-layouts  11.2 us
    reshape x9, local copies, waits for them, and re-layouts, per_device(): row = lambda v: v.reshape(1, -1)  9.91 us
    ppermute x1, waiting for transfers between devices, per_device(): lax.ppermute(tokens[:, h - 3:], 'sp', down).reshape(n_img, 3 * across, C)  8.6 us
  transfers between devices with their start and end apart: 5, of which 3 were waited for; matrix products, arithmetic and copies ran while one was open for 6% of the time, Pallas kernels for 0%

profile of v1, /device:TPU:0, one launch (start us, length us, event | category | flops | bytes accessed | tf_op | source)
XLA Modules:
  0.0 405.9 jit_solution(16732349256773492273)
XLA Ops:
  7.2 0.0 copy-start.7
  7.2 0.0 copy-start.6
  7.2 0.0 all-reduce.6.cloned.1.call-start
  7.2 2.9 fusion.2
  10.2 5.0 %collective-permute-start = (bf16[16,3,32,384]{3,2,1,0:T(8,128)(2,1)}, bf16[16,3,32,384]{3,2,1,0:T(8,128)(2,1)S(1)}, u32[]{:S(2)}, u32[]{:S(2)}) collective-permute-start(bf16[16,3,32,384]{3,2,1,0:T(8,128)(2,1)} %get-tuple-element.82), channel_id=1, source_target_pairs={{0,8},{8,16},{16,24},{1,9},{9,17},{17,25},{2,10},{10,18},{18,26},{... | collective-permute-start | bytes 3538952 | tf_op jit(solution)/shard_map/ppermute | solution.py:401
  15.2 1.3 collective-permute-start.1
  16.5 1.5 reshape.101
  18.0 0.8 copy.38
  18.8 1.2 reshape.103.ng
  20.0 0.0 copy-done.7
  20.0 0.6 reshape.107.ls
  20.6 1.2 reshape.108.dg
  21.8 1.3 reshape.105.eb
  23.1 1.3 reshape.111.db
  24.4 1.2 reshape.102.dwb
  25.6 1.2 reshape.104.nb
  26.9 0.0 copy-done.6
  26.9 0.6 reshape.106.pb
  27.4 1.2 reshape.109.ds
  28.7 0.1 pad_add_fusion
  28.8 0.6 broadcast_subtract_fusion.ext
  29.4 2.7 fusion.3.spec
  32.0 8.6 %collective-permute-done = bf16[16,3,32,384]{3,2,1,0:T(8,128)(2,1)S(1)} collective-permute-done((bf16[16,3,32,384]{3,2,1,0:T(8,128)(2,1)}, bf16[16,3,32,384]{3,2,1,0:T(8,128)(2,1)S(1)}, u32[]{:S(2)}, u32[]{:S(2)}) %collective-permute-start) | collective-permute-done | bytes 1179680 | tf_op jit(solution)/shard_map/ppermute | solution.py:401
  40.6 0.0 copy-start.3
  40.6 3.9 collective-permute-done.1
  44.5 0.0 copy-start.4
  44.5 0.0 copy-done.3
  44.5 1.0 copy-done.4
  45.5 64.3 %forward.1 = (bf16[16,64,768]{2,1,0:T(8,128)(2,1)}, bf16[4096,1536]{1,0:T(8,128)(2,1)}, bf16[4096,1536]{1,0:T(8,128)(2,1)}, bf16[16,512,384]{2,1,0:T(8,128)(2,1)...) custom-call(s32[16,2]{1,0:T(8,128)} %broadcast_subtract_fusion.ext, ...), custom_call_target="tpu_custom_call" | custom-call | tf_op jit(solution)/shard_map/forward/pallas_call | solution.py:210
  109.8 59.2 %backward.1 = (bf16[16,256,384]{2,1,0:T(8,128)(2,1)}, bf16[16,96,384]{2,1,0:T(8,128)(2,1)}, bf16[16,96,384]{2,1,0:T(8,128)(2,1)}, f32[384,1536]{1,0:T(8,128)}, f...) custom-call(s32[16,2]{1,0:T(8,128)} %broadcast_subtract_fusion.ext, ...), custom_call_target="tpu_custom_call" | custom-call | tf_op jit(solution)/shard_map/backward/pallas_call | solution.py:363
  169.1 0.0 copy-start
  169.1 0.0 all-reduce.6.cloned.1.call-update
  169.1 0.0 copy-start.5
  169.1 3.6 collective-permute-start.2
  172.8 1.3 collective-permute-start.3
  174.1 0.0 copy-done
  174.1 0.6 copy.39
  174.7 0.7 reduce.3
  175.5 0.7 reduce.7
  176.2 0.0 copy-done.5
  176.2 73.5 %all-reduce.2 = (f32[8,384]{1,0:T(8,128)S(1)}, f32[1536]{0:T(1024)}, f32[768]{0:T(1024)}) all-reduce(f32[8,384]{1,0:T(8,128)S(1)} %copy-done.5, f32[1536]{0:T(1024)S(1)} %reduce.3, f32[768]{0:T(1024)S(1)} %reduce.7), channel_id=1, replica_groups=mesh['sp'=4,'dp'=8] {'sp','dp'}, use_global_device_ids=true, to_apply=%region_1.2 | all-reduce | flops 5376 | bytes 43008 | tf_op jit(solution)/shard_map/psum | solution.py:429
  249.7 0.6 slice_reduce_fusion
  250.3 0.0 copy-start.9
  250.3 0.0 collective-permute-done.2
  250.3 0.0 collective-permute-done.3
  250.3 4.7 %fusion.1 = bf16[16,8,32,384]{3,2,1,0:T(8,128)(2,1)} fusion(bf16[16,8,32,384]{3,2,1,0:T(8,128)(2,1)} %bitcast.22, bf16[16,3,32,384]{3,2,1,0:T(8,128)(2,1)} %bitcast.9, bf16[16,3,32,384]{3,2,1,0:T(8,128)(2,1)S(1)} %bitcast.26), kind=kLoop, calls=%fused_computation.2 | loop fusion | flops 9437184 | bytes 8650752 | tf_op jit(solution)/shard_map/convert_element_type | solution.py:428
  255.1 132.7 %all-reduce.6.cloned.1.call-done = (f32[56,384]{1,0:T(8,128)}, f32[384,1536]{1,0:T(8,128)}, f32[1536,384]{0,1:T(8,128)}, f32[2,2,384,768]{3,2,1,0:T(8,128)}) async-done(((f32[56,384]{1,0:T(8,128)}, f32[384,1536]{1,0:T(8,128)}, f32[1536,384]{0,1:T(8,128)}, f32[2,2,384,768]{3,2,1,0:T(8,128)}), (f32[56,384]{1,0:T(8,128)}, f32[384,1536]{1,0:T(8,128)}, f32[1536,384]{0,1:T(8,128)}, ...) | async-done | bytes 9523216 | tf_op jit(solution)/shard_map/psum | solution.py:429
  387.8 0.0 copy-start.1
  387.8 3.2 copy.40
  391.0 0.0 copy-done.1
  391.0 0.0 copy-start.8
  391.0 0.3 multiply_reduce_fusion
  391.3 1.5 reshape.115
  392.9 0.0 copy-done.9
  392.9 0.0 copy-done.8
  392.9 0.6 add_divide_fusion
  393.5 0.0 copy-start.2
  393.5 3.4 copy.45
  396.8 0.0 copy-done.2
  396.9 2.2 copy.46
Async XLA Ops:
  7.2 12.8 %copy-start.7 = (f32[384]{0:T(512)S(1)}, f32[384]{0:T(512)}, u32[]{:S(2)}) copy-start(f32[384]{0:T(512)} %param.35) | copy-start | bytes 4612
  7.2 19.7 %copy-start.6 = (f32[384]{0:T(512)S(1)}, f32[384]{0:T(512)}, u32[]{:S(2)}) copy-start(f32[384]{0:T(512)} %param.34) | copy-start | bytes 4612
  7.2 380.6 %all-reduce.6.cloned.1.call-start = ((), (), s32[]{:S(2)}) async-start(), calls=%async_computation | async-start | bytes 19046400 | tf_op jit(solution)/shard_map/psum | solution.py:429
  10.2 30.4 %collective-permute-start = (bf16[16,3,32,384]{3,2,1,0:T(8,128)(2,1)}, bf16[16,3,32,384]{3,2,1,0:T(8,128)(2,1)S(1)}, u32[]{:S(2)}, u32[]{:S(2)}) collective-permute-start(bf16[16,3,32,384]{3,2,1,0:T(8,128)(2,1)} %get-tuple-element.82), channel_id=1, source_target_pairs={{0,8},{8,16},{16,24},{1,9},{9,17},{17,25},{2,10},{10,18},{18,26},{... | collective-permute-start | bytes 3538952 | tf_op jit(solution)/shard_map/ppermute | solution.py:401
  15.2 29.3 %collective-permute-start.1 = (bf16[16,3,32,384]{3,2,1,0:T(8,128)(2,1)S(1)}, bf16[16,3,32,384]{3,2,1,0:T(8,128)(2,1)S(1)}, u32[]{:S(2)}, u32[]{:S(2)}) collective-permute-start(bf16[16,3,32,384]{3,2,1,0:T(8,128)(2,1)S(1)} %get-tuple-element.81), channel_id=1, source_target_pairs={{8,0},{16,8},{24,16},{9,1},{17,9},{25,17},{10,2},{18,10},{26,18},{... | collective-permute-start | bytes 3538952 | tf_op jit(solution)/shard_map/ppermute | solution.py:402
  40.6 3.9 copy-start.3
  44.5 1.0 copy-start.4
  169.1 5.0 %copy-start = (bf16[1536,384]{1,0:T(8,128)(2,1)S(1)}, bf16[1536,384]{1,0:T(8,128)(2,1)}, u32[]{:S(2)}) copy-start(bf16[1536,384]{1,0:T(8,128)(2,1)} %pw.3) | copy-start | bytes 3538948
  169.1 7.1 %copy-start.5 = (f32[8,384]{1,0:T(8,128)S(1)}, f32[8,384]{1,0:T(8,128)}, u32[]{:S(2)}) copy-start(f32[8,384]{1,0:T(8,128)} %get-tuple-element.47) | copy-start | bytes 36868
  169.1 81.2 %collective-permute-start.2 = (bf16[16,96,384]{2,1,0:T(8,128)(2,1)}, bf16[16,96,384]{2,1,0:T(8,128)(2,1)S(1)}, u32[]{:S(2)}, u32[]{:S(2)}) collective-permute-start(bf16[16,96,384]{2,1,0:T(8,128)(2,1)} %get-tuple-element.44), channel_id=1, source_target_pairs={{0,8},{8,16},{16,24},{1,9},{9,17},{17,25},{2,10},{10,18},{18,26},{... | collective-permute-start | bytes 3538952 | tf_op jit(solution)/shard_map/ppermute | solution.py:421
  172.8 77.6 %collective-permute-start.3 = (bf16[16,96,384]{2,1,0:T(8,128)(2,1)}, bf16[16,96,384]{2,1,0:T(8,128)(2,1)}, u32[]{:S(2)}, u32[]{:S(2)}) collective-permute-start(bf16[16,96,384]{2,1,0:T(8,128)(2,1)} %get-tuple-element.45), channel_id=1, source_target_pairs={{8,0},{16,8},{24,16},{9,1},{17,9},{25,17},{10,2},{18,10},{26,18},{... | collective-permute-start | bytes 3538952 | tf_op jit(solution)/shard_map/ppermute | solution.py:422
  250.3 142.5 %copy-start.9 = (f32[384]{0:T(512)}, f32[384]{0:T(512)S(1)}, u32[]{:S(2)}) copy-start(f32[384]{0:T(512)S(1)} %get-tuple-element.92) | copy-start | bytes 4612
  387.8 3.2 copy-start.1
  391.0 1.9 copy-start.8
  393.5 3.4 copy-start.2
Sparse Core Ops, SparseCore 0:
  169.2 218.5 all-reduce.5

commit v2 on v1

--- a/solution.py
+++ b/solution.py
@@ -12,7 +12,7 @@
 f32 = jnp.float32
 epsilon = 1e-06
 survival = 0.875
-VMEM = 60 * 1024 * 1024
+VMEM = 63 * 1024 * 1024
 
 
 def tables(h, across):
@@ -125,7 +125,7 @@
     G, h, across, nf,
     ext, keep, top, own, bot, cot, fwd, inv, spec, dwb, ng, nb, ew, eb, pw, pb, ls, dg, ds, dw, db,
     out, act, slope, xhat, fh_out, nm, inv1_out, sh_out, inv2_out, gdw,
-    mix, field, fac,
+    mix, field, fac, gdw_s,
 ):
     g = pl.program_id(0)
     pixels = h * across
@@ -184,14 +184,18 @@
 
     @pl.when(g == 0)
     def _():
-        gdw[...] = term
+        gdw_s[...] = term
 
     @pl.when(g != 0)
     def _():
-        gdw[...] += term
-
-
-def forward(G, h, across, nf, n_img, ext, keep, top, own, bot, cot, *consts):
+        gdw_s[...] += term
+
+    @pl.when(g == pl.num_programs(0) - 1)
+    def _():
+        gdw[...] = gdw_s[...].astype(gdw.dtype)
+
+
+def forward(sum_type, G, h, across, nf, n_img, ext, keep, top, own, bot, cot, *consts):
     pixels, C, CO = h * across, own.shape[-1], cot.shape[-1]
     HID = consts[6].shape[1]
     Q, NP = pixels // 4, n_img * pixels
@@ -219,17 +223,18 @@
         out_shape=[
             sds((n_img, Q, CO), bf16), sds((NP, HID), bf16), sds((NP, HID), bf16), sds((n_img, 2 * nf, C), bf16),
             sds((NP, C), bf16), sds((NP, C), bf16), sds((NP, 128), f32), sds((NP, C), bf16), sds((NP, 128), f32),
-            sds((4 * C, CO), f32),
+            sds((4 * C, CO), sum_type),
         ],
         scratch_shapes=[
             pltpu.VMEM((G * pixels, C), f32), pltpu.VMEM((G * pixels, C), f32), pltpu.VMEM((G * pixels, 128), f32),
+            pltpu.VMEM((4 * C, CO), f32),
         ],
         compiler_params=pltpu.CompilerParams(vmem_limit_bytes=VMEM),
         name="forward",
     )(ext, keep, top, own, bot, cot, *consts)
 
 
-def backward_kernel(
+def local_backward_kernel(
     G, h, across, nf,
     ext, keep, cot, sh_in, inv2, act, slope, nm, fh_in, inv1, xhat,
     dw, dg, ls, pw, ew, ng, fwd_own, inv_all, spec, back,
@@ -333,7 +338,7 @@
         )
 
 
-def backward(G, h, across, nf, n_img, ext, keep, cot, sh, inv2, act, slope, nm, fh, inv1, xhat, *consts):
+def local_backward(G, h, across, nf, n_img, ext, keep, cot, sh, inv2, act, slope, nm, fh, inv1, xhat, *consts):
     pixels, C, CO = h * across, sh.shape[-1], cot.shape[-1]
     HID = act.shape[1]
     Q, NP, steps = pixels // 4, n_img * pixels, n_img // G
@@ -361,7 +366,7 @@
     smem = pl.BlockSpec(memory_space=pltpu.SMEM)
     sds = jax.ShapeDtypeStruct
     return pl.pallas_call(
-        functools.partial(backward_kernel, G, h, across, nf),
+        functools.partial(local_backward_kernel, G, h, across, nf),
         grid=(3, steps),
         in_specs=[
             smem, smem, img(0, Q, CO), pix(0, C), pix(0, 128), pix(0, HID), pix(1, HID), pix(1, C), pix(1, C), pix(1, 128),
@@ -380,19 +385,442 @@
             pltpu.VMEM((NP, C), bf16), pltpu.VMEM((NP, C), bf16), pltpu.VMEM((NP, C), bf16), pltpu.VMEM((2 * nf, C), f32),
         ],
         compiler_params=pltpu.CompilerParams(vmem_limit_bytes=VMEM),
+        name="local_backward",
+    )(ext, keep, cot, sh, inv2, act, slope, nm, fh, inv1, xhat, *consts)
+
+
+class Sum:
+    def __init__(self, place, full, half, plane_in, z_in, send, recv, out, first_col=0, by_cols=False):
+        self.place, self.full, self.half = place, full, half
+        self.plane_in, self.z_in, self.send, self.recv = plane_in, z_in, send, recv
+        self.out, self.by_cols = out, by_cols
+        self.col = first_col
+        self.rows, self.cols = half.shape
+        self.plane_rows = self.rows // place.planes
+        self.z_rows = self.plane_rows if by_cols else self.plane_rows // place.zs
+        self.z_cols = self.cols // place.zs if by_cols else self.cols
+
+    def z_at(self, j, base, first_col):
+        if self.by_cols:
+            return (pl.ds(base, self.z_rows), pl.ds(pl.multiple_of(first_col + j * self.z_cols, self.z_cols), self.z_cols))
+        return (pl.ds(pl.multiple_of(base + j * self.z_rows, self.z_rows), self.z_rows), pl.ds(first_col, self.z_cols))
+
+    def copy(self, src, dst, slot, where):
+        return pltpu.make_async_remote_copy(
+            src_ref=src,
+            dst_ref=dst,
+            send_sem=self.send.at[slot],
+            recv_sem=self.recv.at[slot],
+            device_id=where,
+            device_id_type=pl.DeviceIdType.MESH,
+        )
+
+    def copies(self, stage):
+        p = self.place
+        wide = pl.ds(self.col, self.cols)
+        mine = pl.multiple_of(p.plane * self.plane_rows, self.plane_rows)
+        first = pl.multiple_of(p.core * self.rows, self.rows)
+        if stage == 0:
+            other = pl.multiple_of((1 - p.core) * self.rows, self.rows)
+            return [self.copy(self.full.at[pl.ds(other, self.rows)], self.half, 0, p.pair)]
+        if stage == 1:
+            return [
+                self.copy(
+                    self.half.at[pl.ds(pl.multiple_of(j * self.plane_rows, self.plane_rows), self.plane_rows)],
+                    self.plane_in.at[d],
+                    1 + d,
+                    where,
+                )
+                for d, (j, where) in enumerate(p.plane_peers)
+            ]
+        base = 1 + len(p.plane_peers)
+        if stage == 2:
+            return [
+                self.copy(self.half.at[self.z_at(j, mine, 0)], self.z_in.at[d], base + d, where)
+                for d, (j, where) in enumerate(p.z_peers)
+            ]
+        base += len(p.z_peers)
+        if stage == 3:
+            there = self.out.at[self.z_at(p.z, first + mine, self.col)]
+            return [
+                self.copy(self.half.at[self.z_at(p.z, mine, 0)], there, base + d, where)
+                for d, (_, where) in enumerate(p.z_peers)
+            ]
+        base += len(p.z_peers)
+        if stage == 4:
+            there = self.out.at[pl.ds(pl.multiple_of(first + mine, self.plane_rows), self.plane_rows), wide]
+            return [self.copy(there, there, base + d, where) for d, (_, where) in enumerate(p.plane_peers)]
+        base += len(p.plane_peers)
+        there = self.out.at[pl.ds(first, self.rows), wide]
+        return [self.copy(there, there, base, p.pair)]
+
+    def own_copy(self):
+        p = self.place
+        mine = pl.multiple_of(p.plane * self.plane_rows, self.plane_rows)
+        first = pl.multiple_of(p.core * self.rows, self.rows)
+        return pltpu.make_async_copy(
+            self.half.at[self.z_at(p.z, mine, 0)],
+            self.out.at[self.z_at(p.z, first + mine, self.col)],
+            self.send.at[self.send.shape[0] - 1],
+        )
+
+    def step(self, stage):
+        p = self.place
+        mine = pl.multiple_of(p.plane * self.plane_rows, self.plane_rows)
+        if stage > 0:
+            for c in self.copies(stage - 1):
+                c.wait_recv()
+        if stage == 1:
+            first = pl.multiple_of(p.core * self.rows, self.rows)
+            own = self.full[pl.ds(first, self.rows), :]
+            self.half[...] = (self.half[...].astype(f32) + own.astype(f32)).astype(self.half.dtype)
+        if stage == 2:
+            at = (pl.ds(mine, self.plane_rows), slice(None))
+            value = self.half[at].astype(f32)
+            for d in range(len(p.plane_peers)):
+                value = value + self.plane_in[d].astype(f32)
+            self.half[at] = value.astype(self.half.dtype)
+        if stage == 3:
+            at = self.z_at(p.z, mine, 0)
+            value = self.half[at].astype(f32)
+            for d in range(len(p.z_peers)):
+                value = value + self.z_in[d].astype(f32)
+            self.half[at] = value.astype(self.half.dtype)
+            self.own_copy().start()
+        if stage == 4:
+            self.own_copy().wait()
+        if stage < 6:
+            for c in self.copies(stage):
+                c.start()
+        else:
+            for k in range(6):
+                for c in self.copies(k):
+                    c.wait_send()
+
+
+class Place:
+    def __init__(self, zs, planes):
+        self.zs, self.planes = zs, planes
+        self.z, dp = lax.axis_index("sp"), lax.axis_index("dp")
+        self.core, self.plane = dp % 2, dp // 2
+        self.pair = self.at(self.z, self.plane * 2 + (1 - self.core))
+        self.plane_peers, self.z_peers = [], []
+        for d in range(1, planes):
+            j = (self.plane + d) % planes
+            self.plane_peers.append((j, self.at(self.z, j * 2 + self.core)))
+        for d in range(1, zs):
+            j = (self.z + d) % zs
+            self.z_peers.append((j, self.at(j, dp)))
+        self.above, self.below = self.at(self.z - 1, dp), self.at(self.z + 1, dp)
+
+    def at(self, z, dp):
+        return {"sp": z, "dp": dp}
+
+
+CHUNK = 512
+SMALL = 256
+
+
+def backward_kernel(
+    G, h, across, nf, steps, chunks, zs, planes, stages,
+    ext, keep, cot, sh_in, inv2, act, slope, nm, fh_in, inv1, xhat, gdw_own,
+    dw, dg, ls, pw, ew, ng, fwd_own, inv_all, spec, back,
+    own_out, top_in, bot_in, gdw_out, gpw_out, gew_out, small_out,
+    q_s, gres_s, gn_s, acc, gpw, gew, geb, gdb, small, halo_top, halo_bot, halo_sem, *sums,
+):
+    step = pl.program_id(0)
+    second = steps * (1 + chunks)
+    third = second + steps
+    pixels = h * across
+    C = sh_in.shape[-1]
+    masks = Masks(h, across)
+    Q = masks.quarter
+    place = Place(zs, planes)
+    buffers = [sums[6 * k : 6 * k + 6] for k in range(3 + chunks)]
+    reduced = {"down": Sum(place, gdw_own, *buffers[0][1:], gdw_out)}
+    reduced["project"] = Sum(place, *buffers[1], gpw_out)
+    reduced["small"] = Sum(place, *buffers[2], small_out)
+    for k in range(chunks):
+        reduced[f"expand{k}"] = Sum(place, *buffers[3 + k], gew_out, first_col=k * CHUNK, by_cols=True)
+
+    @pl.when(step == 0)
+    def _():
+        barrier = pltpu.get_barrier_semaphore()
+        peers = [place.pair] + [w for _, w in place.plane_peers] + [w for _, w in place.z_peers]
+        for where in peers:
+            pl.semaphore_signal(barrier, inc=1, device_id=where, device_id_type=pl.DeviceIdType.MESH)
+        pl.semaphore_wait(barrier, len(peers))
+        for ref in (gpw, geb, gdb, small, acc):
+            ref[...] = jnp.zeros_like(ref)
+
+    def run(at):
+        for name, stage in stages.get(at, ()):
+            if stage == 0 and name == "project":
+                reduced[name].full[...] = gpw[...].T.astype(bf16)
+            if stage == 0 and name.startswith("expand"):
+                reduced[name].full[...] = gew[...].astype(bf16)
+            if stage == 0 and name == "small":
+                for k in range(geb.shape[1] // C):
+                    small[64 + k : 65 + k, :] = geb[:, k * C : (k + 1) * C]
+                for k in range(gdb.shape[1] // C):
+                    small[72 + k : 73 + k, :] = gdb[:, k * C : (k + 1) * C]
+                reduced[name].full[...] = small[...]
+            reduced[name].step(stage)
+
+    for at in range(third + steps):
+        if at in stages:
+            pl.when(step == at)(functools.partial(run, at))
+
+    @pl.when(step < steps)
+    def _():
+        g = step
+        rows_here = pl.ds(pl.multiple_of(g * (G * pixels), G * pixels), G * pixels)
+        ups, valids = [], []
+        for b in range(G):
+            valid = masks.own(ext[g * G + b, 0], ext[g * G + b, 1])
+            valids.append(valid)
+            ups.append(cot[b] * lanes(valid[:Q].astype(bf16), cot.shape[-1]))
+        up = jnp.concatenate(ups, axis=0)
+        gdb[...] += total(up.astype(f32))
+        gp = dot_nt(up, dw[...])
+        slabs = []
+        for b in range(G):
+            for k in range(4):
+                slabs.append(gp[b * Q : (b + 1) * Q, k * C : (k + 1) * C])
+        valid = jnp.concatenate(valids, axis=0)
+        gr = jnp.concatenate(slabs, axis=0) * lanes(valid, C)
+        sh = sh_in[...].astype(f32)
+        small[56:57, :] += total(gr * sh)
+        small[57:58, :] += total(gr)
+        u = gr * dg[...]
+        gres = lanes(inv2[...], C) * (u - mean(u) - sh * mean(u * sh))
+        gres_s[rows_here, :] = gres.astype(bf16)
+        fac = jnp.concatenate(
+            [valids[b] * (keep[g * G + b].astype(f32) * (1.0 / survival)) for b in range(G)], axis=0
+        )
+        gb = (gres * lanes(fac, C) * ls[...]).astype(bf16)
+        for b in range(G):
+            q_s[g * G + b, :pixels, :] = gb[b * pixels : (b + 1) * pixels]
+        small[58:59, :] += total(gb.astype(f32))
+        gpw[...] += dot_tn(gb, act[...])
+
+    @pl.when((step >= steps) & (step < second))
+    def _():
+        g = (step - steps) % steps
+        rows_here = pl.ds(pl.multiple_of(g * (G * pixels), G * pixels), G * pixels)
+        k = (step - steps) // steps
+        gb = jnp.concatenate([q_s[g * G + b, :pixels, :] for b in range(G)], axis=0)
+        ga = dot_nt(gb, pw[...])
+        gh = (ga * slope[...].astype(f32)).astype(bf16)
+        part = pl.ds(pl.multiple_of(k * CHUNK, CHUNK), CHUNK)
+        geb[:, part] += total(gh.astype(f32))
+        term = dot_tn(nm[...], gh)
+
+        @pl.when(g == 0)
+        def _():
+            gew[...] = term
+
+        @pl.when(g != 0)
+        def _():
+            gew[...] += term
+
+        gn = dot_nt(gh, ew[...])
+
+        @pl.when(k == 0)
+        def _():
+            gn_s[rows_here, :] = gn
+
+        @pl.when(k != 0)
+        def _():
+            gn_s[rows_here, :] += gn
+
+    @pl.when((step >= second) & (step < third))
+    def _():
+        g = step - second
+        rows_here = pl.ds(pl.multiple_of(g * (G * pixels), G * pixels), G * pixels)
+        kr, ki = spec[:nf], spec[nf:]
+        gn = gn_s[rows_here, :]
+        fh = fh_in[...].astype(f32)
+        small[59:60, :] += total(gn * fh)
+        small[60:61, :] += total(gn)
+        w = gn * ng[...]
+        gm = lanes(inv1[...], C) * (w - mean(w) - fh * mean(w * fh))
+        small[61:62, :] += total(gm)
+        gm = gm.astype(bf16)
+        sr, si = acc[:nf], acc[nf:]
+        for b in range(G):
+            hat = dot(fwd_own[...], gm[b * pixels : (b + 1) * pixels])
+            gr, gi = hat[:nf], hat[nf:]
+            xr, xi = xhat[b, :nf].astype(f32), xhat[b, nf:].astype(f32)
+            sr = sr + gr * xr + gi * xi
+            si = si + gr * xi - gi * xr
+            q_s[g * G + b, :nf, :] = (gr * kr + gi * ki).astype(bf16)
+            q_s[g * G + b, nf:, :] = (gi * kr - gr * ki).astype(bf16)
+        acc[:nf] = sr
+        acc[nf:] = si
+
+    @pl.when(step == third - 1)
+    def _():
+        small[0:56, :] = jnp.dot(
+            back[...], acc[...], preferred_element_type=f32, precision=lax.Precision.HIGHEST
+        )
+
+    def halo(buffer, target, g, side, where):
+        part = pl.ds(pl.multiple_of(g * G, G), G)
+        return pltpu.make_async_remote_copy(
+            src_ref=buffer.at[part],
+            dst_ref=target.at[part],
+            send_sem=halo_sem.at[0, side, g],
+            recv_sem=halo_sem.at[1, side, g],
+            device_id=where,
+            device_id_type=pl.DeviceIdType.MESH,
+        )
+
+    above, below = place.above, place.below
+
+    @pl.when(step >= third)
+    def _():
+        g = step - third
+        for b in range(G):
+            here = pl.ds(pl.multiple_of((g * G + b) * pixels, pixels), pixels)
+            q = jnp.concatenate([q_s[g * G + b], gres_s[here, :]], axis=0)
+            o = dot(inv_all[...], q)
+            o = (o * lanes(masks.every(ext[g * G + b, 0], ext[g * G + b, 1]), C)).astype(bf16)
+            halo_top[g * G + b] = o[: 3 * across]
+            own_out[b] = o[3 * across : 3 * across + pixels]
+            halo_bot[g * G + b] = o[3 * across + pixels :]
+
+        @pl.when(place.z > 0)
+        def _():
+            halo(halo_top, bot_in, g, 0, above).start()
+
+        @pl.when(place.z < zs - 1)
+        def _():
+            halo(halo_bot, top_in, g, 1, below).start()
+
+    @pl.when(step == third + steps - 1)
+    def _():
+        run(third + steps)
+
+        @pl.when(place.z > 0)
+        def _():
+            for g in range(steps):
+                halo(halo_top, bot_in, g, 0, above).wait_send()
+                halo(halo_bot, top_in, g, 1, below).wait_recv()
+
+        @pl.when(place.z < zs - 1)
+        def _():
+            for g in range(steps):
+                halo(halo_bot, top_in, g, 1, below).wait_send()
+                halo(halo_top, bot_in, g, 0, above).wait_recv()
+
+
+def schedule(steps, chunks):
+    at = {
+        "down": (0, 1, 4, 7, 10, 16, 18),
+        "project": (4, 5, 9, 11, 13, 18, 20),
+        "expand0": (8, 9, 11, 13, 15, 18, 20),
+        "expand1": (12, 13, 15, 16, 17, 19, 21),
+        "expand2": (16, 17, 18, 19, 20, 21, 22),
+        "small": (20, 21, 22, 23, 24, 24, 24),
+    }
+    table = {}
+    for name, when in at.items():
+        for stage, step in enumerate(when):
+            table.setdefault(step, []).append((name, stage))
+    return table
+
+
+def backward(zs, planes, G, h, across, nf, n_img, ext, keep, cot, sh, inv2, act, slope, nm, fh, inv1, xhat, gdw, *consts):
+    pixels, C, CO = h * across, sh.shape[-1], cot.shape[-1]
+    HID = act.shape[1]
+    Q, NP, steps = pixels // 4, n_img * pixels, n_img // G
+    chunks = HID // CHUNK
+    second = steps * (1 + chunks)
+    third = second + steps
+    dw, dg, ls, pw, ew, ng, fwd_own, inv_all, spec, back = consts
+
+    def whole(a):
+        return pl.BlockSpec(a.shape, lambda t: (0,) * a.ndim, pipeline_mode=pl.Buffered(1))
+
+    def group(first):
+        return lambda t: jnp.clip(t - first, 0, steps - 1)
+
+    def img(first, *s):
+        return pl.BlockSpec((G,) + s, lambda t: (group(first)(t),) + (0,) * len(s))
+
+    def pix(first, c):
+        return pl.BlockSpec((G * pixels, c), lambda t: (group(first)(t), 0))
+
+    def inner(t):
+        n = jnp.clip(t - steps, 0, steps * chunks - 1)
+        return n % steps, n // steps
+
+    any_space = pl.BlockSpec(memory_space=pl.ANY)
+    smem = pl.BlockSpec(memory_space=pltpu.SMEM)
+    sds = jax.ShapeDtypeStruct
+
+    def sum_buffers(rows, cols, by_cols, dtype, full):
+        half, plane = rows // 2, rows // 2 // planes
+        z = (plane, cols // zs) if by_cols else (plane // zs, cols)
+        n = 2 + 2 * (planes - 1) + 2 * (zs - 1)
+        return [
+            pltpu.VMEM((rows, cols) if full else (16, 128), dtype),
+            pltpu.VMEM((half, cols), dtype),
+            pltpu.VMEM((planes - 1, plane, cols), dtype),
+            pltpu.VMEM((zs - 1,) + z, dtype),
+            pltpu.SemaphoreType.DMA((n + 1,)),
+            pltpu.SemaphoreType.DMA((n,)),
+        ]
+
+    sums = sum_buffers(4 * C, CO, False, bf16, False)
+    sums += sum_buffers(HID, C, False, bf16, True)
+    sums += sum_buffers(SMALL, C, False, f32, True)
+    for _ in range(chunks):
+        sums += sum_buffers(C, CHUNK, True, bf16, True)
+    return pl.pallas_call(
+        functools.partial(
+            backward_kernel, G, h, across, nf, steps, chunks, zs, planes, schedule(steps, chunks)
+        ),
+        grid=(third + steps,),
+        in_specs=[
+            smem, smem, img(0, Q, CO), pix(0, C), pix(0, 128), pix(0, HID),
+            pl.BlockSpec((G * pixels, CHUNK), lambda t: inner(t)),
+            pl.BlockSpec((G * pixels, C), lambda t: (inner(t)[0], 0)),
+            pix(second, C), pix(second, 128), img(second, 2 * nf, C), whole(gdw),
+            whole(dw), whole(dg), whole(ls),
+            pl.BlockSpec((CHUNK, C), lambda t: (inner(t)[1], 0)),
+            pl.BlockSpec((C, CHUNK), lambda t: (0, inner(t)[1])),
+            whole(ng), whole(fwd_own), whole(inv_all), whole(spec), whole(back),
+        ],
+        out_specs=[img(third, pixels, C)] + [any_space] * 6,
+        out_shape=[
+            sds((n_img, pixels, C), bf16), sds((n_img, 3 * across, C), bf16), sds((n_img, 3 * across, C), bf16),
+            sds((4 * C, CO), bf16), sds((HID, C), bf16), sds((C, HID), bf16), sds((SMALL, C), f32),
+        ],
+        scratch_shapes=[
+            pltpu.VMEM((n_img, 2 * nf, C), bf16), pltpu.VMEM((NP, C), bf16), pltpu.VMEM((NP, C), f32),
+            pltpu.VMEM((2 * nf, C), f32), pltpu.VMEM((C, HID), f32), pltpu.VMEM((C, CHUNK), f32),
+            pltpu.VMEM((1, HID), f32), pltpu.VMEM((1, CO), f32), pltpu.VMEM((SMALL, C), f32),
+            pltpu.VMEM((n_img, 3 * across, C), bf16), pltpu.VMEM((n_img, 3 * across, C), bf16),
+            pltpu.SemaphoreType.DMA((2, 2, steps)),
+        ]
+        + sums,
+        compiler_params=pltpu.CompilerParams(vmem_limit_bytes=VMEM, collective_id=0, has_side_effects=True),
         name="backward",
-    )(ext, keep, cot, sh, inv2, act, slope, nm, fh, inv1, xhat, *consts)
-
-
-def per_device(n_sp, *arrays):
+    )(ext, keep, cot, sh, inv2, act, slope, nm, fh, inv1, xhat, gdw, *consts)
+
+
+def per_device(n_sp, n_dp, *arrays):
     (
         tokens, extents, keep_mask, cotangent, dw_kernel, dw_bias, norm_gain, norm_bias, expand_weight, expand_bias,
         project_weight, project_bias, layer_scale, down_gain, down_shift, down_weight, down_bias,
     ) = arrays
     n_img, h, across, C = tokens.shape
-    CO = cotangent.shape[-1]
+    CO, HID = cotangent.shape[-1], expand_weight.shape[1]
     pixels = h * across
     G = 1024 // pixels
+    fused = n_sp == 4 and n_dp == 8 and n_img // G == 4 and HID == 3 * CHUNK
     nf, fwd, inv, fwd_own, inv_all, spectrum, back = tables(h, across)
     fwd, inv, fwd_own, inv_all = (jnp.asarray(a, bf16) for a in (fwd, inv, fwd_own, inv_all))
     back = jnp.asarray(back, f32)
@@ -400,7 +828,8 @@
     up = [(i + 1, i) for i in range(n_sp - 1)]
     top = lax.ppermute(tokens[:, h - 3 :], "sp", down).reshape(n_img, 3 * across, C)
     bot = lax.ppermute(tokens[:, :3], "sp", up).reshape(n_img, 3 * across, C)
-    first = lax.axis_index("sp") * h
+    z = lax.axis_index("sp")
+    first = z * h
     ext = extents - jnp.stack([first, jnp.zeros_like(first)])[None, :]
     spec = jnp.dot(
         jnp.asarray(spectrum, f32), dw_kernel.reshape(49, C), preferred_element_type=f32, precision=lax.Precision.HIGHEST
@@ -410,35 +839,49 @@
     row = lambda v: v.reshape(1, -1)
     dw = down_weight.reshape(4 * C, CO)
     out, act, slope, xhat, fh, nm, inv1, sh, inv2, gdw = forward(
+        bf16 if fused else f32,
         G, h, across, nf, n_img, ext, keep_mask, top, own, bot, cot, fwd, inv, spec, row(dw_bias), row(norm_gain),
         row(norm_bias), expand_weight, row(expand_bias), project_weight, row(project_bias), row(layer_scale),
         row(down_gain), row(down_shift), dw, row(down_bias),
     )
-    grad, top_g, bot_g, gpw, gew, gdk, vecs, geb, gdb = backward(
-        G, h, across, nf, n_img, ext, keep_mask, cot, sh, inv2, act, slope, nm, fh, inv1, xhat, dw, row(down_gain),
-        row(layer_scale), project_weight, expand_weight, row(norm_gain), fwd_own, inv_all, spec, back,
+    consts = (
+        dw, row(down_gain), row(layer_scale), project_weight, expand_weight, row(norm_gain), fwd_own, inv_all, spec, back
     )
-    from_above = lax.ppermute(bot_g, "sp", down).reshape(n_img, 3, across, C)
-    from_below = lax.ppermute(top_g, "sp", up).reshape(n_img, 3, across, C)
-    grad = grad.reshape(n_img, h, across, C)
+    saved = (ext, keep_mask, cot, sh, inv2, act, slope, nm, fh, inv1, xhat)
+    if fused:
+        grad, from_above, from_below, gdw, gpw, gew, small = backward(
+            n_sp, n_dp // 2, G, h, across, nf, n_img, *saved, gdw, *consts
+        )
+        from_above = jnp.where(z > 0, from_above, jnp.zeros_like(from_above))
+        from_below = jnp.where(z < n_sp - 1, from_below, jnp.zeros_like(from_below))
+        gdw, gpw, gew = (a.astype(f32) for a in (gdw, gpw, gew))
+        gdk, vecs, geb, gdb = small[:49], small[56:64], small[64 : 64 + HID // C].reshape(HID), small[72 : 72 + CO // C].reshape(CO)
+    else:
+        grad, top_g, bot_g, gpw, gew, gdk, vecs, geb, gdb = local_backward(
+            G, h, across, nf, n_img, *saved, *consts
+        )
+        from_above = lax.ppermute(bot_g, "sp", down)
+        from_below = lax.ppermute(top_g, "sp", up)
+        gdw, gpw, gew, gdk, vecs, geb, gdb = lax.psum((gdw, gpw, gew, gdk, vecs, geb, gdb), ("sp", "dp"))
+        gpw, gdk, geb, gdb = gpw.T, gdk[:49], geb[0], gdb[0]
     gap = ((0, 0), (0, h - 3), (0, 0), (0, 0))
     pog = ((0, 0), (h - 3, 0), (0, 0), (0, 0))
     grad = (
-        grad.astype(f32) + jnp.pad(from_above, gap).astype(f32) + jnp.pad(from_below, pog).astype(f32)
+        grad.reshape(n_img, h, across, C).astype(f32)
+        + jnp.pad(from_above.reshape(n_img, 3, across, C), gap).astype(f32)
+        + jnp.pad(from_below.reshape(n_img, 3, across, C), pog).astype(f32)
     ).astype(bf16)
-    gdw, gpw, gew, gdk, vecs, geb, gdb = lax.psum((gdw, gpw, gew, gdk, vecs, geb, gdb), ("sp", "dp"))
-    gpw = gpw.T
     gls = (jnp.sum(project_weight.astype(f32) * gpw, axis=0) + project_bias * vecs[2]) / layer_scale
     return (
-        out.reshape(n_img, h // 2, across // 2, CO), grad, gdk[:49].reshape(7, 7, C), vecs[5], vecs[3], vecs[4], gew,
-        geb[0], gpw, vecs[2], gls, vecs[0], vecs[1], gdw.reshape(down_weight.shape), gdb[0],
+        out.reshape(n_img, h // 2, across // 2, CO), grad, gdk.reshape(7, 7, C), vecs[5], vecs[3], vecs[4], gew,
+        geb, gpw, vecs[2], gls, vecs[0], vecs[1], gdw.reshape(down_weight.shape), gdb,
     )
 
 
 def solution(mesh):
     maps = P("dp", "sp", None, None)
     return jax.shard_map(
-        functools.partial(per_device, mesh.shape["sp"]),
+        functools.partial(per_device, mesh.shape["sp"], mesh.shape["dp"]),
         mesh=mesh,
         in_specs=(maps, P("dp", None), P("dp"), maps) + (P(),) * 13,
         out_specs=(maps, maps) + (P(),) * 13,

time: 407 us -> 244 us (0.60)
  waiting for transfers between devices: 145 us -> 20.5 us
  blocking collectives: 73.5 us -> 0 us
  Pallas kernels: 124 us -> 186 us
  between operations: 14.2 us -> 0.85 us
  local copies, waits for them, and re-layouts: 27.8 us -> 15.6 us
    psum x1 -> x0, waiting for transfers between devices: 133 us -> none  [per_device(): lax.psum((gdw, gpw, gew, gdk, vecs, geb, gdb), ('sp', 'dp'))]
    psum x1 -> x0, blocking collectives: 73.5 us -> none  [per_device(): lax.psum((gdw, gpw, gew, gdk, vecs, geb, gdb), ('sp', 'dp'))]
    pallas_call x1, Pallas kernels: 59.2 us -> 122 us  [backward(): pl.pallas_call(functools.partial(backward_kernel, G, h, across, nf, steps...]
    unnamed x25 -> x39, local copies, waits for them, and re-layouts: 11.2 us -> 2.59 us
    ppermute x1, waiting for transfers between devices: 8.6 us -> 15.2 us  [per_device(): lax.ppermute(tokens[:, h - 3:], 'sp', down).reshape(n_img, 3 * across, C)]
    ppermute x2 -> x0, starting transfers between devices: 4.92 us -> none  [the longest x1 3.63 us: per_device(): from_above = lax.ppermute(bot_g, 'sp', down).reshape(n_img, 3, across, C)]
    reshape x9, local copies, waits for them, and re-layouts: 9.91 us -> 5.13 us  [per_device(): row = lambda v: v.reshape(1, -1)]
  transfers between devices with their start and end apart: 5 -> 2, of which waited for: 3 -> 2; matrix products, arithmetic and copies ran while one was open for 6% -> 3% of each run, Pallas kernels for 0% -> 0%
where the time goes in v2:
time: 244 us; the launch traced here: 243 us
  Pallas kernels  186 us (76%)
  waiting for transfers between devices  20.5 us (8%)
  local copies, waits for them, and re-layouts  15.6 us (6%)
  other arithmetic  11.3 us (5%)
  starting transfers between devices  7.26 us (3%)
    pallas_call x1, Pallas kernels, backward(): pl.pallas_call(functools.partial(backward_kernel, G, h, across, nf, steps...  122 us
    pallas_call x1, Pallas kernels, forward(): pl.pallas_call(functools.partial(forward_kernel, G, h, across, nf), grid=...  63.8 us
    ppermute x1, waiting for transfers between devices, per_device(): lax.ppermute(tokens[:, h - 3:], 'sp', down).reshape(n_img, 3 * across, C)  15.2 us
    ppermute x1, starting transfers between devices, per_device(): lax.ppermute(tokens[:, h - 3:], 'sp', down).reshape(n_img, 3 * across, C)  5.98 us
    ppermute x1, waiting for transfers between devices, per_device(): bot = lax.ppermute(tokens[:, :3], 'sp', up).reshape(n_img, 3 * across, C)  5.25 us
    reshape x9, local copies, waits for them, and re-layouts, per_device(): row = lambda v: v.reshape(1, -1)  5.13 us
  transfers between devices with their start and end apart: 2, of which 2 were waited for; matrix products, arithmetic and copies ran while one was open for 3% of the time, Pallas kernels for 0%

profile of v2, /device:TPU:0, one launch (start us, length us, event | category | flops | bytes accessed | tf_op | source)
XLA Modules:
  0.0 243.3 jit_solution(18388539097366624909)
XLA Ops:
  0.6 0.0 copy-start.6
  0.7 0.0 copy-start.18
  0.7 0.0 copy-start.7
  0.7 0.0 copy-start.13
  0.7 0.0 copy-start.14
  0.7 0.0 copy-start.15
  0.7 0.0 copy-start.10
  0.7 0.0 copy-start.8
  0.7 0.0 copy-start.9
  0.7 0.0 copy-start.16
  0.8 0.0 copy-start.17
  0.8 0.0 copy-start.12
  0.8 2.0 fusion.2
  2.8 6.0 %collective-permute-start = (bf16[16,3,32,384]{3,2,1,0:T(8,128)(2,1)S(1)}, bf16[16,3,32,384]{3,2,1,0:T(8,128)(2,1)}, u32[]{:S(2)}, u32[]{:S(2)}) collective-permute-start(bf16[16,3,32,384]{3,2,1,0:T(8,128)(2,1)S(1)} %get-tuple-element.58), channel_id=1, source_target_pairs={{0,8},{8,16},{16,24},{1,9},{9,17},{17,25},{2,10},{10,18},{18,26},{... | collective-permute-start | bytes 3538952 | tf_op jit(solution)/shard_map/ppermute | solution.py:829
  8.7 1.3 collective-permute-start.1
  10.0 0.0 copy-done.18
  10.0 0.1 copy.38
  10.1 0.0 copy-done.7
  10.1 0.0 copy-done.13
  10.1 0.6 reshape.111.dwb
  10.7 0.0 copy-done.14
  10.7 0.6 reshape.112.ng
  11.3 0.0 copy-done.15
  11.3 0.6 reshape.113.nb
  11.8 0.0 copy-done.10
  11.8 0.6 reshape.114.eb
  12.4 0.0 copy-done.8
  12.4 0.6 reshape.115.pb
  13.0 0.0 copy-done.9
  13.0 0.6 reshape.116.ls
  13.6 0.0 copy-done.16
  13.6 0.6 reshape.117.dg
  14.1 0.0 copy-done.17
  14.1 0.6 reshape.118.ds
  14.7 0.0 copy-done.12
  14.7 0.6 reshape.120.db
  15.3 0.1 pad_add_fusion
  15.4 0.6 broadcast_subtract_fusion.ext
  16.0 0.0 copy-done.6
  16.0 1.7 fusion.3.spec
  17.7 15.2 %collective-permute-done = bf16[16,3,32,384]{3,2,1,0:T(8,128)(2,1)} collective-permute-done((bf16[16,3,32,384]{3,2,1,0:T(8,128)(2,1)S(1)}, bf16[16,3,32,384]{3,2,1,0:T(8,128)(2,1)}, u32[]{:S(2)}, u32[]{:S(2)}) %collective-permute-start) | collective-permute-done | bytes 1179680 | tf_op jit(solution)/shard_map/ppermute | solution.py:829
  32.9 5.2 %collective-permute-done.1 = bf16[16,3,32,384]{3,2,1,0:T(8,128)(2,1)} collective-permute-done((bf16[16,3,32,384]{3,2,1,0:T(8,128)(2,1)S(1)}, bf16[16,3,32,384]{3,2,1,0:T(8,128)(2,1)}, u32[]{:S(2)}, u32[]{:S(2)}) %collective-permute-start.1) | collective-permute-done | bytes 1179680 | tf_op jit(solution)/shard_map/ppermute | solution.py:830
  38.1 63.8 %forward.1 = (bf16[16,64,768]{2,1,0:T(8,128)(2,1)}, bf16[4096,1536]{1,0:T(8,128)(2,1)}, bf16[4096,1536]{1,0:T(8,128)(2,1)}, bf16[16,512,384]{2,1,0:T(8,128)(2,1)...) custom-call(s32[16,2]{1,0:T(8,128)} %broadcast_subtract_fusion.ext, ...), custom_call_target="tpu_custom_call" | custom-call | tf_op jit(solution)/shard_map/forward/pallas_call | solution.py:214
  101.9 122.4 %backward.1 = (bf16[16,256,384]{2,1,0:T(8,128)(2,1)}, bf16[16,96,384]{2,1,0:T(8,128)(2,1)}, bf16[16,96,384]{2,1,0:T(8,128)(2,1)}, bf16[1536,768]{1,0:T(8,128)(2,...) custom-call(s32[16,2]{1,0:T(8,128)} %broadcast_subtract_fusion.ext, s32[16]{0:T(128)} %keep.3, ...), custom_call_target="tpu_custom_call" | custom-call | tf_op jit(solution)/shard_map/backward/pallas_call | solution.py:781
  224.4 0.0 copy-start
  224.4 0.0 copy-start.5
  224.4 1.0 slice.43
  225.4 1.6 slice_reduce_fusion
  227.0 0.7 slice.47
  227.7 0.7 slice.51
  228.4 0.6 reshape.124
  229.1 3.0 %convert_element_type.34 = f32[384,1536]{1,0:T(8,128)} convert(bf16[384,1536]{1,0:T(8,128)(2,1)} %get-tuple-element.46) | non-fusion elementwise | flops 589824 | bytes 3538944 | tf_op jit(solution)/shard_map/convert_element_type | solution.py:857
  232.0 0.6 reshape.125
  232.6 0.0 copy-done
  232.6 0.0 copy-done.5
  232.6 1.7 multiply_reduce_fusion
  234.4 0.8 copy-done.2
  235.2 2.6 %convert.3 = f32[2,2,384,768]{3,2,1,0:T(8,128)} convert(bf16[2,2,384,768]{3,2,1,0:T(8,128)(2,1)S(1)} %bitcast.23) | non-fusion elementwise | flops 1179648 | bytes 7077888 | tf_op jit(solution)/shard_map/reshape | solution.py:877
  237.8 0.6 reshape.128
  238.4 0.6 add_divide_fusion
  239.0 0.0 copy-done.4
  239.0 0.2 broadcast_select_fusion
  239.2 1.7 copy-done.1
  240.8 2.5 %fusion.1 = bf16[16,8,32,384]{3,2,1,0:T(8,128)(2,1)} fusion(bf16[16,8,32,384]{3,2,1,0:T(8,128)(2,1)S(1)} %bitcast.22, bf16[16,3,32,384]{3,2,1,0:T(8,128)(2,1)S(1)} %bitcast.20, bf16[16,3,32,384]{3,2,1,0:T(8,128)(2,1)S(1)} %bitcast.21), kind=kLoop, calls=%fused_computation.2 | loop fusion | flops 9437184 | bytes 8650752 | tf_op jit(solution)/shard_map/convert_element_type | solution.py:873
  (8 shorter events, 0.0 us)
Async XLA Ops:
  0.6 15.3 %copy-start.6 = (f32[512,49]{1,0:T(8,128)S(1)}, f32[512,49]{1,0:T(8,128)}, u32[]{:S(2)}) copy-start(f32[512,49]{1,0:T(8,128)} %constant.35.clone) | copy-start | bytes 301060
  0.7 9.4 %copy-start.18 = (s32[16,2]{0,1:T(2,128)S(1)}, s32[16,2]{0,1:T(2,128)}, u32[]{:S(2)}) copy-start(s32[16,2]{0,1:T(2,128)} %param.24) | copy-start | bytes 388
  0.7 9.4 %copy-start.7 = (f32[7,7,384]{2,1,0:T(8,128)S(1)}, f32[7,7,384]{2,1,0:T(8,128)}, u32[]{:S(2)}) copy-start(f32[7,7,384]{2,1,0:T(8,128)} %param.27) | copy-start | bytes 225796
  0.7 9.5 %copy-start.13 = (f32[384]{0:T(512)S(1)}, f32[384]{0:T(512)}, u32[]{:S(2)}) copy-start(f32[384]{0:T(512)} %param.28) | copy-start | bytes 4612
  0.7 10.0 %copy-start.14 = (f32[384]{0:T(512)S(1)}, f32[384]{0:T(512)}, u32[]{:S(2)}) copy-start(f32[384]{0:T(512)} %param.29) | copy-start | bytes 4612
  0.7 10.6 %copy-start.15 = (f32[384]{0:T(512)S(1)}, f32[384]{0:T(512)}, u32[]{:S(2)}) copy-start(f32[384]{0:T(512)} %param.30) | copy-start | bytes 4612
  0.7 11.1 %copy-start.10 = (f32[1536]{0:T(1024)S(1)}, f32[1536]{0:T(1024)}, u32[]{:S(2)}) copy-start(f32[1536]{0:T(1024)} %param.32) | copy-start | bytes 18436
  0.7 11.7 %copy-start.8 = (f32[384]{0:T(512)S(1)}, f32[384]{0:T(512)}, u32[]{:S(2)}) copy-start(f32[384]{0:T(512)} %param.34) | copy-start | bytes 4612
  0.7 12.3 %copy-start.9 = (f32[384]{0:T(512)S(1)}, f32[384]{0:T(512)}, u32[]{:S(2)}) copy-start(f32[384]{0:T(512)} %param.35) | copy-start | bytes 4612
  0.7 12.8 %copy-start.16 = (f32[384]{0:T(512)S(1)}, f32[384]{0:T(512)}, u32[]{:S(2)}) copy-start(f32[384]{0:T(512)} %param.36) | copy-start | bytes 4612
  0.8 13.4 %copy-start.17 = (f32[384]{0:T(512)S(1)}, f32[384]{0:T(512)}, u32[]{:S(2)}) copy-start(f32[384]{0:T(512)} %param.37) | copy-start | bytes 4612
  0.8 13.9 %copy-start.12 = (f32[768]{0:T(1024)S(1)}, f32[768]{0:T(1024)}, u32[]{:S(2)}) copy-start(f32[768]{0:T(1024)} %param.39) | copy-start | bytes 9220
  2.8 30.1 %collective-permute-start = (bf16[16,3,32,384]{3,2,1,0:T(8,128)(2,1)S(1)}, bf16[16,3,32,384]{3,2,1,0:T(8,128)(2,1)}, u32[]{:S(2)}, u32[]{:S(2)}) collective-permute-start(bf16[16,3,32,384]{3,2,1,0:T(8,128)(2,1)S(1)} %get-tuple-element.58), channel_id=1, source_target_pairs={{0,8},{8,16},{16,24},{1,9},{9,17},{17,25},{2,10},{10,18},{18,26},{... | collective-permute-start | bytes 3538952 | tf_op jit(solution)/shard_map/ppermute | solution.py:829
  8.7 29.4 %collective-permute-start.1 = (bf16[16,3,32,384]{3,2,1,0:T(8,128)(2,1)S(1)}, bf16[16,3,32,384]{3,2,1,0:T(8,128)(2,1)}, u32[]{:S(2)}, u32[]{:S(2)}) collective-permute-start(bf16[16,3,32,384]{3,2,1,0:T(8,128)(2,1)S(1)} %get-tuple-element.57), channel_id=1, source_target_pairs={{8,0},{16,8},{24,16},{9,1},{17,9},{25,17},{10,2},{18,10},{26,18},{... | collective-permute-start | bytes 3538952 | tf_op jit(solution)/shard_map/ppermute | solution.py:830
  224.4 8.3 %copy-start = (bf16[1536,384]{1,0:T(8,128)(2,1)S(1)}, bf16[1536,384]{1,0:T(8,128)(2,1)}, u32[]{:S(2)}) copy-start(bf16[1536,384]{1,0:T(8,128)(2,1)} %pw.3) | copy-start | bytes 3538948
  224.4 8.3 %copy-start.5 = (bf16[1536,384]{1,0:T(8,128)(2,1)S(1)}, bf16[1536,384]{1,0:T(8,128)(2,1)}, u32[]{:S(2)}) copy-start(bf16[1536,384]{1,0:T(8,128)(2,1)} %get-tuple-element.47) | copy-start | bytes 3538948
  227.0 11.4 %copy-start.11 = (f32[384]{0:T(512)}, f32[384]{0:T(512)S(1)}, u32[]{:S(2)}) copy-start(f32[384]{0:T(512)S(1)} %get-tuple-element.51) | copy-start | bytes 4612
  232.6 2.5 %copy-start.2 = (bf16[1536,768]{1,0:T(8,128)(2,1)S(1)}, bf16[1536,768]{1,0:T(8,128)(2,1)}, u32[]{:S(2)}) copy-start(bf16[1536,768]{1,0:T(8,128)(2,1)} %get-tuple-element.48) | copy-start | bytes 7077892
  235.2 3.8 %copy-start.3 = (bf16[16,96,384]{2,1,0:T(8,128)(2,1)S(1)}, bf16[16,96,384]{2,1,0:T(8,128)(2,1)}, u32[]{:S(2)}) copy-start(bf16[16,96,384]{2,1,0:T(8,128)(2,1)} %get-tuple-element.43) | copy-start | bytes 3538948
  235.2 3.8 %copy-start.4 = (bf16[16,96,384]{2,1,0:T(8,128)(2,1)S(1)}, bf16[16,96,384]{2,1,0:T(8,128)(2,1)}, u32[]{:S(2)}) copy-start(bf16[16,96,384]{2,1,0:T(8,128)(2,1)} %get-tuple-element.44) | copy-start | bytes 3538948
  239.0 1.9 copy-start.1

commit v3 on v1

v3 whole, which is shorter than its diff:
```python
import functools

import jax
import jax.numpy as jnp
import numpy as np
from jax import lax
from jax.experimental import pallas as pl
from jax.experimental.pallas import tpu as pltpu
from jax.sharding import PartitionSpec as P

bf16 = jnp.bfloat16
f32 = jnp.float32
epsilon = 1e-06
survival = 0.875
VMEM = 63 * 1024 * 1024
MESH = pl.DeviceIdType.MESH
EARLY = 1024
DWB, NG, NB, PB, LS, DG, DS, DB, EB = 0, 1, 2, 3, 4, 5, 6, 7, 9
SMALL, V_DG, V_DS, V_PB, V_NG, V_NB, V_DWB, V_EB, V_DB = 128, 56, 57, 58, 59, 60, 61, 64, 72


def tables(h, across):
    nr, nc = h + 6, across + 3
    us, vs, ms = [], [], []
    for v in range(nc // 2 + 1):
        for u in range(nr):
            mu, mv = (-u) % nr, (-v) % nc
            if (mv, mu) < (v, u):
                continue
            us.append(u)
            vs.append(v)
            ms.append(1.0 if (mu, mv) == (u, v) else 2.0)
    n = len(us)
    nf = -(-n // 128) * 128
    us, vs, ms = (np.array(a + [0] * (nf - n), np.float64) for a in (us, vs, ms))
    live = (np.arange(nf) < n)[:, None]

    def angle(r, c):
        turns = (np.outer(us, r.ravel()) * nc + np.outer(vs, c.ravel()) * nr) % (nr * nc)
        return 2 * np.pi * turns / (nr * nc)

    def waves(a):
        return np.concatenate([np.cos(a) * live, -np.sin(a) * live])

    every = waves(angle(*np.meshgrid(np.arange(h + 6), np.arange(across), indexing="ij")))
    own = waves(angle(*np.meshgrid(np.arange(h), np.arange(across), indexing="ij")))
    ki, kj = np.meshgrid(np.arange(7), np.arange(8) - 3, indexing="ij")
    taps = angle(ki, kj)
    weight = (ms / (nr * nc))[:, None] * (kj.ravel() < 4)[None, :]
    spectrum = np.concatenate([np.cos(taps) * weight, np.sin(taps) * weight])
    back = np.concatenate([np.cos(taps) * weight, -np.sin(taps) * weight]).T
    return nf, every, own.T, own, every.T, spectrum, back


def dot(a, b):
    return jnp.dot(a, b, preferred_element_type=f32)


def dot_nt(a, b):
    return lax.dot_general(a, b, (((1,), (1,)), ((), ())), preferred_element_type=f32)


def dot_tn(a, b):
    return lax.dot_general(a, b, (((0,), (0,)), ((), ())), preferred_element_type=f32)


def dot_exact(a, b):
    return jnp.dot(a, b, preferred_element_type=f32, precision=lax.Precision.HIGHEST)


def mean(x):
    return jnp.sum(x, axis=-1, keepdims=True) * (1.0 / x.shape[-1])


def total(x):
    return jnp.sum(x, axis=0, keepdims=True)


def lanes(x, width):
    return jnp.concatenate([x] * (width // x.shape[1]), axis=1)


def stack(parts, axis):
    return parts[0] if len(parts) == 1 else jnp.concatenate(parts, axis=axis)


def gelu_parts(v):
    u = v * v
    p = 0.7978667366454887 + u * (
        0.03640226973029483
        + u * (-9.53235048862514e-05 + u * (-3.491248211005391e-05 + u * 1.3019431827058075e-06))
    )
    phi = 0.5 + 0.5 * jnp.tanh(v * p)
    density = jnp.exp2(u * -0.7213475204444817 - 1.3257480647361595)
    return v * phi, phi + v * density


class Masks:
    def __init__(self, h, across):
        n = lax.broadcasted_iota(jnp.int32, ((h + 6) * across, 128), 0)
        self.row, self.col = (n >> (across.bit_length() - 1)) - 3, n & (across - 1)
        self.own_rows = slice(3 * across, (3 + h) * across)
        q = lax.broadcasted_iota(jnp.int32, (h * across // 4, 128), 0)
        half = across // 2
        self.coarse_row, self.coarse_col = 2 * (q >> (half.bit_length() - 1)), 2 * (q & (half - 1))

    def every(self, rows, cols):
        return ((self.row < rows) & (self.col < cols)).astype(f32)

    def own(self, rows, cols):
        r, c = self.row[self.own_rows], self.col[self.own_rows]
        return ((r < rows) & (c < cols)).astype(f32)

    def coarse(self, rows, cols):
        return ((self.coarse_row < rows) & (self.coarse_col < cols)).astype(f32)


def remote(src, dst, send, recv, where):
    return pltpu.make_async_remote_copy(
        src_ref=src, dst_ref=dst, send_sem=send, recv_sem=recv, device_id=where, device_id_type=MESH
    )


def greet(peers):
    barrier = pltpu.get_barrier_semaphore()
    for where in peers:
        pl.semaphore_signal(barrier, inc=1, device_id=where, device_id_type=MESH)
    pl.semaphore_wait(barrier, len(peers))


def tap_rows(dwk):
    gap = jnp.zeros((1, dwk.shape[-1]), f32)
    return jnp.concatenate([x for i in range(7) for x in (dwk[i], gap)], axis=0)


def forward_kernel(
    G, T, h, across, nf, zs, steps,
    ext, keep, tok, own, cot, fwd, inv, taps, dwk, vec, ew, pw, dw,
    out, act, slope_early, slope_late, xhat, fh_out, nm, inv1_out, sh_out, inv2_out, gdw,
    top, bot, spec, red, gdw_s, sem,
):
    g = pl.program_id(0)
    pixels = h * across
    edge = 3 * across
    C = own.shape[-1]
    z, dp = lax.axis_index("sp"), lax.axis_index("dp")
    above, below = {"sp": z - 1, "dp": dp}, {"sp": z + 1, "dp": dp}

    def halo(k, up):
        part = pl.ds(k * G, G)
        if up:
            return remote(tok.at[part, pl.ds(0, edge)], bot.at[part], sem.at[0, 0, k], sem.at[1, 0, k], above)
        return remote(tok.at[part, pl.ds(pixels - edge, edge)], top.at[part], sem.at[0, 1, k], sem.at[1, 1, k], below)

    def each(k, up_act, down_act):
        if up_act is not None:
            pl.when(z > 0)(lambda: up_act(halo(k, True)))
        if down_act is not None:
            pl.when(z < zs - 1)(lambda: down_act(halo(k, False)))

    @pl.when(g == 0)
    def _():
        greet([{"sp": (z + 1) % zs, "dp": dp}, {"sp": (z + zs - 1) % zs, "dp": dp}])
        for k in range(steps):
            each(k, lambda c: c.start(), lambda c: c.start())

        @pl.when(z == 0)
        def _():
            top[...] = jnp.zeros_like(top)

        @pl.when(z == zs - 1)
        def _():
            bot[...] = jnp.zeros_like(bot)

        spec[...] = dot_exact(taps[...], tap_rows(dwk))

    for k in range(steps):

        @pl.when(g == k)
        def _():
            pl.when(z < zs - 1)(lambda: halo(k, True).wait_recv())
            pl.when(z > 0)(lambda: halo(k, False).wait_recv())

    masks = Masks(h, across)
    kr, ki = lanes(spec[:nf], T * C), lanes(spec[nf:], T * C)
    eb = jnp.concatenate([vec[EB + k : EB + k + 1, :] for k in range(ew.shape[1] // C)], axis=1)
    db = jnp.concatenate([vec[DB + k : DB + k + 1, :] for k in range(cot.shape[-1] // C)], axis=1)
    HC = 512
    for team in range(G // T):
        xs, fields, valids, facs = [], [], [], []
        for t in range(T):
            b = team * T + t
            rows, cols = ext[g * G + b, 0], ext[g * G + b, 1]
            x = jnp.concatenate([top[g * G + b], own[b], bot[g * G + b]], axis=0)
            every = masks.every(rows, cols)
            x = x * lanes(every.astype(bf16), C)
            xs.append(x)
            fields.append(x[masks.own_rows])
            valids.append(every[masks.own_rows])
            facs.append(valids[-1] * (keep[g * G + b].astype(f32) * (1.0 / survival)))
        hat = dot(fwd[...], stack(xs, 1))
        xr, xi = hat[:nf], hat[nf:]
        for t in range(T):
            xhat[team * T + t] = hat[:, t * C : (t + 1) * C].astype(bf16)
        product = jnp.concatenate(
            [(xr * kr - xi * ki).astype(bf16), (xr * ki + xi * kr).astype(bf16)], axis=0
        )
        mixed = dot(inv[...], product)
        mixed = stack([mixed[:, t * C : (t + 1) * C] for t in range(T)], 0) + vec[DWB : DWB + 1, :]
        here = pl.ds(team * T * pixels, T * pixels)
        d = mixed - mean(mixed)
        inv1 = lax.rsqrt(mean(d * d) + epsilon)
        fh = d * inv1
        fh_out[here, :] = fh.astype(bf16)
        inv1_out[here, :] = jnp.broadcast_to(inv1, (T * pixels, 128))
        normed = (fh * vec[NG : NG + 1, :] + vec[NB : NB + 1, :]).astype(bf16)
        nm[here, :] = normed
        branch = vec[PB : PB + 1, :]
        for k in range(ew.shape[1] // HC):
            part = slice(k * HC, (k + 1) * HC)
            a, s = gelu_parts(dot(normed, ew[:, part]) + eb[:, part])
            a = a.astype(bf16)
            act[here, part] = a
            if k * HC < EARLY:
                slope_early[here, part] = s.astype(bf16)
            else:
                slope_late[here, k * HC - EARLY : (k + 1) * HC - EARLY] = s.astype(bf16)
            branch = branch + dot(a, pw[part, :])
        valid, fac = stack(valids, 0), stack(facs, 0)
        res = stack(fields, 0).astype(f32) + lanes(fac, C) * (branch * vec[LS : LS + 1, :])
        d = res - mean(res)
        inv2 = lax.rsqrt(mean(d * d) + epsilon)
        sh = d * inv2
        sh_out[here, :] = sh.astype(bf16)
        inv2_out[here, :] = jnp.broadcast_to(inv2, (T * pixels, 128))
        reduced = (sh * vec[DG : DG + 1, :] + vec[DS : DS + 1, :]) * lanes(valid, C)
        rows_here = T * h // 2
        for k in range(C // 128):
            slab = reduced[:, k * 128 : (k + 1) * 128].reshape(rows_here, 2, across, 128)
            red[k, team * rows_here : (team + 1) * rows_here] = slab
    patch = jnp.concatenate(
        [
            red[k, :, p, pl.ds(q, across // 2, stride=2), :].reshape(G * pixels // 4, 128).astype(bf16)
            for p in range(2)
            for q in range(2)
            for k in range(C // 128)
        ],
        axis=1,
    )
    coarse = stack([masks.coarse(ext[g * G + b, 0], ext[g * G + b, 1]) for b in range(G)], 0)
    coarse = lanes(coarse, cot.shape[-1])
    up = cot[...].reshape(coarse.shape) * coarse.astype(bf16)
    out[...] = ((dot(patch, dw[...]) + db) * coarse).astype(bf16).reshape(out.shape)
    term = dot_tn(patch, up)

    @pl.when(g == 0)
    def _():
        gdw_s[...] = term

    @pl.when(g != 0)
    def _():
        gdw_s[...] += term

    @pl.when(g == steps - 1)
    def _():
        gdw[...] = gdw_s[...].astype(gdw.dtype)
        for k in range(steps):
            each(k, lambda c: c.wait_send(), lambda c: c.wait_send())


def whole(a):
    return pl.BlockSpec(a.shape, lambda t: (0,) * a.ndim, pipeline_mode=pl.Buffered(1))


def forward(sum_type, zs, G, T, h, across, nf, n_img, ext, keep, own, cot, *consts):
    pixels, C, CO = h * across, own.shape[-1], cot.shape[-1]
    HID = consts[-3].shape[1]
    Q, NP, steps = pixels // 4, n_img * pixels, n_img // G

    def img(*s):
        return pl.BlockSpec((G,) + s, lambda g: (g,) + (0,) * len(s))

    def pix(c):
        return pl.BlockSpec((G * pixels, c), lambda g: (g, 0))

    smem = pl.BlockSpec(memory_space=pltpu.SMEM)
    sds = jax.ShapeDtypeStruct
    return pl.pallas_call(
        functools.partial(forward_kernel, G, T, h, across, nf, zs, steps),
        grid=(steps,),
        in_specs=[smem, smem, pl.BlockSpec(memory_space=pl.ANY), img(pixels, C), img(Q, CO)] + [whole(a) for a in consts],
        out_specs=[
            img(Q, CO), pix(HID), pix(EARLY), pix(HID - EARLY), img(2 * nf, C), pix(C), pix(C), pix(128), pix(C), pix(128),
            pl.BlockSpec((4 * C, CO), lambda g: (0, 0)),
        ],
        out_shape=[
            sds((n_img, Q, CO), bf16), sds((NP, HID), bf16), sds((NP, EARLY), bf16), sds((NP, HID - EARLY), bf16), sds((n_img, 2 * nf, C), bf16),
            sds((NP, C), bf16), sds((NP, C), bf16), sds((NP, 128), f32), sds((NP, C), bf16), sds((NP, 128), f32),
            sds((4 * C, CO), sum_type),
        ],
        scratch_shapes=[
            pltpu.VMEM((n_img, 3 * across, C), bf16), pltpu.VMEM((n_img, 3 * across, C), bf16),
            pltpu.VMEM((2 * nf, C), f32), pltpu.VMEM((C // 128, G * h // 2, 2, across, 128), f32), pltpu.VMEM((4 * C, CO), f32),
            pltpu.SemaphoreType.DMA((2, 2, steps)),
        ],
        compiler_params=pltpu.CompilerParams(vmem_limit_bytes=VMEM, collective_id=1, has_side_effects=True),
        name="forward",
    )(ext, keep, own, own, cot, *consts)


class Place:
    def __init__(self, zs):
        self.z, self.dp = lax.axis_index("sp"), lax.axis_index("dp")
        self.core, self.chip = self.dp % 2, self.dp // 2
        self.pair = self.at(self.z, self.dp + 1 - 2 * self.core)
        self.above, self.below = self.at(self.z - 1, self.dp), self.at(self.z + 1, self.dp)
        self.plane, self.column, self.others = [], [], []
        for d in range(1, 4):
            j = (self.chip + d) % 4
            self.plane.append((j, self.at(self.z, j * 2 + self.core)))
        for d in range(1, zs):
            j = (self.z + d) % zs
            self.column.append((j, self.at(j, self.dp)))
        self.me = self.z * 4 + self.chip
        for d in range(1, 4 * zs):
            j = (self.me + d) % (4 * zs)
            self.others.append((j, self.at(j // 4, (j % 4) * 2 + self.core)))

    def at(self, z, dp):
        return {"sp": z, "dp": dp}


class Sum:
    def __init__(self, place, zs, full, half, plane_in, z_in, send, recv, out, by_cols=False):
        self.place, self.full, self.half, self.plane_in, self.z_in = place, full, half, plane_in, z_in
        self.send, self.recv, self.out, self.by_cols = send, recv, out, by_cols
        p = place
        self.R, self.cols = half.shape
        self.rows = self.R // 4
        self.base = pl.multiple_of(p.core * self.R, self.R)
        self.other = pl.multiple_of((1 - p.core) * self.R, self.R)
        self.mine = pl.multiple_of(p.chip * self.rows, self.rows)
        self.z_rows = self.rows if by_cols else self.rows // zs
        self.z_cols = self.cols // zs if by_cols else self.cols

    def z_at(self, j, base):
        if self.by_cols:
            return (pl.ds(base, self.z_rows), pl.ds(pl.multiple_of(j * self.z_cols, self.z_cols), self.z_cols))
        return (pl.ds(pl.multiple_of(base + j * self.z_rows, self.z_rows), self.z_rows), slice(None))

    def copies(self, stage):
        p, n = self.place, len(self.place.column)
        slot = (0, 1, 4, 4 + n, 4 + 2 * n, 7 + 2 * n)[stage]

        def copy(src, dst, where, d=0):
            return remote(src, dst, self.send.at[slot + d], self.recv.at[slot + d], where)

        if stage == 0:
            return [copy(self.full.at[pl.ds(self.other, self.R)], self.half, p.pair)]
        if stage == 1:
            return [
                copy(
                    self.half.at[pl.ds(pl.multiple_of(j * self.rows, self.rows), self.rows)],
                    self.plane_in.at[d],
                    where,
                    d,
                )
                for d, (j, where) in enumerate(p.plane)
            ]
        if stage == 2:
            return [
                copy(self.half.at[self.z_at(j, self.mine)], self.z_in.at[d], where, d)
                for d, (j, where) in enumerate(p.column)
            ]
        if stage == 3:
            src, dst = self.own()
            return [copy(src, dst, where, d) for d, (_, where) in enumerate(p.column)]
        if stage == 4:
            there = self.out.at[pl.ds(pl.multiple_of(self.base + self.mine, self.rows), self.rows)]
            return [copy(there, there, where, d) for d, (_, where) in enumerate(p.plane)]
        there = self.out.at[pl.ds(self.base, self.R)]
        return [copy(there, there, p.pair)]

    def own(self):
        p = self.place
        return self.half.at[self.z_at(p.z, self.mine)], self.out.at[self.z_at(p.z, self.base + self.mine)]

    def own_copy(self):
        src, dst = self.own()
        return pltpu.make_async_copy(src, dst, self.send.at[self.send.shape[0] - 1])

    def add(self, at, parts):
        value = self.half[at].astype(f32)
        for part in parts:
            value = value + part.astype(f32)
        self.half[at] = value.astype(self.half.dtype)

    def step(self, stage):
        if stage > 0:
            for c in self.copies(stage - 1):
                c.wait_recv()
        if stage == 1:
            self.add((slice(None), slice(None)), [self.full[pl.ds(self.base, self.R), :]])
        if stage == 2:
            self.add((pl.ds(self.mine, self.rows), slice(None)), [self.plane_in[d] for d in range(3)])
        if stage == 3:
            n = len(self.place.column)
            self.add(self.z_at(self.place.z, self.mine), [self.z_in[d] for d in range(n)])
            self.own_copy().start()
        if stage == 4:
            self.own_copy().wait()
        if stage < 6:
            for c in self.copies(stage):
                c.start()
        else:
            for k in range(6):
                for c in self.copies(k):
                    c.wait_send()


class SmallSum:
    def __init__(self, place, zs, full, pair_in, rows_in, send, recv, out):
        self.place, self.full, self.pair_in, self.rows_in = place, full, pair_in, rows_in
        self.send, self.recv, self.out = send, recv, out
        p = place
        n = self.n = 4 * zs
        self.rows = full.shape[0] // n
        self.me, self.others = p.me, p.others

    def part(self, j):
        return pl.ds(pl.multiple_of(j * self.rows, self.rows), self.rows)

    def copies(self, stage):
        n = self.n
        if stage == 0:
            return [remote(self.full, self.pair_in, self.send.at[0], self.recv.at[0], self.place.pair)]
        out = []
        for d, (j, where) in enumerate(self.others):
            slot = (stage - 1) * (n - 1) + 1 + d
            if stage == 1:
                src, dst = self.full.at[self.part(j)], self.rows_in.at[d]
            else:
                src, dst = self.full.at[self.part(self.me)], self.out.at[self.part(self.me)]
            out.append(remote(src, dst, self.send.at[slot], self.recv.at[slot], where))
        return out

    def own_copy(self):
        return pltpu.make_async_copy(
            self.full.at[self.part(self.me)], self.out.at[self.part(self.me)], self.send.at[self.send.shape[0] - 1]
        )

    def step(self, stage):
        if stage > 0:
            for c in self.copies(stage - 1):
                c.wait_recv()
        if stage == 1:
            for c in self.copies(0):
                c.wait_send()
            self.full[...] += self.pair_in[...]
        if stage == 2:
            value = self.full[self.part(self.me), :]
            for d in range(self.n - 1):
                value = value + self.rows_in[d]
            self.full[self.part(self.me), :] = value
            self.own_copy().start()
        if stage < 3:
            for c in self.copies(stage):
                c.start()
        else:
            self.own_copy().wait()
            for k in (1, 2):
                for c in self.copies(k):
                    c.wait_send()


class LateSum:
    def __init__(self, place, zs, full, half, parts_in, send, recv, out):
        self.place, self.full, self.half, self.parts_in = place, full, half, parts_in
        self.send, self.recv, self.out, self.zs = send, recv, out, zs
        p = place
        n = self.n = 4 * zs
        self.R = half.shape[0]
        self.rows, self.cols = half.shape[0] // 4, half.shape[1] // zs
        self.base = pl.multiple_of(p.core * self.R, self.R)
        self.me, self.others = p.me, p.others

    def part(self, j, base):
        return (
            pl.ds(pl.multiple_of(base + (j % 4) * self.rows, self.rows), self.rows),
            pl.ds(pl.multiple_of((j // 4) * self.cols, self.cols), self.cols),
        )

    def copies(self, stage):
        p, n = self.place, self.n
        if stage == 0:
            other = pl.multiple_of((1 - p.core) * self.R, self.R)
            return [remote(self.full.at[pl.ds(other, self.R)], self.half, self.send.at[0], self.recv.at[0], p.pair)]
        if stage == 3:
            there = self.out.at[pl.ds(self.base, self.R)]
            return [remote(there, there, self.send.at[2 * n - 1], self.recv.at[2 * n - 1], p.pair)]
        out = []
        for d, (j, where) in enumerate(self.others):
            slot = (stage - 1) * (n - 1) + 1 + d
            if stage == 1:
                src, dst = self.half.at[self.part(j, 0)], self.parts_in.at[d]
            else:
                src, dst = self.half.at[self.part(self.me, 0)], self.out.at[self.part(self.me, self.base)]
            out.append(remote(src, dst, self.send.at[slot], self.recv.at[slot], where))
        return out

    def own_copy(self):
        return pltpu.make_async_copy(
            self.half.at[self.part(self.me, 0)], self.out.at[self.part(self.me, self.base)], self.send.at[2 * self.n]
        )

    def step(self, stage):
        if stage > 0:
            for c in self.copies(stage - 1):
                c.wait_recv()
        if stage == 1:
            own = self.full[pl.ds(self.base, self.R), :].astype(f32)
            self.half[...] = (self.half[...].astype(f32) + own).astype(self.half.dtype)
        if stage == 2:
            at = self.part(self.me, 0)
            value = self.half[at].astype(f32)
            for d in range(self.n - 1):
                value = value + self.parts_in[d].astype(f32)
            self.half[at] = value.astype(self.half.dtype)
            self.own_copy().start()
        if stage == 3:
            self.own_copy().wait()
        if stage < 4:
            for c in self.copies(stage):
                c.start()
        else:
            for k in range(4):
                for c in self.copies(k):
                    c.wait_send()


def backward_kernel(
    G, T, h, across, nf, steps, zs, stages,
    ext, keep, cot, sh_in, inv2, act, slope_early, slope_late, nm, fh_in, inv1, xhat, gdw_own,
    dw, vec, pw, ew, fwd_own, inv_all, taps, dwk, back,
    own_out, top_in, bot_in, gdw_out, gpw_out, gew_out, small_out,
    held, gres_s, gn_s, gr_s, acc, spec, gpw, gew, geb, small, halo_sem, *sums,
):
    step = pl.program_id(0)
    pixels = h * across
    C, HID = sh_in.shape[-1], act.shape[-1]
    HC = 512
    masks = Masks(h, across)
    place = Place(zs)
    names = ("down", "project", "early")
    outs = (gdw_out, gpw_out, gew_out.at[:, pl.ds(0, EARLY)])
    reduced = {}
    if stages is not None:
        for k, name in enumerate(names):
            buffers = list(sums[6 * k : 6 * k + 6])
            if name == "down":
                buffers[0] = gdw_own
            reduced[name] = Sum(place, zs, *buffers, outs[k], by_cols=name == "early")
        reduced["late"] = LateSum(place, zs, *sums[22:27], gew_out.at[:, pl.ds(EARLY, HID - EARLY)])
        reduced["small"] = SmallSum(place, zs, small, *sums[18:22], small_out)

    peers = [place.pair] + [w for _, w in place.others] if stages is not None else [w for _, w in place.column]

    @pl.when(step == 0)
    def _():
        barrier = pltpu.get_barrier_semaphore()
        for where in peers:
            pl.semaphore_signal(barrier, inc=1, device_id=where, device_id_type=MESH)
        for ref in (gpw, gew, geb, small, acc):
            ref[...] = jnp.zeros_like(ref)
        spec[...] = dot_exact(taps[...], tap_rows(dwk))

    @pl.when(step == 1)
    def _():
        pl.semaphore_wait(pltpu.get_barrier_semaphore(), len(peers))

    def run(at):
        for name, stage in stages.get(at, ()):
            if stage == 0 and name == "project":
                reduced[name].full[...] = gpw[...].T.astype(bf16)
            if stage == 0 and name == "early":
                reduced[name].full[...] = gew[:, :EARLY].astype(bf16)
            if stage == 0 and name == "late":
                reduced[name].full[...] = gew[:, EARLY:].astype(bf16)
            reduced[name].step(stage)

    if stages is not None:
        for at in range(4 * steps):
            if at in stages:
                pl.when(step == at)(functools.partial(run, at))

    def row(k):
        return vec[k : k + 1, :]

    def extent(b, g):
        return ext[g * G + b, 0], ext[g * G + b, 1]

    @pl.when(step < steps)
    def _():
        g = step
        coarse = lanes(stack([masks.coarse(*extent(b, g)) for b in range(G)], 0).astype(bf16), cot.shape[-1])
        up = cot[...].reshape(coarse.shape) * coarse
        gdb = total(up.astype(f32))
        for k in range(cot.shape[-1] // C):
            small[V_DB + k : V_DB + k + 1, :] += gdb[:, k * C : (k + 1) * C]
        for p in range(2):
            for q in range(2):
                k = 2 * p + q
                slab = dot_nt(up, dw[k * C : (k + 1) * C, :])
                for n in range(C // 128):
                    gr_s[n, :, p, pl.ds(q, across // 2, stride=2), :] = slab[:, n * 128 : (n + 1) * 128].reshape(
                        G * h // 2, across // 2, 128
                    )
        for team in range(G // T):
            here = pl.ds(team * T * pixels, T * pixels)
            valids = [masks.own(*extent(team * T + t, g)) for t in range(T)]
            facs = [
                valids[t] * (keep[g * G + team * T + t].astype(f32) * (1.0 / survival)) for t in range(T)
            ]
            rows = T * h // 2
            gr = stack(
                [gr_s[n, team * rows : (team + 1) * rows].reshape(T * pixels, 128) for n in range(C // 128)], 1
            )
            gr = gr * lanes(stack(valids, 0), C)
            sh = sh_in[here, :].astype(f32)
            small[V_DG : V_DG + 1, :] += total(gr * sh)
            small[V_DS : V_DS + 1, :] += total(gr)
            u = gr * row(DG)
            gres = lanes(inv2[here, :], C) * (u - mean(u) - sh * mean(u * sh))
            first = pl.multiple_of(g * (G * pixels) + team * T * pixels, T * pixels)
            gres_s[pl.ds(first, T * pixels), :] = gres.astype(bf16)
            gb = (gres * lanes(stack(facs, 0), C) * row(LS)).astype(bf16)
            for t in range(T):
                held[g * G + team * T + t, :pixels] = gb[t * pixels : (t + 1) * pixels]
            small[V_PB : V_PB + 1, :] += total(gb.astype(f32))
            gpw[...] += dot_tn(gb, act[here, :])

    def hidden_back(g, team, slope, columns):
        here = pl.ds(team * T * pixels, T * pixels)
        gb = stack([held[g * G + team * T + t, :pixels] for t in range(T)], 0)
        gn = None
        for first in range(columns.start, columns.stop, HC):
            part = slice(first, first + HC)
            own = slice(first - columns.start, first - columns.start + HC)
            gh = (dot_nt(gb, pw[part, :]) * slope[here, own].astype(f32)).astype(bf16)
            geb[:, part] += total(gh.astype(f32))
            gew[:, part] += dot_tn(nm[here, :], gh)
            term = dot_nt(gh, ew[:, part])
            gn = term if gn is None else gn + term
        return gn

    @pl.when((step >= steps) & (step < 2 * steps))
    def _():
        g = step - steps
        for team in range(G // T):
            gn = hidden_back(g, team, slope_early, slice(0, EARLY))
            gn_s[pl.ds(pl.multiple_of(g * (G * pixels) + team * T * pixels, T * pixels), T * pixels), :] = gn

    @pl.when((step >= 2 * steps) & (step < 3 * steps))
    def _():
        g = step - 2 * steps
        for team in range(G // T):
            gn = hidden_back(g, team, slope_late, slice(EARLY, HID))
            gn_s[pl.ds(pl.multiple_of(g * (G * pixels) + team * T * pixels, T * pixels), T * pixels), :] += gn

    def halo(target, g, side, where):
        part, edge = pl.ds(pl.multiple_of(g * G, G), G), 3 * across
        src = held.at[part, pl.ds(side * edge, edge)]
        return remote(src, target.at[part], halo_sem.at[0, side, g], halo_sem.at[1, side, g], where)

    def up(g):
        return halo(bot_in, g, 0, place.above)

    def down(g):
        return halo(top_in, g, 1, place.below)

    @pl.when(step >= 3 * steps)
    def _():
        g = step - 3 * steps
        edge = 3 * across
        kr, ki = lanes(spec[:nf], T * C), lanes(spec[nf:], T * C)
        for team in range(G // T):
            here = pl.ds(team * T * pixels, T * pixels)
            first = pl.multiple_of(g * (G * pixels) + team * T * pixels, T * pixels)
            gn = gn_s[pl.ds(first, T * pixels), :]
            fh = fh_in[here, :].astype(f32)
            small[V_NG : V_NG + 1, :] += total(gn * fh)
            small[V_NB : V_NB + 1, :] += total(gn)
            w = gn * row(NG)
            gm = lanes(inv1[here, :], C) * (w - mean(w) - fh * mean(w * fh))
            small[V_DWB : V_DWB + 1, :] += total(gm)
            gm = gm.astype(bf16)
            gm = stack([gm[t * pixels : (t + 1) * pixels] for t in range(T)], 1)
            hat = dot(fwd_own[...], gm)
            gr, gi = hat[:nf], hat[nf:]
            sr, si = acc[:nf], acc[nf:]
            for t in range(T):
                at = slice(t * C, (t + 1) * C)
                xr, xi = xhat[team * T + t, :nf].astype(f32), xhat[team * T + t, nf:].astype(f32)
                sr = sr + gr[:, at] * xr + gi[:, at] * xi
                si = si + gr[:, at] * xi - gi[:, at] * xr
            acc[:nf] = sr
            acc[nf:] = si
            product = jnp.concatenate(
                [(gr * kr + gi * ki).astype(bf16), (gi * kr - gr * ki).astype(bf16)], axis=0
            )
            o = dot(inv_all[...], product)
            for t in range(T):
                b = g * G + team * T + t
                each = o[:, t * C : (t + 1) * C] * lanes(masks.every(ext[b, 0], ext[b, 1]), C)
                held[b, :edge] = each[:edge].astype(bf16)
                own = gres_s[pl.ds(pl.multiple_of(b * pixels, pixels), pixels), :].astype(f32)
                own_out[team * T + t] = (each[edge : edge + pixels] + own).astype(bf16)
                held[b, edge : 2 * edge] = each[edge + pixels :].astype(bf16)
        pl.when(place.z > 0)(lambda: up(g).start())
        pl.when(place.z < zs - 1)(lambda: down(g).start())

    @pl.when(step == 4 * steps - 1)
    def _():
        small[0:56, :] = dot_exact(back[...], acc[...])
        for k in range(HID // C):
            small[V_EB + k : V_EB + k + 1, :] = geb[:, k * C : (k + 1) * C]
        if stages is not None:
            run(4 * steps)
        else:
            for k, (src, dst) in enumerate(((gpw, gpw_out), (gew, gew_out), (small, small_out))):
                c = pltpu.make_async_copy(src, dst, sums[0].at[k])
                c.start()
                c.wait()

        @pl.when(place.z > 0)
        def _():
            for g in range(steps):
                up(g).wait_send()
                down(g).wait_recv()

        @pl.when(place.z < zs - 1)
        def _():
            for g in range(steps):
                down(g).wait_send()
                up(g).wait_recv()


def schedule():
    at = {
        "down": (1, 2, 7, 10, 13),
        "project": (4, 5, 9, 12, 14),
        "early": (8, 9, 12, 14, 15),
        "late": (12, 13, 15),
    }
    table = {}
    for name, when in at.items():
        for stage, step in enumerate(when):
            table.setdefault(step, []).append((name, stage))
    d, p, e, q, s = "down", "project", "early", "late", "small"
    table[16] = [
        (s, 0), (d, 5), (s, 1), (p, 5), (e, 5), (q, 3), (s, 2), (d, 6), (p, 6), (e, 6), (q, 4), (s, 3),
    ]
    return table


def backward(fused, zs, G, T, h, across, nf, n_img, ext, keep, cot, sh, inv2, act, slope_early, slope_late, nm, fh, inv1, xhat, gdw, *consts):
    pixels, C, CO = h * across, sh.shape[-1], cot.shape[-1]
    HID = act.shape[1]
    Q, NP, steps = pixels // 4, n_img * pixels, n_img // G

    def group(first):
        return lambda t: jnp.clip(t - first, 0, steps - 1)

    def img(first, *s):
        return pl.BlockSpec((G,) + s, lambda t: (group(first)(t),) + (0,) * len(s))

    def pix(first, c):
        return pl.BlockSpec((G * pixels, c), lambda t: (group(first)(t), 0))

    any_space = pl.BlockSpec(memory_space=pl.ANY)
    smem = pl.BlockSpec(memory_space=pltpu.SMEM)
    sds = jax.ShapeDtypeStruct

    def sum_buffers(rows, cols, by_cols, dtype, full):
        half = rows // 2
        z = (half // 4, cols // zs) if by_cols else (half // 4 // zs, cols)
        n = 8 + 2 * (zs - 1)
        return [
            pltpu.VMEM((rows, cols) if full else (16, 128), dtype),
            pltpu.VMEM((half, cols), dtype),
            pltpu.VMEM((3, half // 4, cols), dtype),
            pltpu.VMEM((zs - 1,) + z, dtype),
            pltpu.SemaphoreType.DMA((n + 1,)),
            pltpu.SemaphoreType.DMA((n,)),
        ]

    if fused:
        sums = sum_buffers(4 * C, CO, False, bf16, False)
        sums += sum_buffers(HID, C, False, bf16, True)
        sums += sum_buffers(C, EARLY, True, bf16, True)
        n = 4 * zs
        sums += [
            pltpu.VMEM((SMALL, C), f32),
            pltpu.VMEM((n - 1, SMALL // n, C), f32),
            pltpu.SemaphoreType.DMA((2 * n,)),
            pltpu.SemaphoreType.DMA((2 * n - 1,)),
        ]
        late = HID - EARLY
        sums += [
            pltpu.VMEM((C, late), bf16),
            pltpu.VMEM((C // 2, late), bf16),
            pltpu.VMEM((n - 1, C // 8, late // zs), bf16),
            pltpu.SemaphoreType.DMA((2 * n + 1,)),
            pltpu.SemaphoreType.DMA((2 * n,)),
        ]
        results = [sds((4 * C, CO), bf16), sds((HID, C), bf16), sds((C, HID), bf16)]
    else:
        sums = [pltpu.SemaphoreType.DMA((3,))]
        results = [sds((16, 128), bf16), sds((C, HID), f32), sds((C, HID), f32)]
        gdw = gdw[:16, :128]
    return pl.pallas_call(
        functools.partial(backward_kernel, G, T, h, across, nf, steps, zs, schedule() if fused else None),
        grid=(4 * steps,),
        in_specs=[
            smem, smem, img(0, Q, CO), pix(0, C), pix(0, 128), pix(0, HID), pix(steps, EARLY),
            pl.BlockSpec((G * pixels, HID - EARLY), lambda t: (group(2 * steps)(t), 0)),
            pl.BlockSpec((G * pixels, C), lambda t: (jnp.clip(t - steps, 0, 2 * steps - 1) % steps, 0)), pix(3 * steps, C),
            pix(3 * steps, 128), img(3 * steps, 2 * nf, C), whole(gdw),
        ]
        + [whole(a) for a in consts],
        out_specs=[img(3 * steps, pixels, C)] + [any_space] * 6,
        out_shape=[
            sds((n_img, pixels, C), bf16), sds((n_img, 3 * across, C), bf16), sds((n_img, 3 * across, C), bf16),
        ]
        + results
        + [sds((SMALL, C), f32)],
        scratch_shapes=[
            pltpu.VMEM((n_img, max(pixels, 6 * across), C), bf16), pltpu.VMEM((NP, C), bf16), pltpu.VMEM((NP, C), f32), pltpu.VMEM((C // 128, G * h // 2, 2, across, 128), f32),
            pltpu.VMEM((2 * nf, C), f32), pltpu.VMEM((2 * nf, C), f32), pltpu.VMEM((C, HID), f32), pltpu.VMEM((C, HID), f32),
            pltpu.VMEM((1, HID), f32), pltpu.VMEM((SMALL, C), f32),
            pltpu.SemaphoreType.DMA((2, 2, steps)),
        ]
        + sums,
        compiler_params=pltpu.CompilerParams(vmem_limit_bytes=VMEM, collective_id=0, has_side_effects=True),
        name="backward",
    )(ext, keep, cot, sh, inv2, act, slope_early, slope_late, nm, fh, inv1, xhat, gdw, *consts)


def per_device(n_sp, n_dp, *arrays):
    (
        tokens, extents, keep_mask, cotangent, dw_kernel, dw_bias, norm_gain, norm_bias, expand_weight, expand_bias,
        project_weight, project_bias, layer_scale, down_gain, down_shift, down_weight, down_bias,
    ) = arrays
    n_img, h, across, C = tokens.shape
    CO, HID = cotangent.shape[-1], expand_weight.shape[1]
    pixels = h * across
    G, T = 1024 // pixels, 512 // pixels
    fused = n_sp == 4 and n_dp == 8 and n_img // G == 4
    if not fused:
        G = T
    nf, fwd, inv, fwd_own, inv_all, spectrum, back = tables(h, across)
    fwd, inv, fwd_own, inv_all = (jnp.asarray(a, bf16) for a in (fwd, inv, fwd_own, inv_all))
    taps, back = jnp.asarray(spectrum, f32), jnp.asarray(back, f32)
    z = lax.axis_index("sp")
    first = z * h
    ext = extents - jnp.stack([first, jnp.zeros_like(first)])[None, :]
    own = tokens.reshape(n_img, pixels, C)
    cot = cotangent.reshape(n_img, pixels // 4, CO)
    dw = down_weight.reshape(4 * C, CO)
    vec = jnp.zeros((16, C), f32)
    for k, v in (
        (DWB, dw_bias), (NG, norm_gain), (NB, norm_bias), (PB, project_bias), (LS, layer_scale), (DG, down_gain),
        (DS, down_shift), (DB, down_bias), (EB, expand_bias),
    ):
        rows = v.size // C
        vec = vec + jnp.pad(v.reshape(rows, C), ((k, 16 - rows - k), (0, 0)))
    out, act, slope_early, slope_late, xhat, fh, nm, inv1, sh, inv2, gdw = forward(
        bf16 if fused else f32, n_sp,
        G, T, h, across, nf, n_img, ext, keep_mask, own, cot, fwd, inv, taps, dw_kernel, vec, expand_weight, project_weight, dw,
    )
    grad, from_above, from_below, gdw_sum, gpw, gew, small = backward(
        fused, n_sp, G, T, h, across, nf, n_img, ext, keep_mask, cot, sh, inv2, act, slope_early,
        slope_late, nm, fh, inv1, xhat, gdw, dw, vec, project_weight, expand_weight, fwd_own, inv_all, taps, dw_kernel, back,
    )
    if fused:
        gdw, gpw, gew = (a.astype(f32) for a in (gdw_sum, gpw, gew))
    else:
        gdw, gpw, gew, small = lax.psum((gdw, gpw, gew, small), ("sp", "dp"))
        gpw = gpw.T
    from_above = jnp.where(z > 0, from_above, jnp.zeros_like(from_above)).reshape(n_img, 3, across, C)
    from_below = jnp.where(z < n_sp - 1, from_below, jnp.zeros_like(from_below)).reshape(n_img, 3, across, C)
    gap = ((0, 0), (0, h - 3), (0, 0), (0, 0))
    pog = ((0, 0), (h - 3, 0), (0, 0), (0, 0))
    grad = (
        grad.reshape(n_img, h, across, C).astype(f32)
        + jnp.pad(from_above, gap).astype(f32)
        + jnp.pad(from_below, pog).astype(f32)
    ).astype(bf16)
    gls = (jnp.sum(project_weight.astype(f32) * gpw, axis=0) + project_bias * small[V_PB]) / layer_scale
    gdk = small[:56].reshape(7, 8, C)[:, :7]
    geb = small[V_EB : V_EB + HID // C].reshape(HID)
    gdb = small[V_DB : V_DB + CO // C].reshape(CO)
    return (
        out.reshape(n_img, h // 2, across // 2, CO), grad, gdk, small[V_DWB], small[V_NG], small[V_NB], gew, geb, gpw,
        small[V_PB], gls, small[V_DG], small[V_DS], gdw.reshape(down_weight.shape), gdb,
    )


def solution(mesh):
    maps = P("dp", "sp", None, None)
    return jax.shard_map(
        functools.partial(per_device, mesh.shape["sp"], mesh.shape["dp"]),
        mesh=mesh,
        in_specs=(maps, P("dp", None), P("dp"), maps) + (P(),) * 13,
        out_specs=(maps, maps) + (P(),) * 13,
        check_vma=False,
    )
```

time: 407 us -> 199 us (0.49)
  waiting for transfers between devices: 145 us -> 0 us
  blocking collectives: 73.5 us -> 0 us
  Pallas kernels: 124 us -> 174 us
  local copies, waits for them, and re-layouts: 27.8 us -> 11.4 us
  between operations: 14.2 us -> 0.72 us
  starting transfers between devices: 11.2 us -> 0 us
  other arithmetic: 7.76 us -> 12 us
    psum x1 -> x0, waiting for transfers between devices: 133 us -> none  [per_device(): lax.psum((gdw, gpw, gew, gdk, vecs, geb, gdb), ('sp', 'dp'))]
    psum x1 -> x0, blocking collectives: 73.5 us -> none  [per_device(): lax.psum((gdw, gpw, gew, gdk, vecs, geb, gdb), ('sp', 'dp'))]
    pallas_call x2, Pallas kernels: 124 us -> 174 us  [the longest x1 109 us: backward(): pl.pallas_call(functools.partial(backward_kernel, G, T, h, across, nf, st...]
    ppermute x4 -> x0, waiting for transfers between devices: 12.5 us -> none  [the longest x1 8.6 us: per_device(): lax.ppermute(tokens[:, h - 3:], 'sp', down).reshape(n_img, 3 * across, C)]
    ppermute x4 -> x0, starting transfers between devices: 11.2 us -> none  [the longest x1 4.99 us: per_device(): lax.ppermute(tokens[:, h - 3:], 'sp', down).reshape(n_img, 3 * across, C)]
    unnamed x25 -> x22, local copies, waits for them, and re-layouts: 11.2 us -> 2.71 us
    reshape x11 -> x12, local copies, waits for them, and re-layouts: 13 us -> 8.03 us  [the longest x9 6.18 us: per_device(): vec = vec + jnp.pad(v.reshape(rows, C), ((k, 16 - rows - k), (0, 0)))]
  transfers between devices with their start and end apart: 5 -> 0, of which waited for: 3 -> 0; matrix products, arithmetic and copies ran while one was open for 6% -> 0% of each run, Pallas kernels for 0% -> 0%
where the time goes in v3:
time: 199 us
  Pallas kernels  174 us (87%)
  other arithmetic  12 us (6%)
  local copies, waits for them, and re-layouts  11.4 us (6%)
    pallas_call x1, Pallas kernels, backward(): pl.pallas_call(functools.partial(backward_kernel, G, T, h, across, nf, st...  109 us
    pallas_call x1, Pallas kernels, forward(): pl.pallas_call(functools.partial(forward_kernel, G, T, h, across, nf, zs,...  65.1 us
    reshape x9, local copies, waits for them, and re-layouts, per_device(): vec = vec + jnp.pad(v.reshape(rows, C), ((k, 16 - rows - k), (0, 0)))  6.18 us

profile of v3, /device:TPU:0, one launch (start us, length us, event | category | flops | bytes accessed | tf_op | source)
XLA Modules:
  0.0 198.5 jit_solution(3001760627376172359)
XLA Ops:
  0.6 0.8 copy.38
  1.4 0.1 pad_add_fusion.1
  1.5 0.6 broadcast_subtract_fusion.ext
  2.1 0.7 reshape.104
  2.8 0.7 reshape.103
  3.5 0.7 reshape.102
  4.2 0.7 reshape.101
  4.8 0.7 reshape.100
  5.5 0.7 reshape.99
  6.2 0.7 reshape.98
  6.9 0.7 reshape.97
  7.6 0.7 reshape.96
  8.3 0.6 pad_add_fusion.vec
  8.9 65.1 %forward.1 = (bf16[16,64,768]{2,1,0:T(8,128)(2,1)}, bf16[4096,1536]{1,0:T(8,128)(2,1)}, bf16[4096,1024]{1,0:T(8,128)(2,1)}, bf16[4096,512]{1,0:T(8,128)(2,1)}, b...) custom-call(s32[16,2]{1,0:T(8,128)} %broadcast_subtract_fusion.ext, ...), custom_call_target="tpu_custom_call" | custom-call | tf_op jit(solution)/shard_map/forward/pallas_call | solution.py:288
  74.0 109.3 %backward.1 = (bf16[16,256,384]{2,1,0:T(8,128)(2,1)}, bf16[16,96,384]{2,1,0:T(8,128)(2,1)}, bf16[16,96,384]{2,1,0:T(8,128)(2,1)}, bf16[1536,768]{1,0:T(8,128)(2,...) custom-call(s32[16,2]{1,0:T(8,128)} %broadcast_subtract_fusion.ext, s32[16]{0:T(128)} %keep.3, ...), custom_call_target="tpu_custom_call" | custom-call | tf_op jit(solution)/shard_map/backward/pallas_call | solution.py:821
  183.4 0.0 copy-start.1
  183.4 1.6 broadcast_select_fusion
  185.0 0.6 copy-done.1
  185.6 0.0 copy-start.6
  185.6 0.0 copy-start.4
  185.6 2.5 %fusion.1 = bf16[16,8,32,384]{3,2,1,0:T(8,128)(2,1)} fusion(bf16[16,8,32,384]{3,2,1,0:T(8,128)(2,1)S(1)} %bitcast.22, bf16[16,3,32,384]{3,2,1,0:T(8,128)(2,1)S(1)} %bitcast.20, bf16[16,3,32,384]{3,2,1,0:T(8,128)(2,1)S(1)} %bitcast.21), kind=kLoop, calls=%fused_computation.2 | loop fusion | flops 9437184 | bytes 8650752 | tf_op jit(solution)/shard_map/convert_element_type | solution.py:898
  188.1 0.0 copy-start
  188.1 0.0 copy-start.5
  188.1 0.0 copy-done.6
  188.1 0.6 slice_bitcast_fusion
  188.7 0.6 slice_reduce_fusion
  189.3 0.0 copy-start.9
  189.3 0.0 copy-done.4
  189.3 1.7 convert_element_type.52
  191.0 0.6 reshape.110
  191.6 0.0 copy-done
  191.7 0.0 copy-done.5
  191.7 0.0 copy-start.7
  191.7 0.0 copy-start.8
  191.7 0.0 copy-start.2
  191.7 1.7 multiply_reduce_fusion
  193.4 0.0 copy-done.9
  193.4 0.0 copy-done.7
  193.4 0.0 copy-done.8
  193.4 0.6 add_divide_fusion
  194.0 0.2 copy-done.2
  194.2 0.0 copy-start.3
  194.2 2.6 %convert.3 = f32[2,2,384,768]{3,2,1,0:T(8,128)} convert(bf16[2,2,384,768]{3,2,1,0:T(8,128)(2,1)S(1)} %bitcast.23) | non-fusion elementwise | flops 1179648 | bytes 7077888 | tf_op jit(solution)/shard_map/reshape | solution.py:905
  196.8 0.6 reshape.113
  197.4 0.0 copy-done.3
  197.4 1.1 copy.40
  (2 shorter events, 0.0 us)
Async XLA Ops:
  183.4 2.2 %copy-start.1 = (bf16[16,256,384]{2,1,0:T(8,128)(2,1)S(1)}, bf16[16,256,384]{2,1,0:T(8,128)(2,1)}, u32[]{:S(2)}) copy-start(bf16[16,256,384]{2,1,0:T(8,128)(2,1)} %get-tuple-element.44) | copy-start | bytes 9437188
  185.6 2.5 %copy-start.6 = (f32[128,384]{1,0:T(8,128)S(1)}, f32[128,384]{1,0:T(8,128)}, u32[]{:S(2)}) copy-start(f32[128,384]{1,0:T(8,128)} %get-tuple-element.47) | copy-start | bytes 589828
  185.6 3.7 %copy-start.4 = (bf16[384,1536]{1,0:T(8,128)(2,1)S(1)}, bf16[384,1536]{1,0:T(8,128)(2,1)}, u32[]{:S(2)}) copy-start(bf16[384,1536]{1,0:T(8,128)(2,1)} %get-tuple-element.48) | copy-start | bytes 3538948
  188.1 3.6 %copy-start = (bf16[1536,384]{1,0:T(8,128)(2,1)S(1)}, bf16[1536,384]{1,0:T(8,128)(2,1)}, u32[]{:S(2)}) copy-start(bf16[1536,384]{1,0:T(8,128)(2,1)} %pw.3) | copy-start | bytes 3538948
  188.1 3.6 %copy-start.5 = (bf16[1536,384]{1,0:T(8,128)(2,1)S(1)}, bf16[1536,384]{1,0:T(8,128)(2,1)}, u32[]{:S(2)}) copy-start(bf16[1536,384]{1,0:T(8,128)(2,1)} %get-tuple-element.49) | copy-start | bytes 3538948
  189.3 4.1 %copy-start.9 = (f32[384]{0:T(512)}, f32[384]{0:T(512)S(1)}, u32[]{:S(2)}) copy-start(f32[384]{0:T(512)S(1)} %get-tuple-element.85) | copy-start | bytes 4612
  191.7 1.8 copy-start.7
  191.7 1.8 copy-start.8
  191.7 2.5 %copy-start.2 = (bf16[1536,768]{1,0:T(8,128)(2,1)S(1)}, bf16[1536,768]{1,0:T(8,128)(2,1)}, u32[]{:S(2)}) copy-start(bf16[1536,768]{1,0:T(8,128)(2,1)} %get-tuple-element.50) | copy-start | bytes 7077892
  194.2 3.2 %copy-start.3 = (bf16[16,64,768]{2,1,0:T(8,128)(2,1)S(1)}, bf16[16,64,768]{2,1,0:T(8,128)(2,1)}, u32[]{:S(2)}) copy-start(bf16[16,64,768]{2,1,0:T(8,128)(2,1)} %get-tuple-element.33) | copy-start | bytes 4718596

commit v4 on v3

--- a/solution.py
+++ b/solution.py
@@ -14,7 +14,6 @@
 survival = 0.875
 VMEM = 63 * 1024 * 1024
 MESH = pl.DeviceIdType.MESH
-EARLY = 1024
 DWB, NG, NB, PB, LS, DG, DS, DB, EB = 0, 1, 2, 3, 4, 5, 6, 7, 9
 SMALL, V_DG, V_DS, V_PB, V_NG, V_NB, V_DWB, V_EB, V_DB = 128, 56, 57, 58, 59, 60, 61, 64, 72
 
@@ -128,6 +127,14 @@
     pl.semaphore_wait(barrier, len(peers))
 
 
+def stack_vectors(vec, refs):
+    C, k = vec.shape[1], 0
+    for ref in refs:
+        for first in range(0, ref.shape[0], C):
+            vec[k : k + 1, :] = ref[first : first + C].reshape(1, C)
+            k += 1
+
+
 def tap_rows(dwk):
     gap = jnp.zeros((1, dwk.shape[-1]), f32)
     return jnp.concatenate([x for i in range(7) for x in (dwk[i], gap)], axis=0)
@@ -135,9 +142,9 @@
 
 def forward_kernel(
     G, T, h, across, nf, zs, steps,
-    ext, keep, tok, own, cot, fwd, inv, taps, dwk, vec, ew, pw, dw,
-    out, act, slope_early, slope_late, xhat, fh_out, nm, inv1_out, sh_out, inv2_out, gdw,
-    top, bot, spec, red, gdw_s, sem,
+    ext, keep, tok, own, cot, fwd, inv, taps, dwk, v0, v1, v2, v3, v4, v5, v6, v7, v8, ew, pw, dw,
+    out, act, slope, xhat, fh_out, nm, inv1_out, sh_out, inv2_out, gdw,
+    top, bot, spec, vec, red, gdw_s, sem,
 ):
     g = pl.program_id(0)
     pixels = h * across
@@ -147,7 +154,7 @@
     above, below = {"sp": z - 1, "dp": dp}, {"sp": z + 1, "dp": dp}
 
     def halo(k, up):
-        part = pl.ds(k * G, G)
+        part = pl.ds(k * T, T)
         if up:
             return remote(tok.at[part, pl.ds(0, edge)], bot.at[part], sem.at[0, 0, k], sem.at[1, 0, k], above)
         return remote(tok.at[part, pl.ds(pixels - edge, edge)], top.at[part], sem.at[0, 1, k], sem.at[1, 1, k], below)
@@ -158,10 +165,16 @@
         if down_act is not None:
             pl.when(z < zs - 1)(lambda: down_act(halo(k, False)))
 
+    parts = steps * G // T
+
+    def arrive(part):
+        pl.when(z < zs - 1)(lambda: halo(part, True).wait_recv())
+        pl.when(z > 0)(lambda: halo(part, False).wait_recv())
+
     @pl.when(g == 0)
     def _():
         greet([{"sp": (z + 1) % zs, "dp": dp}, {"sp": (z + zs - 1) % zs, "dp": dp}])
-        for k in range(steps):
+        for k in range(parts):
             each(k, lambda c: c.start(), lambda c: c.start())
 
         @pl.when(z == 0)
@@ -172,14 +185,16 @@
         def _():
             bot[...] = jnp.zeros_like(bot)
 
+        gdw_s[...] = jnp.zeros_like(gdw_s)
         spec[...] = dot_exact(taps[...], tap_rows(dwk))
-
-    for k in range(steps):
+        stack_vectors(vec, (v0, v1, v2, v3, v4, v5, v6, v7, v8))
+
+    for k in range(1, steps):
 
         @pl.when(g == k)
         def _():
-            pl.when(z < zs - 1)(lambda: halo(k, True).wait_recv())
-            pl.when(z > 0)(lambda: halo(k, False).wait_recv())
+            for part in range(k * (G // T), (k + 1) * (G // T)):
+                arrive(part)
 
     masks = Masks(h, across)
     kr, ki = lanes(spec[:nf], T * C), lanes(spec[nf:], T * C)
@@ -187,6 +202,7 @@
     db = jnp.concatenate([vec[DB + k : DB + k + 1, :] for k in range(cot.shape[-1] // C)], axis=1)
     HC = 512
     for team in range(G // T):
+        pl.when(g == 0)(functools.partial(arrive, team))
         xs, fields, valids, facs = [], [], [], []
         for t in range(T):
             b = team * T + t
@@ -221,10 +237,7 @@
             a, s = gelu_parts(dot(normed, ew[:, part]) + eb[:, part])
             a = a.astype(bf16)
             act[here, part] = a
-            if k * HC < EARLY:
-                slope_early[here, part] = s.astype(bf16)
-            else:
-                slope_late[here, k * HC - EARLY : (k + 1) * HC - EARLY] = s.astype(bf16)
+            slope[here, part] = s.astype(bf16)
             branch = branch + dot(a, pw[part, :])
         valid, fac = stack(valids, 0), stack(facs, 0)
         res = stack(fields, 0).astype(f32) + lanes(fac, C) * (branch * vec[LS : LS + 1, :])
@@ -251,20 +264,12 @@
     coarse = lanes(coarse, cot.shape[-1])
     up = cot[...].reshape(coarse.shape) * coarse.astype(bf16)
     out[...] = ((dot(patch, dw[...]) + db) * coarse).astype(bf16).reshape(out.shape)
-    term = dot_tn(patch, up)
-
-    @pl.when(g == 0)
-    def _():
-        gdw_s[...] = term
-
-    @pl.when(g != 0)
-    def _():
-        gdw_s[...] += term
+    gdw_s[...] += dot_tn(patch, up)
 
     @pl.when(g == steps - 1)
     def _():
         gdw[...] = gdw_s[...].astype(gdw.dtype)
-        for k in range(steps):
+        for k in range(parts):
             each(k, lambda c: c.wait_send(), lambda c: c.wait_send())
 
 
@@ -290,18 +295,19 @@
         grid=(steps,),
         in_specs=[smem, smem, pl.BlockSpec(memory_space=pl.ANY), img(pixels, C), img(Q, CO)] + [whole(a) for a in consts],
         out_specs=[
-            img(Q, CO), pix(HID), pix(EARLY), pix(HID - EARLY), img(2 * nf, C), pix(C), pix(C), pix(128), pix(C), pix(128),
+            img(Q, CO), pix(HID), pix(HID), img(2 * nf, C), pix(C), pix(C), pix(128), pix(C), pix(128),
             pl.BlockSpec((4 * C, CO), lambda g: (0, 0)),
         ],
         out_shape=[
-            sds((n_img, Q, CO), bf16), sds((NP, HID), bf16), sds((NP, EARLY), bf16), sds((NP, HID - EARLY), bf16), sds((n_img, 2 * nf, C), bf16),
+            sds((n_img, Q, CO), bf16), sds((NP, HID), bf16), sds((NP, HID), bf16), sds((n_img, 2 * nf, C), bf16),
             sds((NP, C), bf16), sds((NP, C), bf16), sds((NP, 128), f32), sds((NP, C), bf16), sds((NP, 128), f32),
             sds((4 * C, CO), sum_type),
         ],
         scratch_shapes=[
             pltpu.VMEM((n_img, 3 * across, C), bf16), pltpu.VMEM((n_img, 3 * across, C), bf16),
-            pltpu.VMEM((2 * nf, C), f32), pltpu.VMEM((C // 128, G * h // 2, 2, across, 128), f32), pltpu.VMEM((4 * C, CO), f32),
-            pltpu.SemaphoreType.DMA((2, 2, steps)),
+            pltpu.VMEM((2 * nf, C), f32), pltpu.VMEM((16, C), f32), pltpu.VMEM((C // 128, G * h // 2, 2, across, 128), f32),
+            pltpu.VMEM((4 * C, CO), f32),
+            pltpu.SemaphoreType.DMA((2, 2, n_img // T)),
         ],
         compiler_params=pltpu.CompilerParams(vmem_limit_bytes=VMEM, collective_id=1, has_side_effects=True),
         name="forward",
@@ -473,77 +479,12 @@
                     c.wait_send()
 
 
-class LateSum:
-    def __init__(self, place, zs, full, half, parts_in, send, recv, out):
-        self.place, self.full, self.half, self.parts_in = place, full, half, parts_in
-        self.send, self.recv, self.out, self.zs = send, recv, out, zs
-        p = place
-        n = self.n = 4 * zs
-        self.R = half.shape[0]
-        self.rows, self.cols = half.shape[0] // 4, half.shape[1] // zs
-        self.base = pl.multiple_of(p.core * self.R, self.R)
-        self.me, self.others = p.me, p.others
-
-    def part(self, j, base):
-        return (
-            pl.ds(pl.multiple_of(base + (j % 4) * self.rows, self.rows), self.rows),
-            pl.ds(pl.multiple_of((j // 4) * self.cols, self.cols), self.cols),
-        )
-
-    def copies(self, stage):
-        p, n = self.place, self.n
-        if stage == 0:
-            other = pl.multiple_of((1 - p.core) * self.R, self.R)
-            return [remote(self.full.at[pl.ds(other, self.R)], self.half, self.send.at[0], self.recv.at[0], p.pair)]
-        if stage == 3:
-            there = self.out.at[pl.ds(self.base, self.R)]
-            return [remote(there, there, self.send.at[2 * n - 1], self.recv.at[2 * n - 1], p.pair)]
-        out = []
-        for d, (j, where) in enumerate(self.others):
-            slot = (stage - 1) * (n - 1) + 1 + d
-            if stage == 1:
-                src, dst = self.half.at[self.part(j, 0)], self.parts_in.at[d]
-            else:
-                src, dst = self.half.at[self.part(self.me, 0)], self.out.at[self.part(self.me, self.base)]
-            out.append(remote(src, dst, self.send.at[slot], self.recv.at[slot], where))
-        return out
-
-    def own_copy(self):
-        return pltpu.make_async_copy(
-            self.half.at[self.part(self.me, 0)], self.out.at[self.part(self.me, self.base)], self.send.at[2 * self.n]
-        )
-
-    def step(self, stage):
-        if stage > 0:
-            for c in self.copies(stage - 1):
-                c.wait_recv()
-        if stage == 1:
-            own = self.full[pl.ds(self.base, self.R), :].astype(f32)
-            self.half[...] = (self.half[...].astype(f32) + own).astype(self.half.dtype)
-        if stage == 2:
-            at = self.part(self.me, 0)
-            value = self.half[at].astype(f32)
-            for d in range(self.n - 1):
-                value = value + self.parts_in[d].astype(f32)
-            self.half[at] = value.astype(self.half.dtype)
-            self.own_copy().start()
-        if stage == 3:
-            self.own_copy().wait()
-        if stage < 4:
-            for c in self.copies(stage):
-                c.start()
-        else:
-            for k in range(4):
-                for c in self.copies(k):
-                    c.wait_send()
-
-
 def backward_kernel(
     G, T, h, across, nf, steps, zs, stages,
-    ext, keep, cot, sh_in, inv2, act, slope_early, slope_late, nm, fh_in, inv1, xhat, gdw_own,
-    dw, vec, pw, ew, fwd_own, inv_all, taps, dwk, back,
+    ext, keep, cot, sh_in, inv2, act, slope, nm, fh_in, inv1, xhat, gdw_own,
+    dw, v0, v1, v2, v3, v4, v5, v6, v7, v8, pw, ew, fwd_own, inv_all, taps, dwk, back,
     own_out, top_in, bot_in, gdw_out, gpw_out, gew_out, small_out,
-    held, gres_s, gn_s, gr_s, acc, spec, gpw, gew, geb, small, halo_sem, *sums,
+    held, gres_s, gn_s, gr_s, acc, spec, vec, gpw, gew, geb, small, halo_sem, *sums,
 ):
     step = pl.program_id(0)
     pixels = h * across
@@ -551,17 +492,16 @@
     HC = 512
     masks = Masks(h, across)
     place = Place(zs)
-    names = ("down", "project", "early")
-    outs = (gdw_out, gpw_out, gew_out.at[:, pl.ds(0, EARLY)])
     reduced = {}
     if stages is not None:
-        for k, name in enumerate(names):
-            buffers = list(sums[6 * k : 6 * k + 6])
-            if name == "down":
-                buffers[0] = gdw_own
-            reduced[name] = Sum(place, zs, *buffers, outs[k], by_cols=name == "early")
-        reduced["late"] = LateSum(place, zs, *sums[22:27], gew_out.at[:, pl.ds(EARLY, HID - EARLY)])
-        reduced["small"] = SmallSum(place, zs, small, *sums[18:22], small_out)
+        wide = gdw_own.shape[1] // 2
+        for k, name in enumerate(("down0", "down1", "project", "expand")):
+            buffers, out = list(sums[6 * k : 6 * k + 6]), {2: gpw_out, 3: gew_out}.get(k)
+            if k < 2:
+                columns = pl.ds(k * wide, wide)
+                buffers[0], out = gdw_own.at[:, columns], gdw_out.at[:, columns]
+            reduced[name] = Sum(place, zs, *buffers, out, by_cols=name == "expand")
+        reduced["small"] = SmallSum(place, zs, small, *sums[24:28], small_out)
 
     peers = [place.pair] + [w for _, w in place.others] if stages is not None else [w for _, w in place.column]
 
@@ -573,6 +513,7 @@
         for ref in (gpw, gew, geb, small, acc):
             ref[...] = jnp.zeros_like(ref)
         spec[...] = dot_exact(taps[...], tap_rows(dwk))
+        stack_vectors(vec, (v0, v1, v2, v3, v4, v5, v6, v7, v8))
 
     @pl.when(step == 1)
     def _():
@@ -582,14 +523,12 @@
         for name, stage in stages.get(at, ()):
             if stage == 0 and name == "project":
                 reduced[name].full[...] = gpw[...].T.astype(bf16)
-            if stage == 0 and name == "early":
-                reduced[name].full[...] = gew[:, :EARLY].astype(bf16)
-            if stage == 0 and name == "late":
-                reduced[name].full[...] = gew[:, EARLY:].astype(bf16)
+            if stage == 0 and name == "expand":
+                reduced[name].full[...] = gew[...].astype(bf16)
             reduced[name].step(stage)
 
     if stages is not None:
-        for at in range(4 * steps):
+        for at in range(3 * steps):
             if at in stages:
                 pl.when(step == at)(functools.partial(run, at))
 
@@ -639,33 +578,21 @@
             small[V_PB : V_PB + 1, :] += total(gb.astype(f32))
             gpw[...] += dot_tn(gb, act[here, :])
 
-    def hidden_back(g, team, slope, columns):
-        here = pl.ds(team * T * pixels, T * pixels)
-        gb = stack([held[g * G + team * T + t, :pixels] for t in range(T)], 0)
-        gn = None
-        for first in range(columns.start, columns.stop, HC):
-            part = slice(first, first + HC)
-            own = slice(first - columns.start, first - columns.start + HC)
-            gh = (dot_nt(gb, pw[part, :]) * slope[here, own].astype(f32)).astype(bf16)
-            geb[:, part] += total(gh.astype(f32))
-            gew[:, part] += dot_tn(nm[here, :], gh)
-            term = dot_nt(gh, ew[:, part])
-            gn = term if gn is None else gn + term
-        return gn
-
     @pl.when((step >= steps) & (step < 2 * steps))
     def _():
         g = step - steps
         for team in range(G // T):
-            gn = hidden_back(g, team, slope_early, slice(0, EARLY))
+            here = pl.ds(team * T * pixels, T * pixels)
+            gb = stack([held[g * G + team * T + t, :pixels] for t in range(T)], 0)
+            gn = None
+            for k in range(HID // HC):
+                part = slice(k * HC, (k + 1) * HC)
+                gh = (dot_nt(gb, pw[part, :]) * slope[here, part].astype(f32)).astype(bf16)
+                geb[:, part] += total(gh.astype(f32))
+                gew[:, part] += dot_tn(nm[here, :], gh)
+                term = dot_nt(gh, ew[:, part])
+                gn = term if gn is None else gn + term
             gn_s[pl.ds(pl.multiple_of(g * (G * pixels) + team * T * pixels, T * pixels), T * pixels), :] = gn
-
-    @pl.when((step >= 2 * steps) & (step < 3 * steps))
-    def _():
-        g = step - 2 * steps
-        for team in range(G // T):
-            gn = hidden_back(g, team, slope_late, slice(EARLY, HID))
-            gn_s[pl.ds(pl.multiple_of(g * (G * pixels) + team * T * pixels, T * pixels), T * pixels), :] += gn
 
     def halo(target, g, side, where):
         part, edge = pl.ds(pl.multiple_of(g * G, G), G), 3 * across
@@ -678,9 +605,9 @@
     def down(g):
         return halo(top_in, g, 1, place.below)
 
-    @pl.when(step >= 3 * steps)
+    @pl.when(step >= 2 * steps)
     def _():
-        g = step - 3 * steps
+        g = step - 2 * steps
         edge = 3 * across
         kr, ki = lanes(spec[:nf], T * C), lanes(spec[nf:], T * C)
         for team in range(G // T):
@@ -719,13 +646,13 @@
         pl.when(place.z > 0)(lambda: up(g).start())
         pl.when(place.z < zs - 1)(lambda: down(g).start())
 
-    @pl.when(step == 4 * steps - 1)
+    @pl.when(step == 3 * steps - 1)
     def _():
         small[0:56, :] = dot_exact(back[...], acc[...])
         for k in range(HID // C):
             small[V_EB + k : V_EB + k + 1, :] = geb[:, k * C : (k + 1) * C]
         if stages is not None:
-            run(4 * steps)
+            run(3 * steps)
         else:
             for k, (src, dst) in enumerate(((gpw, gpw_out), (gew, gew_out), (small, small_out))):
                 c = pltpu.make_async_copy(src, dst, sums[0].at[k])
@@ -746,24 +673,26 @@
 
 
 def schedule():
-    at = {
-        "down": (1, 2, 7, 10, 13),
-        "project": (4, 5, 9, 12, 14),
-        "early": (8, 9, 12, 14, 15),
-        "late": (12, 13, 15),
+    return {
+        1: [("down0", 0)],
+        2: [("down0", 1), ("down1", 0)],
+        3: [("down1", 1)],
+        4: [("project", 0)],
+        5: [("down0", 2), ("project", 1)],
+        6: [("down0", 3), ("down1", 2)],
+        7: [("down1", 3), ("project", 2)],
+        8: [("project", 3), ("expand", 0)],
+        9: [("expand", 1)],
+        10: [("down1", 4), ("expand", 2)],
+        11: [("down0", 4), ("project", 4), ("expand", 3)],
+        12: [
+            ("small", 0), ("down1", 5), ("small", 1), ("down0", 5), ("project", 5), ("expand", 4), ("small", 2), ("expand", 5),
+            ("down0", 6), ("down1", 6), ("project", 6), ("small", 3), ("expand", 6),
+        ],
     }
-    table = {}
-    for name, when in at.items():
-        for stage, step in enumerate(when):
-            table.setdefault(step, []).append((name, stage))
-    d, p, e, q, s = "down", "project", "early", "late", "small"
-    table[16] = [
-        (s, 0), (d, 5), (s, 1), (p, 5), (e, 5), (q, 3), (s, 2), (d, 6), (p, 6), (e, 6), (q, 4), (s, 3),
-    ]
-    return table
-
-
-def backward(fused, zs, G, T, h, across, nf, n_img, ext, keep, cot, sh, inv2, act, slope_early, slope_late, nm, fh, inv1, xhat, gdw, *consts):
+
+
+def backward(fused, zs, G, T, h, across, nf, n_img, ext, keep, cot, sh, inv2, act, slope, nm, fh, inv1, xhat, gdw, *consts):
     pixels, C, CO = h * across, sh.shape[-1], cot.shape[-1]
     HID = act.shape[1]
     Q, NP, steps = pixels // 4, n_img * pixels, n_img // G
@@ -795,23 +724,15 @@
         ]
 
     if fused:
-        sums = sum_buffers(4 * C, CO, False, bf16, False)
+        sums = sum_buffers(4 * C, CO // 2, False, bf16, False) * 2
         sums += sum_buffers(HID, C, False, bf16, True)
-        sums += sum_buffers(C, EARLY, True, bf16, True)
+        sums += sum_buffers(C, HID, True, bf16, True)
         n = 4 * zs
         sums += [
             pltpu.VMEM((SMALL, C), f32),
             pltpu.VMEM((n - 1, SMALL // n, C), f32),
             pltpu.SemaphoreType.DMA((2 * n,)),
             pltpu.SemaphoreType.DMA((2 * n - 1,)),
-        ]
-        late = HID - EARLY
-        sums += [
-            pltpu.VMEM((C, late), bf16),
-            pltpu.VMEM((C // 2, late), bf16),
-            pltpu.VMEM((n - 1, C // 8, late // zs), bf16),
-            pltpu.SemaphoreType.DMA((2 * n + 1,)),
-            pltpu.SemaphoreType.DMA((2 * n,)),
         ]
         results = [sds((4 * C, CO), bf16), sds((HID, C), bf16), sds((C, HID), bf16)]
     else:
@@ -820,15 +741,13 @@
         gdw = gdw[:16, :128]
     return pl.pallas_call(
         functools.partial(backward_kernel, G, T, h, across, nf, steps, zs, schedule() if fused else None),
-        grid=(4 * steps,),
+        grid=(3 * steps,),
         in_specs=[
-            smem, smem, img(0, Q, CO), pix(0, C), pix(0, 128), pix(0, HID), pix(steps, EARLY),
-            pl.BlockSpec((G * pixels, HID - EARLY), lambda t: (group(2 * steps)(t), 0)),
-            pl.BlockSpec((G * pixels, C), lambda t: (jnp.clip(t - steps, 0, 2 * steps - 1) % steps, 0)), pix(3 * steps, C),
-            pix(3 * steps, 128), img(3 * steps, 2 * nf, C), whole(gdw),
+            smem, smem, img(0, Q, CO), pix(0, C), pix(0, 128), pix(0, HID), pix(steps, HID), pix(steps, C), pix(2 * steps, C),
+            pix(2 * steps, 128), img(2 * steps, 2 * nf, C), whole(gdw),
         ]
         + [whole(a) for a in consts],
-        out_specs=[img(3 * steps, pixels, C)] + [any_space] * 6,
+        out_specs=[img(2 * steps, pixels, C)] + [any_space] * 6,
         out_shape=[
             sds((n_img, pixels, C), bf16), sds((n_img, 3 * across, C), bf16), sds((n_img, 3 * across, C), bf16),
         ]
@@ -836,14 +755,14 @@
         + [sds((SMALL, C), f32)],
         scratch_shapes=[
             pltpu.VMEM((n_img, max(pixels, 6 * across), C), bf16), pltpu.VMEM((NP, C), bf16), pltpu.VMEM((NP, C), f32), pltpu.VMEM((C // 128, G * h // 2, 2, across, 128), f32),
-            pltpu.VMEM((2 * nf, C), f32), pltpu.VMEM((2 * nf, C), f32), pltpu.VMEM((C, HID), f32), pltpu.VMEM((C, HID), f32),
+            pltpu.VMEM((2 * nf, C), f32), pltpu.VMEM((2 * nf, C), f32), pltpu.VMEM((16, C), f32), pltpu.VMEM((C, HID), f32), pltpu.VMEM((C, HID), f32),
             pltpu.VMEM((1, HID), f32), pltpu.VMEM((SMALL, C), f32),
             pltpu.SemaphoreType.DMA((2, 2, steps)),
         ]
         + sums,
         compiler_params=pltpu.CompilerParams(vmem_limit_bytes=VMEM, collective_id=0, has_side_effects=True),
         name="backward",
-    )(ext, keep, cot, sh, inv2, act, slope_early, slope_late, nm, fh, inv1, xhat, gdw, *consts)
+    )(ext, keep, cot, sh, inv2, act, slope, nm, fh, inv1, xhat, gdw, *consts)
 
 
 def per_device(n_sp, n_dp, *arrays):
@@ -867,34 +786,30 @@
     own = tokens.reshape(n_img, pixels, C)
     cot = cotangent.reshape(n_img, pixels // 4, CO)
     dw = down_weight.reshape(4 * C, CO)
-    vec = jnp.zeros((16, C), f32)
-    for k, v in (
-        (DWB, dw_bias), (NG, norm_gain), (NB, norm_bias), (PB, project_bias), (LS, layer_scale), (DG, down_gain),
-        (DS, down_shift), (DB, down_bias), (EB, expand_bias),
-    ):
-        rows = v.size // C
-        vec = vec + jnp.pad(v.reshape(rows, C), ((k, 16 - rows - k), (0, 0)))
-    out, act, slope_early, slope_late, xhat, fh, nm, inv1, sh, inv2, gdw = forward(
+    vectors = (
+        dw_bias, norm_gain, norm_bias, project_bias, layer_scale, down_gain, down_shift, down_bias, expand_bias
+    )
+    out, act, slope, xhat, fh, nm, inv1, sh, inv2, gdw = forward(
         bf16 if fused else f32, n_sp,
-        G, T, h, across, nf, n_img, ext, keep_mask, own, cot, fwd, inv, taps, dw_kernel, vec, expand_weight, project_weight, dw,
+        G, T, h, across, nf, n_img, ext, keep_mask, own, cot, fwd, inv, taps, dw_kernel, *vectors, expand_weight, project_weight, dw,
     )
     grad, from_above, from_below, gdw_sum, gpw, gew, small = backward(
-        fused, n_sp, G, T, h, across, nf, n_img, ext, keep_mask, cot, sh, inv2, act, slope_early,
-        slope_late, nm, fh, inv1, xhat, gdw, dw, vec, project_weight, expand_weight, fwd_own, inv_all, taps, dw_kernel, back,
+        fused, n_sp, G, T, h, across, nf, n_img, ext, keep_mask, cot, sh, inv2, act, slope,
+        nm, fh, inv1, xhat, gdw, dw, *vectors, project_weight, expand_weight, fwd_own, inv_all, taps, dw_kernel, back,
     )
     if fused:
         gdw, gpw, gew = (a.astype(f32) for a in (gdw_sum, gpw, gew))
     else:
         gdw, gpw, gew, small = lax.psum((gdw, gpw, gew, small), ("sp", "dp"))
         gpw = gpw.T
-    from_above = jnp.where(z > 0, from_above, jnp.zeros_like(from_above)).reshape(n_img, 3, across, C)
-    from_below = jnp.where(z < n_sp - 1, from_below, jnp.zeros_like(from_below)).reshape(n_img, 3, across, C)
+    from_above = jnp.where(z > 0, from_above, jnp.zeros_like(from_above))
+    from_below = jnp.where(z < n_sp - 1, from_below, jnp.zeros_like(from_below))
     gap = ((0, 0), (0, h - 3), (0, 0), (0, 0))
     pog = ((0, 0), (h - 3, 0), (0, 0), (0, 0))
     grad = (
         grad.reshape(n_img, h, across, C).astype(f32)
-        + jnp.pad(from_above, gap).astype(f32)
-        + jnp.pad(from_below, pog).astype(f32)
+        + jnp.pad(from_above.reshape(n_img, 3, across, C), gap).astype(f32)
+        + jnp.pad(from_below.reshape(n_img, 3, across, C), pog).astype(f32)
     ).astype(bf16)
     gls = (jnp.sum(project_weight.astype(f32) * gpw, axis=0) + project_bias * small[V_PB]) / layer_scale
     gdk = small[:56].reshape(7, 8, C)[:, :7]

time: 199 us -> 180 us (0.905)
  Pallas kernels: 174 us -> 162 us
  local copies, waits for them, and re-layouts: 11.4 us -> 5.19 us
    pallas_call x1, Pallas kernels: 109 us -> 100 us  [backward(): pl.pallas_call(functools.partial(backward_kernel, G, T, h, across, nf, st...]
    reshape x9 -> x0, local copies, waits for them, and re-layouts: 6.18 us -> none  [per_device(): vec = vec + jnp.pad(v.reshape(rows, C), ((k, 16 - rows - k), (0, 0)))]
    pallas_call x1, Pallas kernels: 65.1 us -> 62.1 us  [forward(): pl.pallas_call(functools.partial(forward_kernel, G, T, h, across, nf, zs,...]
where the time goes in v4:
time: 180 us; the launch traced here: 179 us
  Pallas kernels  162 us (90%)
  other arithmetic  11.4 us (6%)
  local copies, waits for them, and re-layouts  5.19 us (3%)
    pallas_call x1, Pallas kernels, backward(): pl.pallas_call(functools.partial(backward_kernel, G, T, h, across, nf, st...  100 us
    pallas_call x1, Pallas kernels, forward(): pl.pallas_call(functools.partial(forward_kernel, G, T, h, across, nf, zs,...  62.1 us

profile of v4, /device:TPU:0, one launch (start us, length us, event | category | flops | bytes accessed | tf_op | source)
XLA Modules:
  0.0 179.4 jit_solution(2780957996877957227)
XLA Ops:
  0.6 0.8 copy.38
  1.4 0.1 pad_add_fusion
  1.5 0.6 broadcast_subtract_fusion.ext
  2.1 62.1 %forward.1 = (bf16[16,64,768]{2,1,0:T(8,128)(2,1)}, bf16[4096,1536]{1,0:T(8,128)(2,1)}, bf16[4096,1536]{1,0:T(8,128)(2,1)}, bf16[16,512,384]{2,1,0:T(8,128)(2,1)...) custom-call(s32[16,2]{1,0:T(8,128)} %broadcast_subtract_fusion.ext, ...), custom_call_target="tpu_custom_call" | custom-call | tf_op jit(solution)/shard_map/forward/pallas_call | solution.py:293
  64.2 100.0 %backward.1 = (bf16[16,256,384]{2,1,0:T(8,128)(2,1)}, bf16[16,96,384]{2,1,0:T(8,128)(2,1)}, bf16[16,96,384]{2,1,0:T(8,128)(2,1)}, bf16[1536,768]{1,0:T(8,128)(2,...) custom-call(s32[16,2]{1,0:T(8,128)} %broadcast_subtract_fusion.ext, s32[16]{0:T(128)} %keep.3, ...), custom_call_target="tpu_custom_call" | custom-call | tf_op jit(solution)/shard_map/backward/pallas_call | solution.py:742
  164.2 0.0 copy-start.1
  164.2 1.6 broadcast_select_fusion
  165.8 0.6 copy-done.1
  166.4 0.0 copy-start.6
  166.4 0.0 copy-start.4
  166.4 2.5 %fusion.1 = bf16[16,8,32,384]{3,2,1,0:T(8,128)(2,1)} fusion(bf16[16,8,32,384]{3,2,1,0:T(8,128)(2,1)S(1)} %bitcast.22, bf16[16,3,32,384]{3,2,1,0:T(8,128)(2,1)S(1)} %bitcast.20, bf16[16,3,32,384]{3,2,1,0:T(8,128)(2,1)S(1)} %bitcast.21), kind=kLoop, calls=%fused_computation.2 | loop fusion | flops 9437184 | bytes 8650752 | tf_op jit(solution)/shard_map/convert_element_type | solution.py:813
  168.9 0.0 copy-start
  168.9 0.0 copy-start.5
  168.9 0.0 copy-done.6
  168.9 0.6 slice_bitcast_fusion
  169.6 0.6 slice_reduce_fusion
  170.2 0.0 copy-start.9
  170.2 0.0 copy-done.4
  170.2 1.7 convert_element_type.34
  171.9 0.6 reshape.74
  172.5 0.0 copy-done
  172.5 0.0 copy-done.5
  172.5 0.0 copy-start.7
  172.5 0.0 copy-start.8
  172.5 0.0 copy-start.2
  172.5 1.7 multiply_reduce_fusion
  174.3 0.0 copy-done.9
  174.3 0.0 copy-done.7
  174.3 0.0 copy-done.8
  174.3 0.6 add_divide_fusion
  174.9 0.2 copy-done.2
  175.0 0.0 copy-start.3
  175.0 2.6 %convert.3 = f32[2,2,384,768]{3,2,1,0:T(8,128)} convert(bf16[2,2,384,768]{3,2,1,0:T(8,128)(2,1)S(1)} %bitcast.23) | non-fusion elementwise | flops 1179648 | bytes 7077888 | tf_op jit(solution)/shard_map/reshape | solution.py:820
  177.6 0.6 reshape.77
  178.2 0.0 copy-done.3
  178.2 1.1 copy.40
  (2 shorter events, 0.0 us)
Async XLA Ops:
  164.2 2.2 %copy-start.1 = (bf16[16,256,384]{2,1,0:T(8,128)(2,1)S(1)}, bf16[16,256,384]{2,1,0:T(8,128)(2,1)}, u32[]{:S(2)}) copy-start(bf16[16,256,384]{2,1,0:T(8,128)(2,1)} %get-tuple-element.42) | copy-start | bytes 9437188
  166.4 2.5 %copy-start.6 = (f32[128,384]{1,0:T(8,128)S(1)}, f32[128,384]{1,0:T(8,128)}, u32[]{:S(2)}) copy-start(f32[128,384]{1,0:T(8,128)} %get-tuple-element.45) | copy-start | bytes 589828
  166.4 3.7 %copy-start.4 = (bf16[384,1536]{1,0:T(8,128)(2,1)S(1)}, bf16[384,1536]{1,0:T(8,128)(2,1)}, u32[]{:S(2)}) copy-start(bf16[384,1536]{1,0:T(8,128)(2,1)} %get-tuple-element.46) | copy-start | bytes 3538948
  168.9 3.6 %copy-start = (bf16[1536,384]{1,0:T(8,128)(2,1)S(1)}, bf16[1536,384]{1,0:T(8,128)(2,1)}, u32[]{:S(2)}) copy-start(bf16[1536,384]{1,0:T(8,128)(2,1)} %pw.3) | copy-start | bytes 3538948
  168.9 3.6 %copy-start.5 = (bf16[1536,384]{1,0:T(8,128)(2,1)S(1)}, bf16[1536,384]{1,0:T(8,128)(2,1)}, u32[]{:S(2)}) copy-start(bf16[1536,384]{1,0:T(8,128)(2,1)} %get-tuple-element.47) | copy-start | bytes 3538948
  170.2 4.1 %copy-start.9 = (f32[384]{0:T(512)}, f32[384]{0:T(512)S(1)}, u32[]{:S(2)}) copy-start(f32[384]{0:T(512)S(1)} %get-tuple-element.83) | copy-start | bytes 4612
  172.5 1.8 copy-start.7
  172.5 1.8 copy-start.8
  172.5 2.5 %copy-start.2 = (bf16[1536,768]{1,0:T(8,128)(2,1)S(1)}, bf16[1536,768]{1,0:T(8,128)(2,1)}, u32[]{:S(2)}) copy-start(bf16[1536,768]{1,0:T(8,128)(2,1)} %get-tuple-element.48) | copy-start | bytes 7077892
  175.0 3.2 %copy-start.3 = (bf16[16,64,768]{2,1,0:T(8,128)(2,1)S(1)}, bf16[16,64,768]{2,1,0:T(8,128)(2,1)}, u32[]{:S(2)}) copy-start(bf16[16,64,768]{2,1,0:T(8,128)(2,1)} %get-tuple-element.32) | copy-start | bytes 4718596

commit v5 on v4

--- a/solution.py
+++ b/solution.py
@@ -15,7 +15,8 @@
 VMEM = 63 * 1024 * 1024
 MESH = pl.DeviceIdType.MESH
 DWB, NG, NB, PB, LS, DG, DS, DB, EB = 0, 1, 2, 3, 4, 5, 6, 7, 9
-SMALL, V_DG, V_DS, V_PB, V_NG, V_NB, V_DWB, V_EB, V_DB = 128, 56, 57, 58, 59, 60, 61, 64, 72
+V_DG, V_DS, V_PB, V_NG, V_NB, V_DWB, V_DB = 0, 1, 2, 3, 4, 5, 6
+SMALL, S_VEC, S_EB = (64, 512), 0, 24
 
 
 def tables(h, across):
@@ -142,9 +143,9 @@
 
 def forward_kernel(
     G, T, h, across, nf, zs, steps,
-    ext, keep, tok, own, cot, fwd, inv, taps, dwk, v0, v1, v2, v3, v4, v5, v6, v7, v8, ew, pw, dw,
+    ext, keep, tok, own, cot, fwd, inv, taps, dwk, v0, v1, v2, v3, v4, v5, v6, v7, v8, ew_far, pw_far, dw_far,
     out, act, slope, xhat, fh_out, nm, inv1_out, sh_out, inv2_out, gdw,
-    top, bot, spec, vec, red, gdw_s, sem,
+    top, bot, spec, vec, red, gdw_s, ew, pw, dw, sem, weight_sem,
 ):
     g = pl.program_id(0)
     pixels = h * across
@@ -171,8 +172,15 @@
         pl.when(z < zs - 1)(lambda: halo(part, True).wait_recv())
         pl.when(z > 0)(lambda: halo(part, False).wait_recv())
 
+    weights = [
+        pltpu.make_async_copy(src, dst, weight_sem.at[k])
+        for k, (src, dst) in enumerate(((ew_far, ew), (pw_far, pw), (dw_far, dw)))
+    ]
+
     @pl.when(g == 0)
     def _():
+        for c in weights:
+            c.start()
         greet([{"sp": (z + 1) % zs, "dp": dp}, {"sp": (z + zs - 1) % zs, "dp": dp}])
         for k in range(parts):
             each(k, lambda c: c.start(), lambda c: c.start())
@@ -188,6 +196,8 @@
         gdw_s[...] = jnp.zeros_like(gdw_s)
         spec[...] = dot_exact(taps[...], tap_rows(dwk))
         stack_vectors(vec, (v0, v1, v2, v3, v4, v5, v6, v7, v8))
+        for c in weights:
+            c.wait()
 
     for k in range(1, steps):
 
@@ -200,7 +210,7 @@
     kr, ki = lanes(spec[:nf], T * C), lanes(spec[nf:], T * C)
     eb = jnp.concatenate([vec[EB + k : EB + k + 1, :] for k in range(ew.shape[1] // C)], axis=1)
     db = jnp.concatenate([vec[DB + k : DB + k + 1, :] for k in range(cot.shape[-1] // C)], axis=1)
-    HC = 512
+    HC = 256
     for team in range(G // T):
         pl.when(g == 0)(functools.partial(arrive, team))
         xs, fields, valids, facs = [], [], [], []
@@ -289,11 +299,12 @@
         return pl.BlockSpec((G * pixels, c), lambda g: (g, 0))
 
     smem = pl.BlockSpec(memory_space=pltpu.SMEM)
+    far = pl.BlockSpec(memory_space=pl.ANY)
     sds = jax.ShapeDtypeStruct
     return pl.pallas_call(
         functools.partial(forward_kernel, G, T, h, across, nf, zs, steps),
         grid=(steps,),
-        in_specs=[smem, smem, pl.BlockSpec(memory_space=pl.ANY), img(pixels, C), img(Q, CO)] + [whole(a) for a in consts],
+        in_specs=[smem, smem, far, img(pixels, C), img(Q, CO)] + [whole(a) for a in consts[:-3]] + [far] * 3,
         out_specs=[
             img(Q, CO), pix(HID), pix(HID), img(2 * nf, C), pix(C), pix(C), pix(128), pix(C), pix(128),
             pl.BlockSpec((4 * C, CO), lambda g: (0, 0)),
@@ -306,8 +317,8 @@
         scratch_shapes=[
             pltpu.VMEM((n_img, 3 * across, C), bf16), pltpu.VMEM((n_img, 3 * across, C), bf16),
             pltpu.VMEM((2 * nf, C), f32), pltpu.VMEM((16, C), f32), pltpu.VMEM((C // 128, G * h // 2, 2, across, 128), f32),
-            pltpu.VMEM((4 * C, CO), f32),
-            pltpu.SemaphoreType.DMA((2, 2, n_img // T)),
+            pltpu.VMEM((4 * C, CO), f32), pltpu.VMEM((C, HID), bf16), pltpu.VMEM((HID, C), bf16), pltpu.VMEM((4 * C, CO), bf16),
+            pltpu.SemaphoreType.DMA((2, 2, n_img // T)), pltpu.SemaphoreType.DMA((3,)),
         ],
         compiler_params=pltpu.CompilerParams(vmem_limit_bytes=VMEM, collective_id=1, has_side_effects=True),
         name="forward",
@@ -425,35 +436,35 @@
 
 
 class SmallSum:
-    def __init__(self, place, zs, full, pair_in, rows_in, send, recv, out):
-        self.place, self.full, self.pair_in, self.rows_in = place, full, pair_in, rows_in
-        self.send, self.recv, self.out = send, recv, out
-        p = place
-        n = self.n = 4 * zs
-        self.rows = full.shape[0] // n
-        self.me, self.others = p.me, p.others
-
-    def part(self, j):
-        return pl.ds(pl.multiple_of(j * self.rows, self.rows), self.rows)
+    def __init__(self, place, zs, full, pair_in, tiles_in, send, recv, out):
+        self.place, self.full, self.pair_in, self.tiles_in = place, full, pair_in, tiles_in
+        self.send, self.recv, self.out, self.n = send, recv, out, 4 * zs
+
+    def tile(self, chip):
+        p = self.place
+        lane = p.core * 256 + (chip % 2) * 128
+        return (pl.ds(pl.multiple_of((chip // 2) * 8, 8), 8), pl.ds(pl.multiple_of(lane, 128), 128))
 
     def copies(self, stage):
-        n = self.n
+        p, n = self.place, self.n
         if stage == 0:
-            return [remote(self.full, self.pair_in, self.send.at[0], self.recv.at[0], self.place.pair)]
+            return [remote(self.full, self.pair_in, self.send.at[0], self.recv.at[0], p.pair)]
+        if stage == 3:
+            there = self.out.at[:, pl.ds(pl.multiple_of(p.core * 256, 256), 256)]
+            return [remote(there, there, self.send.at[2 * n - 1], self.recv.at[2 * n - 1], p.pair)]
         out = []
-        for d, (j, where) in enumerate(self.others):
+        for d, (j, where) in enumerate(p.others):
             slot = (stage - 1) * (n - 1) + 1 + d
             if stage == 1:
-                src, dst = self.full.at[self.part(j)], self.rows_in.at[d]
+                src, dst = self.full.at[self.tile(j)], self.tiles_in.at[d]
             else:
-                src, dst = self.full.at[self.part(self.me)], self.out.at[self.part(self.me)]
+                src, dst = self.full.at[self.tile(p.me)], self.out.at[self.tile(p.me)]
             out.append(remote(src, dst, self.send.at[slot], self.recv.at[slot], where))
         return out
 
     def own_copy(self):
-        return pltpu.make_async_copy(
-            self.full.at[self.part(self.me)], self.out.at[self.part(self.me)], self.send.at[self.send.shape[0] - 1]
-        )
+        at = self.tile(self.place.me)
+        return pltpu.make_async_copy(self.full.at[at], self.out.at[at], self.send.at[2 * self.n])
 
     def step(self, stage):
         if stage > 0:
@@ -464,27 +475,29 @@
                 c.wait_send()
             self.full[...] += self.pair_in[...]
         if stage == 2:
-            value = self.full[self.part(self.me), :]
+            at = self.tile(self.place.me)
+            value = self.full[at]
             for d in range(self.n - 1):
-                value = value + self.rows_in[d]
-            self.full[self.part(self.me), :] = value
+                value = value + self.tiles_in[d]
+            self.full[at] = value
             self.own_copy().start()
-        if stage < 3:
+        if stage == 3:
+            self.own_copy().wait()
+        if stage < 4:
             for c in self.copies(stage):
                 c.start()
         else:
-            self.own_copy().wait()
-            for k in (1, 2):
+            for k in (1, 2, 3):
                 for c in self.copies(k):
                     c.wait_send()
 
 
 def backward_kernel(
     G, T, h, across, nf, steps, zs, stages,
-    ext, keep, cot, sh_in, inv2, act, slope, nm, fh_in, inv1, xhat, gdw_own,
-    dw, v0, v1, v2, v3, v4, v5, v6, v7, v8, pw, ew, fwd_own, inv_all, taps, dwk, back,
+    ext, keep, cot, sh_in, inv2, act, slope, nm, fh_in, inv1, xhat, gdw_far,
+    dw_far, v0, v1, v2, v3, v4, v5, v6, v7, v8, pw_far, ew_far, fwd_own, inv_all, taps, dwk, back,
     own_out, top_in, bot_in, gdw_out, gpw_out, gew_out, small_out,
-    held, gres_s, gn_s, gr_s, acc, spec, vec, gpw, gew, geb, small, halo_sem, *sums,
+    held, gres_s, gn_s, gr_s, acc, spec, vec, gpw, gew, geb, vsum, small, gdw_own, dw, pw, ew, weight_sem, halo_sem, *sums,
 ):
     step = pl.program_id(0)
     pixels = h * across
@@ -505,18 +518,28 @@
 
     peers = [place.pair] + [w for _, w in place.others] if stages is not None else [w for _, w in place.column]
 
+    weights = [
+        pltpu.make_async_copy(src, dst, weight_sem.at[k])
+        for k, (src, dst) in enumerate(((dw_far, dw), (gdw_far, gdw_own), (pw_far, pw), (ew_far, ew)))
+    ]
+
     @pl.when(step == 0)
     def _():
+        for c in weights:
+            c.start()
         barrier = pltpu.get_barrier_semaphore()
         for where in peers:
             pl.semaphore_signal(barrier, inc=1, device_id=where, device_id_type=MESH)
-        for ref in (gpw, gew, geb, small, acc):
+        for ref in (gpw, gew, geb, vsum, acc):
             ref[...] = jnp.zeros_like(ref)
         spec[...] = dot_exact(taps[...], tap_rows(dwk))
         stack_vectors(vec, (v0, v1, v2, v3, v4, v5, v6, v7, v8))
+        weights[0].wait()
 
     @pl.when(step == 1)
     def _():
+        for c in weights[1:]:
+            c.wait()
         pl.semaphore_wait(pltpu.get_barrier_semaphore(), len(peers))
 
     def run(at):
@@ -545,7 +568,7 @@
         up = cot[...].reshape(coarse.shape) * coarse
         gdb = total(up.astype(f32))
         for k in range(cot.shape[-1] // C):
-            small[V_DB + k : V_DB + k + 1, :] += gdb[:, k * C : (k + 1) * C]
+            vsum[V_DB + k : V_DB + k + 1, :] += gdb[:, k * C : (k + 1) * C]
         for p in range(2):
             for q in range(2):
                 k = 2 * p + q
@@ -566,8 +589,8 @@
             )
             gr = gr * lanes(stack(valids, 0), C)
             sh = sh_in[here, :].astype(f32)
-            small[V_DG : V_DG + 1, :] += total(gr * sh)
-            small[V_DS : V_DS + 1, :] += total(gr)
+            vsum[V_DG : V_DG + 1, :] += total(gr * sh)
+            vsum[V_DS : V_DS + 1, :] += total(gr)
             u = gr * row(DG)
             gres = lanes(inv2[here, :], C) * (u - mean(u) - sh * mean(u * sh))
             first = pl.multiple_of(g * (G * pixels) + team * T * pixels, T * pixels)
@@ -575,7 +598,7 @@
             gb = (gres * lanes(stack(facs, 0), C) * row(LS)).astype(bf16)
             for t in range(T):
                 held[g * G + team * T + t, :pixels] = gb[t * pixels : (t + 1) * pixels]
-            small[V_PB : V_PB + 1, :] += total(gb.astype(f32))
+            vsum[V_PB : V_PB + 1, :] += total(gb.astype(f32))
             gpw[...] += dot_tn(gb, act[here, :])
 
     @pl.when((step >= steps) & (step < 2 * steps))
@@ -615,11 +638,11 @@
             first = pl.multiple_of(g * (G * pixels) + team * T * pixels, T * pixels)
             gn = gn_s[pl.ds(first, T * pixels), :]
             fh = fh_in[here, :].astype(f32)
-            small[V_NG : V_NG + 1, :] += total(gn * fh)
-            small[V_NB : V_NB + 1, :] += total(gn)
+            vsum[V_NG : V_NG + 1, :] += total(gn * fh)
+            vsum[V_NB : V_NB + 1, :] += total(gn)
             w = gn * row(NG)
             gm = lanes(inv1[here, :], C) * (w - mean(w) - fh * mean(w * fh))
-            small[V_DWB : V_DWB + 1, :] += total(gm)
+            vsum[V_DWB : V_DWB + 1, :] += total(gm)
             gm = gm.astype(bf16)
             gm = stack([gm[t * pixels : (t + 1) * pixels] for t in range(T)], 1)
             hat = dot(fwd_own[...], gm)
@@ -648,9 +671,13 @@
 
     @pl.when(step == 3 * steps - 1)
     def _():
-        small[0:56, :] = dot_exact(back[...], acc[...])
-        for k in range(HID // C):
-            small[V_EB + k : V_EB + k + 1, :] = geb[:, k * C : (k + 1) * C]
+        small[...] = jnp.zeros_like(small)
+        small[0:56, 0:C] = dot_exact(back[...], acc[...])
+        for k in range(8 * C // 128):
+            v, at = divmod(k, C // 128)
+            small[S_VEC + k : S_VEC + k + 1, C:] = vsum[v : v + 1, at * 128 : (at + 1) * 128]
+        for k in range(HID // 128):
+            small[S_EB + k : S_EB + k + 1, C:] = geb[:, k * 128 : (k + 1) * 128]
         if stages is not None:
             run(3 * steps)
         else:
@@ -674,20 +701,20 @@
 
 def schedule():
     return {
-        1: [("down0", 0)],
-        2: [("down0", 1), ("down1", 0)],
-        3: [("down1", 1)],
+        1: [("down1", 0)],
+        2: [("down1", 1), ("down0", 0)],
+        3: [("down0", 1)],
         4: [("project", 0)],
-        5: [("down0", 2), ("project", 1)],
-        6: [("down0", 3), ("down1", 2)],
-        7: [("down1", 3), ("project", 2)],
-        8: [("project", 3), ("expand", 0)],
-        9: [("expand", 1)],
-        10: [("down1", 4), ("expand", 2)],
-        11: [("down0", 4), ("project", 4), ("expand", 3)],
+        5: [("down1", 2), ("project", 1)],
+        6: [("down0", 2), ("down1", 3)],
+        7: [("down0", 3), ("project", 2)],
+        8: [("expand", 0), ("project", 3)],
+        9: [("down0", 4), ("expand", 1)],
+        10: [("project", 4), ("expand", 2)],
+        11: [("down1", 4), ("expand", 3)],
         12: [
-            ("small", 0), ("down1", 5), ("small", 1), ("down0", 5), ("project", 5), ("expand", 4), ("small", 2), ("expand", 5),
-            ("down0", 6), ("down1", 6), ("project", 6), ("small", 3), ("expand", 6),
+            ("small", 0), ("down0", 5), ("small", 1), ("project", 5), ("expand", 4), ("down1", 5), ("small", 2), ("expand", 5),
+            ("small", 3), ("down0", 6), ("project", 6), ("down1", 6), ("small", 4), ("expand", 6),
         ],
     }
 
@@ -729,10 +756,10 @@
         sums += sum_buffers(C, HID, True, bf16, True)
         n = 4 * zs
         sums += [
-            pltpu.VMEM((SMALL, C), f32),
-            pltpu.VMEM((n - 1, SMALL // n, C), f32),
+            pltpu.VMEM(SMALL, f32),
+            pltpu.VMEM((n - 1, 8, 128), f32),
+            pltpu.SemaphoreType.DMA((2 * n + 1,)),
             pltpu.SemaphoreType.DMA((2 * n,)),
-            pltpu.SemaphoreType.DMA((2 * n - 1,)),
         ]
         results = [sds((4 * C, CO), bf16), sds((HID, C), bf16), sds((C, HID), bf16)]
     else:
@@ -744,20 +771,23 @@
         grid=(3 * steps,),
         in_specs=[
             smem, smem, img(0, Q, CO), pix(0, C), pix(0, 128), pix(0, HID), pix(steps, HID), pix(steps, C), pix(2 * steps, C),
-            pix(2 * steps, 128), img(2 * steps, 2 * nf, C), whole(gdw),
+            pix(2 * steps, 128), img(2 * steps, 2 * nf, C), any_space, any_space,
         ]
-        + [whole(a) for a in consts],
+        + [whole(a) for a in consts[1:10]]
+        + [any_space] * 2
+        + [whole(a) for a in consts[12:]],
         out_specs=[img(2 * steps, pixels, C)] + [any_space] * 6,
         out_shape=[
             sds((n_img, pixels, C), bf16), sds((n_img, 3 * across, C), bf16), sds((n_img, 3 * across, C), bf16),
         ]
         + results
-        + [sds((SMALL, C), f32)],
+        + [sds(SMALL, f32)],
         scratch_shapes=[
             pltpu.VMEM((n_img, max(pixels, 6 * across), C), bf16), pltpu.VMEM((NP, C), bf16), pltpu.VMEM((NP, C), f32), pltpu.VMEM((C // 128, G * h // 2, 2, across, 128), f32),
             pltpu.VMEM((2 * nf, C), f32), pltpu.VMEM((2 * nf, C), f32), pltpu.VMEM((16, C), f32), pltpu.VMEM((C, HID), f32), pltpu.VMEM((C, HID), f32),
-            pltpu.VMEM((1, HID), f32), pltpu.VMEM((SMALL, C), f32),
-            pltpu.SemaphoreType.DMA((2, 2, steps)),
+            pltpu.VMEM((1, HID), f32), pltpu.VMEM((8, C), f32), pltpu.VMEM(SMALL, f32),
+            pltpu.VMEM(gdw.shape, gdw.dtype), pltpu.VMEM((4 * C, CO), bf16), pltpu.VMEM((HID, C), bf16), pltpu.VMEM((C, HID), bf16),
+            pltpu.SemaphoreType.DMA((4,)), pltpu.SemaphoreType.DMA((2, 2, steps)),
         ]
         + sums,
         compiler_params=pltpu.CompilerParams(vmem_limit_bytes=VMEM, collective_id=0, has_side_effects=True),
@@ -811,13 +841,18 @@
         + jnp.pad(from_above.reshape(n_img, 3, across, C), gap).astype(f32)
         + jnp.pad(from_below.reshape(n_img, 3, across, C), pog).astype(f32)
     ).astype(bf16)
-    gls = (jnp.sum(project_weight.astype(f32) * gpw, axis=0) + project_bias * small[V_PB]) / layer_scale
-    gdk = small[:56].reshape(7, 8, C)[:, :7]
-    geb = small[V_EB : V_EB + HID // C].reshape(HID)
-    gdb = small[V_DB : V_DB + CO // C].reshape(CO)
+    vectors = small[:, C:].reshape(-1)
+
+    def vector(first, size):
+        return vectors[first * 128 : first * 128 + size]
+
+    gdg, gds, gpb, gng, gnb, gdwb = (vector(S_VEC + k * C // 128, C) for k in range(6))
+    gdb, geb = vector(S_VEC + V_DB * C // 128, CO), vector(S_EB, HID)
+    gls = (jnp.sum(project_weight.astype(f32) * gpw, axis=0) + project_bias * gpb) / layer_scale
+    gdk = small[:56, :C].reshape(7, 8, C)[:, :7]
     return (
-        out.reshape(n_img, h // 2, across // 2, CO), grad, gdk, small[V_DWB], small[V_NG], small[V_NB], gew, geb, gpw,
-        small[V_PB], gls, small[V_DG], small[V_DS], gdw.reshape(down_weight.shape), gdb,
+        out.reshape(n_img, h // 2, across // 2, CO), grad, gdk, gdwb, gng, gnb, gew, geb, gpw, gpb, gls, gdg, gds,
+        gdw.reshape(down_weight.shape), gdb,
     )
 
 

time: 180 us -> 174 us (0.967)
  Pallas kernels: 162 us -> 156 us
    pallas_call x1, Pallas kernels: 62.1 us -> 58.5 us  [forward(): pl.pallas_call(functools.partial(forward_kernel, G, T, h, across, nf, zs,...]
    pallas_call x1, Pallas kernels: 100 us -> 97.9 us  [backward(): pl.pallas_call(functools.partial(backward_kernel, G, T, h, across, nf, st...]
where the time goes in v5:
time: 174 us
  Pallas kernels  156 us (90%)
  other arithmetic  11.4 us (7%)
  local copies, waits for them, and re-layouts  5.12 us (3%)
    pallas_call x1, Pallas kernels, backward(): pl.pallas_call(functools.partial(backward_kernel, G, T, h, across, nf, st...  97.9 us
    pallas_call x1, Pallas kernels, forward(): pl.pallas_call(functools.partial(forward_kernel, G, T, h, across, nf, zs,...  58.5 us

profile of v5, /device:TPU:0, one launch (start us, length us, event | category | flops | bytes accessed | tf_op | source)
XLA Modules:
  0.0 173.6 jit_solution(11244057016508718930)
XLA Ops:
  0.6 0.8 copy.38
  1.4 0.1 pad_add_fusion
  1.5 0.6 broadcast_subtract_fusion.ext
  2.1 58.5 %forward.1 = (bf16[16,64,768]{2,1,0:T(8,128)(2,1)}, bf16[4096,1536]{1,0:T(8,128)(2,1)}, bf16[4096,1536]{1,0:T(8,128)(2,1)}, bf16[16,512,384]{2,1,0:T(8,128)(2,1)...) custom-call(s32[16,2]{1,0:T(8,128)} %broadcast_subtract_fusion.ext, ...), custom_call_target="tpu_custom_call" | custom-call | tf_op jit(solution)/shard_map/forward/pallas_call | solution.py:304
  60.6 97.9 %backward.1 = (bf16[16,256,384]{2,1,0:T(8,128)(2,1)}, bf16[16,96,384]{2,1,0:T(8,128)(2,1)}, bf16[16,96,384]{2,1,0:T(8,128)(2,1)}, bf16[1536,768]{1,0:T(8,128)(2,...) custom-call(s32[16,2]{1,0:T(8,128)} %broadcast_subtract_fusion.ext, s32[16]{0:T(128)} %keep.3, ...), custom_call_target="tpu_custom_call" | custom-call | tf_op jit(solution)/shard_map/backward/pallas_call | solution.py:769
  158.5 0.0 copy-start.1
  158.5 1.6 broadcast_select_fusion
  160.1 0.6 copy-done.1
  160.7 0.0 copy-start.6
  160.7 0.0 copy-start.4
  160.7 2.5 %fusion.1 = bf16[16,8,32,384]{3,2,1,0:T(8,128)(2,1)} fusion(bf16[16,8,32,384]{3,2,1,0:T(8,128)(2,1)S(1)} %bitcast.39, bf16[16,3,32,384]{3,2,1,0:T(8,128)(2,1)S(1)} %bitcast.37, bf16[16,3,32,384]{3,2,1,0:T(8,128)(2,1)S(1)} %bitcast.38), kind=kLoop, calls=%fused_computation.2 | loop fusion | flops 9437184 | bytes 8650752 | tf_op jit(solution)/shard_map/convert_element_type | solution.py:843
  163.2 0.0 copy-start
  163.2 0.0 copy-start.5
  163.2 0.0 copy-done.6
  163.2 0.6 slice_bitcast_fusion
  163.8 0.6 slice_bitcast_fusion.3
  164.4 0.0 copy-done.4
  164.4 1.7 convert_element_type.34
  166.1 0.6 slice_bitcast_fusion.1
  166.7 0.0 copy-done
  166.7 0.0 copy-done.5
  166.7 0.0 copy-start.7
  166.7 0.0 copy-start.8
  166.8 0.0 copy-start.2
  166.8 1.8 %multiply_reduce_fusion = (f32[384]{0:T(512)S(1)}, f32[1536,384]{1,0:T(8,128)}) fusion(bf16[1536,384]{1,0:T(8,128)(2,1)S(1)} %copy-done, bf16[1536,384]{1,0:T(8,128)(2,1)S(1)} %copy-done.5), kind=kLoop, calls=%fused_computation.3 | loop fusion | flops 2358912 | bytes 4720128 | tf_op jit(solution)/shard_map/reduce_sum | solution.py:851
  168.5 0.0 copy-done.7
  168.5 0.0 copy-done.8
  168.5 0.6 add_divide_fusion
  169.1 0.2 copy-done.2
  169.3 0.0 copy-start.3
  169.3 2.6 %convert.3 = f32[2,2,384,768]{3,2,1,0:T(8,128)} convert(bf16[2,2,384,768]{3,2,1,0:T(8,128)(2,1)S(1)} %bitcast.40) | non-fusion elementwise | flops 1179648 | bytes 7077888 | tf_op jit(solution)/shard_map/reshape | solution.py:855
  171.9 0.6 slice_bitcast_fusion.2
  172.5 0.0 copy-done.3
  172.5 1.1 copy.40
Async XLA Ops:
  158.5 2.2 %copy-start.1 = (bf16[16,256,384]{2,1,0:T(8,128)(2,1)S(1)}, bf16[16,256,384]{2,1,0:T(8,128)(2,1)}, u32[]{:S(2)}) copy-start(bf16[16,256,384]{2,1,0:T(8,128)(2,1)} %get-tuple-element.42) | copy-start | bytes 9437188
  160.7 2.5 %copy-start.6 = (f32[64,512]{1,0:T(8,128)S(1)}, f32[64,512]{1,0:T(8,128)}, u32[]{:S(2)}) copy-start(f32[64,512]{1,0:T(8,128)} %get-tuple-element.45) | copy-start | bytes 393220
  160.7 3.7 %copy-start.4 = (bf16[384,1536]{1,0:T(8,128)(2,1)S(1)}, bf16[384,1536]{1,0:T(8,128)(2,1)}, u32[]{:S(2)}) copy-start(bf16[384,1536]{1,0:T(8,128)(2,1)} %get-tuple-element.46) | copy-start | bytes 3538948
  163.2 3.5 %copy-start = (bf16[1536,384]{1,0:T(8,128)(2,1)S(1)}, bf16[1536,384]{1,0:T(8,128)(2,1)}, u32[]{:S(2)}) copy-start(bf16[1536,384]{1,0:T(8,128)(2,1)} %pw_far.3) | copy-start | bytes 3538948
  163.2 3.5 %copy-start.5 = (bf16[1536,384]{1,0:T(8,128)(2,1)S(1)}, bf16[1536,384]{1,0:T(8,128)(2,1)}, u32[]{:S(2)}) copy-start(bf16[1536,384]{1,0:T(8,128)(2,1)} %get-tuple-element.47) | copy-start | bytes 3538948
  166.7 1.8 %copy-start.7 = (f32[384]{0:T(512)S(1)}, f32[384]{0:T(512)}, u32[]{:S(2)}) copy-start(f32[384]{0:T(512)} %v3.3) | copy-start | bytes 4612
  166.7 1.8 %copy-start.8 = (f32[384]{0:T(512)S(1)}, f32[384]{0:T(512)}, u32[]{:S(2)}) copy-start(f32[384]{0:T(512)} %v4.3) | copy-start | bytes 4612
  166.8 2.5 %copy-start.2 = (bf16[1536,768]{1,0:T(8,128)(2,1)S(1)}, bf16[1536,768]{1,0:T(8,128)(2,1)}, u32[]{:S(2)}) copy-start(bf16[1536,768]{1,0:T(8,128)(2,1)} %get-tuple-element.48) | copy-start | bytes 7077892
  169.3 3.2 %copy-start.3 = (bf16[16,64,768]{2,1,0:T(8,128)(2,1)S(1)}, bf16[16,64,768]{2,1,0:T(8,128)(2,1)}, u32[]{:S(2)}) copy-start(bf16[16,64,768]{2,1,0:T(8,128)(2,1)} %get-tuple-element.32) | copy-start | bytes 4718596

commit v6 on v5

--- a/solution.py
+++ b/solution.py
@@ -502,7 +502,7 @@
     step = pl.program_id(0)
     pixels = h * across
     C, HID = sh_in.shape[-1], act.shape[-1]
-    HC = 512
+    HC = 768
     masks = Masks(h, across)
     place = Place(zs)
     reduced = {}
@@ -701,21 +701,18 @@
 
 def schedule():
     return {
-        1: [("down1", 0)],
-        2: [("down1", 1), ("down0", 0)],
-        3: [("down0", 1)],
-        4: [("project", 0)],
-        5: [("down1", 2), ("project", 1)],
-        6: [("down0", 2), ("down1", 3)],
-        7: [("down0", 3), ("project", 2)],
-        8: [("expand", 0), ("project", 3)],
-        9: [("down0", 4), ("expand", 1)],
-        10: [("project", 4), ("expand", 2)],
-        11: [("down1", 4), ("expand", 3)],
-        12: [
-            ("small", 0), ("down0", 5), ("small", 1), ("project", 5), ("expand", 4), ("down1", 5), ("small", 2), ("expand", 5),
-            ("small", 3), ("down0", 6), ("project", 6), ("down1", 6), ("small", 4), ("expand", 6),
-        ],
+        1: [('down0', 0)],
+        2: [('down0', 1), ('down1', 0)],
+        3: [('down1', 1)],
+        4: [('project', 0)],
+        5: [('down0', 2), ('project', 1)],
+        6: [('down0', 3), ('down1', 2)],
+        7: [('down1', 3), ('project', 2)],
+        8: [('project', 3), ('expand', 0)],
+        9: [('expand', 1)],
+        10: [('down1', 4), ('expand', 2)],
+        11: [('down0', 4), ('project', 4), ('expand', 3)],
+        12: [('small', 0), ('down1', 5), ('small', 1), ('down0', 5), ('project', 5), ('expand', 4), ('small', 2), ('expand', 5), ('small', 3), ('down0', 6), ('down1', 6), ('project', 6), ('small', 4), ('expand', 6)],
     }
 
 

time: 174 us -> 171 us (0.983)
  Pallas kernels: 156 us -> 153 us
    pallas_call x1, Pallas kernels: 97.9 us -> 94.9 us  [backward(): pl.pallas_call(functools.partial(backward_kernel, G, T, h, across, nf, st...]
where the time goes in v6:
time: 171 us
  Pallas kernels  153 us (89%)
  other arithmetic  11.4 us (7%)
  local copies, waits for them, and re-layouts  5.12 us (3%)
    pallas_call x1, Pallas kernels, backward(): pl.pallas_call(functools.partial(backward_kernel, G, T, h, across, nf, st...  94.9 us
    pallas_call x1, Pallas kernels, forward(): pl.pallas_call(functools.partial(forward_kernel, G, T, h, across, nf, zs,...  58.5 us

profile of v6, /device:TPU:0, one launch (start us, length us, event | category | flops | bytes accessed | tf_op | source)
XLA Modules:
  0.0 170.7 jit_solution(8279483423371996900)
XLA Ops:
  0.6 0.8 copy.38
  1.4 0.1 pad_add_fusion
  1.5 0.6 broadcast_subtract_fusion.ext
  2.1 58.5 %forward.1 = (bf16[16,64,768]{2,1,0:T(8,128)(2,1)}, bf16[4096,1536]{1,0:T(8,128)(2,1)}, bf16[4096,1536]{1,0:T(8,128)(2,1)}, bf16[16,512,384]{2,1,0:T(8,128)(2,1)...) custom-call(s32[16,2]{1,0:T(8,128)} %broadcast_subtract_fusion.ext, ...), custom_call_target="tpu_custom_call" | custom-call | tf_op jit(solution)/shard_map/forward/pallas_call | solution.py:304
  60.6 94.9 %backward.1 = (bf16[16,256,384]{2,1,0:T(8,128)(2,1)}, bf16[16,96,384]{2,1,0:T(8,128)(2,1)}, bf16[16,96,384]{2,1,0:T(8,128)(2,1)}, bf16[1536,768]{1,0:T(8,128)(2,...) custom-call(s32[16,2]{1,0:T(8,128)} %broadcast_subtract_fusion.ext, s32[16]{0:T(128)} %keep.3, ...), custom_call_target="tpu_custom_call" | custom-call | tf_op jit(solution)/shard_map/backward/pallas_call | solution.py:766
  155.5 0.0 copy-start.1
  155.5 1.6 broadcast_select_fusion
  157.2 0.6 copy-done.1
  157.8 0.0 copy-start.6
  157.8 0.0 copy-start.4
  157.8 2.5 %fusion.1 = bf16[16,8,32,384]{3,2,1,0:T(8,128)(2,1)} fusion(bf16[16,8,32,384]{3,2,1,0:T(8,128)(2,1)S(1)} %bitcast.39, bf16[16,3,32,384]{3,2,1,0:T(8,128)(2,1)S(1)} %bitcast.37, bf16[16,3,32,384]{3,2,1,0:T(8,128)(2,1)S(1)} %bitcast.38), kind=kLoop, calls=%fused_computation.2 | loop fusion | flops 9437184 | bytes 8650752 | tf_op jit(solution)/shard_map/convert_element_type | solution.py:840
  160.2 0.0 copy-start
  160.2 0.0 copy-start.5
  160.2 0.0 copy-done.6
  160.2 0.6 slice_bitcast_fusion
  160.9 0.6 slice_bitcast_fusion.3
  161.5 0.0 copy-done.4
  161.5 1.7 convert_element_type.34
  163.2 0.6 slice_bitcast_fusion.1
  163.8 0.0 copy-done
  163.8 0.0 copy-done.5
  163.8 0.0 copy-start.7
  163.8 0.0 copy-start.8
  163.8 0.0 copy-start.2
  163.8 1.8 %multiply_reduce_fusion = (f32[384]{0:T(512)S(1)}, f32[1536,384]{1,0:T(8,128)}) fusion(bf16[1536,384]{1,0:T(8,128)(2,1)S(1)} %copy-done, bf16[1536,384]{1,0:T(8,128)(2,1)S(1)} %copy-done.5), kind=kLoop, calls=%fused_computation.3 | loop fusion | flops 2358912 | bytes 4720128 | tf_op jit(solution)/shard_map/reduce_sum | solution.py:848
  165.6 0.0 copy-done.7
  165.6 0.0 copy-done.8
  165.6 0.6 add_divide_fusion
  166.2 0.2 copy-done.2
  166.3 0.0 copy-start.3
  166.3 2.6 %convert.3 = f32[2,2,384,768]{3,2,1,0:T(8,128)} convert(bf16[2,2,384,768]{3,2,1,0:T(8,128)(2,1)S(1)} %bitcast.40) | non-fusion elementwise | flops 1179648 | bytes 7077888 | tf_op jit(solution)/shard_map/reshape | solution.py:852
  168.9 0.6 slice_bitcast_fusion.2
  169.5 0.0 copy-done.3
  169.5 1.1 copy.40
Async XLA Ops:
  155.5 2.2 %copy-start.1 = (bf16[16,256,384]{2,1,0:T(8,128)(2,1)S(1)}, bf16[16,256,384]{2,1,0:T(8,128)(2,1)}, u32[]{:S(2)}) copy-start(bf16[16,256,384]{2,1,0:T(8,128)(2,1)} %get-tuple-element.42) | copy-start | bytes 9437188
  157.8 2.5 %copy-start.6 = (f32[64,512]{1,0:T(8,128)S(1)}, f32[64,512]{1,0:T(8,128)}, u32[]{:S(2)}) copy-start(f32[64,512]{1,0:T(8,128)} %get-tuple-element.45) | copy-start | bytes 393220
  157.8 3.7 %copy-start.4 = (bf16[384,1536]{1,0:T(8,128)(2,1)S(1)}, bf16[384,1536]{1,0:T(8,128)(2,1)}, u32[]{:S(2)}) copy-start(bf16[384,1536]{1,0:T(8,128)(2,1)} %get-tuple-element.46) | copy-start | bytes 3538948
  160.2 3.5 %copy-start = (bf16[1536,384]{1,0:T(8,128)(2,1)S(1)}, bf16[1536,384]{1,0:T(8,128)(2,1)}, u32[]{:S(2)}) copy-start(bf16[1536,384]{1,0:T(8,128)(2,1)} %pw_far.3) | copy-start | bytes 3538948
  160.2 3.5 %copy-start.5 = (bf16[1536,384]{1,0:T(8,128)(2,1)S(1)}, bf16[1536,384]{1,0:T(8,128)(2,1)}, u32[]{:S(2)}) copy-start(bf16[1536,384]{1,0:T(8,128)(2,1)} %get-tuple-element.47) | copy-start | bytes 3538948
  163.8 1.8 %copy-start.7 = (f32[384]{0:T(512)S(1)}, f32[384]{0:T(512)}, u32[]{:S(2)}) copy-start(f32[384]{0:T(512)} %v3.3) | copy-start | bytes 4612
  163.8 1.8 %copy-start.8 = (f32[384]{0:T(512)S(1)}, f32[384]{0:T(512)}, u32[]{:S(2)}) copy-start(f32[384]{0:T(512)} %v4.3) | copy-start | bytes 4612
  163.8 2.5 %copy-start.2 = (bf16[1536,768]{1,0:T(8,128)(2,1)S(1)}, bf16[1536,768]{1,0:T(8,128)(2,1)}, u32[]{:S(2)}) copy-start(bf16[1536,768]{1,0:T(8,128)(2,1)} %get-tuple-element.48) | copy-start | bytes 7077892
  166.3 3.2 %copy-start.3 = (bf16[16,64,768]{2,1,0:T(8,128)(2,1)S(1)}, bf16[16,64,768]{2,1,0:T(8,128)(2,1)}, u32[]{:S(2)}) copy-start(bf16[16,64,768]{2,1,0:T(8,128)(2,1)} %get-tuple-element.32) | copy-start | bytes 4718596

commit v7 on v6

--- a/solution.py
+++ b/solution.py
@@ -144,8 +144,8 @@
 def forward_kernel(
     G, T, h, across, nf, zs, steps,
     ext, keep, tok, own, cot, fwd, inv, taps, dwk, v0, v1, v2, v3, v4, v5, v6, v7, v8, ew_far, pw_far, dw_far,
-    out, act, slope, xhat, fh_out, nm, inv1_out, sh_out, inv2_out, gdw,
-    top, bot, spec, vec, red, gdw_s, ew, pw, dw, sem, weight_sem,
+    out, act, slope, xhat, fh_out, nm, inv1_out, sh_out, inv2_out, gdw, spec,
+    top, bot, vec, red, gdw_s, ew, pw, dw, sem, weight_sem,
 ):
     g = pl.program_id(0)
     pixels = h * across
@@ -307,16 +307,16 @@
         in_specs=[smem, smem, far, img(pixels, C), img(Q, CO)] + [whole(a) for a in consts[:-3]] + [far] * 3,
         out_specs=[
             img(Q, CO), pix(HID), pix(HID), img(2 * nf, C), pix(C), pix(C), pix(128), pix(C), pix(128),
-            pl.BlockSpec((4 * C, CO), lambda g: (0, 0)),
+            pl.BlockSpec((4 * C, CO), lambda g: (0, 0)), pl.BlockSpec((2 * nf, C), lambda g: (0, 0)),
         ],
         out_shape=[
             sds((n_img, Q, CO), bf16), sds((NP, HID), bf16), sds((NP, HID), bf16), sds((n_img, 2 * nf, C), bf16),
             sds((NP, C), bf16), sds((NP, C), bf16), sds((NP, 128), f32), sds((NP, C), bf16), sds((NP, 128), f32),
-            sds((4 * C, CO), sum_type),
+            sds((4 * C, CO), sum_type), sds((2 * nf, C), f32),
         ],
         scratch_shapes=[
             pltpu.VMEM((n_img, 3 * across, C), bf16), pltpu.VMEM((n_img, 3 * across, C), bf16),
-            pltpu.VMEM((2 * nf, C), f32), pltpu.VMEM((16, C), f32), pltpu.VMEM((C // 128, G * h // 2, 2, across, 128), f32),
+            pltpu.VMEM((16, C), f32), pltpu.VMEM((C // 128, G * h // 2, 2, across, 128), f32),
             pltpu.VMEM((4 * C, CO), f32), pltpu.VMEM((C, HID), bf16), pltpu.VMEM((HID, C), bf16), pltpu.VMEM((4 * C, CO), bf16),
             pltpu.SemaphoreType.DMA((2, 2, n_img // T)), pltpu.SemaphoreType.DMA((3,)),
         ],
@@ -495,7 +495,7 @@
 def backward_kernel(
     G, T, h, across, nf, steps, zs, stages,
     ext, keep, cot, sh_in, inv2, act, slope, nm, fh_in, inv1, xhat, gdw_far,
-    dw_far, v0, v1, v2, v3, v4, v5, v6, v7, v8, pw_far, ew_far, fwd_own, inv_all, taps, dwk, back,
+    dw_far, v0, v1, v2, v3, v4, v5, v6, v7, v8, pw_far, ew_far, fwd_own, inv_all, spec_far, back,
     own_out, top_in, bot_in, gdw_out, gpw_out, gew_out, small_out,
     held, gres_s, gn_s, gr_s, acc, spec, vec, gpw, gew, geb, vsum, small, gdw_own, dw, pw, ew, weight_sem, halo_sem, *sums,
 ):
@@ -520,7 +520,7 @@
 
     weights = [
         pltpu.make_async_copy(src, dst, weight_sem.at[k])
-        for k, (src, dst) in enumerate(((dw_far, dw), (gdw_far, gdw_own), (pw_far, pw), (ew_far, ew)))
+        for k, (src, dst) in enumerate(((dw_far, dw), (gdw_far, gdw_own), (pw_far, pw), (ew_far, ew), (spec_far, spec)))
     ]
 
     @pl.when(step == 0)
@@ -532,7 +532,6 @@
             pl.semaphore_signal(barrier, inc=1, device_id=where, device_id_type=MESH)
         for ref in (gpw, gew, geb, vsum, acc):
             ref[...] = jnp.zeros_like(ref)
-        spec[...] = dot_exact(taps[...], tap_rows(dwk))
         stack_vectors(vec, (v0, v1, v2, v3, v4, v5, v6, v7, v8))
         weights[0].wait()
 
@@ -617,10 +616,10 @@
                 gn = term if gn is None else gn + term
             gn_s[pl.ds(pl.multiple_of(g * (G * pixels) + team * T * pixels, T * pixels), T * pixels), :] = gn
 
-    def halo(target, g, side, where):
-        part, edge = pl.ds(pl.multiple_of(g * G, G), G), 3 * across
+    def halo(target, n, side, where):
+        part, edge = pl.ds(pl.multiple_of(n * T, T), T), 3 * across
         src = held.at[part, pl.ds(side * edge, edge)]
-        return remote(src, target.at[part], halo_sem.at[0, side, g], halo_sem.at[1, side, g], where)
+        return remote(src, target.at[part], halo_sem.at[0, side, n], halo_sem.at[1, side, n], where)
 
     def up(g):
         return halo(bot_in, g, 0, place.above)
@@ -666,8 +665,9 @@
                 own = gres_s[pl.ds(pl.multiple_of(b * pixels, pixels), pixels), :].astype(f32)
                 own_out[team * T + t] = (each[edge : edge + pixels] + own).astype(bf16)
                 held[b, edge : 2 * edge] = each[edge + pixels :].astype(bf16)
-        pl.when(place.z > 0)(lambda: up(g).start())
-        pl.when(place.z < zs - 1)(lambda: down(g).start())
+            n = g * (G // T) + team
+            pl.when(place.z > 0)(lambda n=n: up(n).start())
+            pl.when(place.z < zs - 1)(lambda n=n: down(n).start())
 
     @pl.when(step == 3 * steps - 1)
     def _():
@@ -688,13 +688,13 @@
 
         @pl.when(place.z > 0)
         def _():
-            for g in range(steps):
+            for g in range(steps * (G // T)):
                 up(g).wait_send()
                 down(g).wait_recv()
 
         @pl.when(place.z < zs - 1)
         def _():
-            for g in range(steps):
+            for g in range(steps * (G // T)):
                 down(g).wait_send()
                 up(g).wait_recv()
 
@@ -772,7 +772,8 @@
         ]
         + [whole(a) for a in consts[1:10]]
         + [any_space] * 2
-        + [whole(a) for a in consts[12:]],
+        + [whole(a) for a in consts[12:14]]
+        + [any_space, whole(consts[15])],
         out_specs=[img(2 * steps, pixels, C)] + [any_space] * 6,
         out_shape=[
             sds((n_img, pixels, C), bf16), sds((n_img, 3 * across, C), bf16), sds((n_img, 3 * across, C), bf16),
@@ -784,7 +785,7 @@
             pltpu.VMEM((2 * nf, C), f32), pltpu.VMEM((2 * nf, C), f32), pltpu.VMEM((16, C), f32), pltpu.VMEM((C, HID), f32), pltpu.VMEM((C, HID), f32),
             pltpu.VMEM((1, HID), f32), pltpu.VMEM((8, C), f32), pltpu.VMEM(SMALL, f32),
             pltpu.VMEM(gdw.shape, gdw.dtype), pltpu.VMEM((4 * C, CO), bf16), pltpu.VMEM((HID, C), bf16), pltpu.VMEM((C, HID), bf16),
-            pltpu.SemaphoreType.DMA((4,)), pltpu.SemaphoreType.DMA((2, 2, steps)),
+            pltpu.SemaphoreType.DMA((5,)), pltpu.SemaphoreType.DMA((2, 2, n_img // T)),
         ]
         + sums,
         compiler_params=pltpu.CompilerParams(vmem_limit_bytes=VMEM, collective_id=0, has_side_effects=True),
@@ -816,13 +817,13 @@
     vectors = (
         dw_bias, norm_gain, norm_bias, project_bias, layer_scale, down_gain, down_shift, down_bias, expand_bias
     )
-    out, act, slope, xhat, fh, nm, inv1, sh, inv2, gdw = forward(
+    out, act, slope, xhat, fh, nm, inv1, sh, inv2, gdw, spec = forward(
         bf16 if fused else f32, n_sp,
         G, T, h, across, nf, n_img, ext, keep_mask, own, cot, fwd, inv, taps, dw_kernel, *vectors, expand_weight, project_weight, dw,
     )
     grad, from_above, from_below, gdw_sum, gpw, gew, small = backward(
         fused, n_sp, G, T, h, across, nf, n_img, ext, keep_mask, cot, sh, inv2, act, slope,
-        nm, fh, inv1, xhat, gdw, dw, *vectors, project_weight, expand_weight, fwd_own, inv_all, taps, dw_kernel, back,
+        nm, fh, inv1, xhat, gdw, dw, *vectors, project_weight, expand_weight, fwd_own, inv_all, spec, back,
     )
     if fused:
         gdw, gpw, gew = (a.astype(f32) for a in (gdw_sum, gpw, gew))

time: 171 us -> 170 us (level)
  no operation moved by 1% of the time
where the time goes in v7:
time: 170 us
  Pallas kernels  153 us (90%)
  other arithmetic  11.4 us (7%)
  local copies, waits for them, and re-layouts  5.12 us (3%)
    pallas_call x1, Pallas kernels, backward(): pl.pallas_call(functools.partial(backward_kernel, G, T, h, across, nf, st...  94.2 us
    pallas_call x1, Pallas kernels, forward(): pl.pallas_call(functools.partial(forward_kernel, G, T, h, across, nf, zs,...  58.7 us

profile of v7, /device:TPU:0, one launch (start us, length us, event | category | flops | bytes accessed | tf_op | source)
XLA Modules:
  0.0 170.2 jit_solution(15680946979077205750)
XLA Ops:
  0.6 0.8 copy.38
  1.4 0.1 pad_add_fusion
  1.5 0.6 broadcast_subtract_fusion.ext
  2.1 58.7 %forward.1 = (bf16[16,64,768]{2,1,0:T(8,128)(2,1)}, bf16[4096,1536]{1,0:T(8,128)(2,1)}, bf16[4096,1536]{1,0:T(8,128)(2,1)}, bf16[16,512,384]{2,1,0:T(8,128)(2,1)...) custom-call(s32[16,2]{1,0:T(8,128)} %broadcast_subtract_fusion.ext, ...), custom_call_target="tpu_custom_call" | custom-call | tf_op jit(solution)/shard_map/forward/pallas_call | solution.py:304
  60.8 94.2 %backward.1 = (bf16[16,256,384]{2,1,0:T(8,128)(2,1)}, bf16[16,96,384]{2,1,0:T(8,128)(2,1)}, bf16[16,96,384]{2,1,0:T(8,128)(2,1)}, bf16[1536,768]{1,0:T(8,128)(2,...) custom-call(s32[16,2]{1,0:T(8,128)} %broadcast_subtract_fusion.ext, s32[16]{0:T(128)} %keep.3, ...), custom_call_target="tpu_custom_call" | custom-call | tf_op jit(solution)/shard_map/backward/pallas_call | solution.py:766
  155.0 0.0 copy-start.1
  155.0 1.6 broadcast_select_fusion
  156.7 0.6 copy-done.1
  157.3 0.0 copy-start.6
  157.3 0.0 copy-start.4
  157.3 2.5 %fusion.1 = bf16[16,8,32,384]{3,2,1,0:T(8,128)(2,1)} fusion(bf16[16,8,32,384]{3,2,1,0:T(8,128)(2,1)S(1)} %bitcast.39, bf16[16,3,32,384]{3,2,1,0:T(8,128)(2,1)S(1)} %bitcast.37, bf16[16,3,32,384]{3,2,1,0:T(8,128)(2,1)S(1)} %bitcast.38), kind=kLoop, calls=%fused_computation.2 | loop fusion | flops 9437184 | bytes 8650752 | tf_op jit(solution)/shard_map/convert_element_type | solution.py:841
  159.7 0.0 copy-start
  159.7 0.0 copy-start.5
  159.7 0.0 copy-done.6
  159.8 0.6 slice_bitcast_fusion
  160.4 0.6 slice_bitcast_fusion.3
  161.0 0.0 copy-done.4
  161.0 1.7 convert_element_type.34
  162.7 0.6 slice_bitcast_fusion.1
  163.3 0.0 copy-done
  163.3 0.0 copy-done.5
  163.3 0.0 copy-start.7
  163.3 0.0 copy-start.8
  163.3 0.0 copy-start.2
  163.3 1.8 %multiply_reduce_fusion = (f32[384]{0:T(512)S(1)}, f32[1536,384]{1,0:T(8,128)}) fusion(bf16[1536,384]{1,0:T(8,128)(2,1)S(1)} %copy-done, bf16[1536,384]{1,0:T(8,128)(2,1)S(1)} %copy-done.5), kind=kLoop, calls=%fused_computation.3 | loop fusion | flops 2358912 | bytes 4720128 | tf_op jit(solution)/shard_map/reduce_sum | solution.py:849
  165.1 0.0 copy-done.7
  165.1 0.0 copy-done.8
  165.1 0.6 add_divide_fusion
  165.7 0.2 copy-done.2
  165.8 0.0 copy-start.3
  165.8 2.6 %convert.3 = f32[2,2,384,768]{3,2,1,0:T(8,128)} convert(bf16[2,2,384,768]{3,2,1,0:T(8,128)(2,1)S(1)} %bitcast.40) | non-fusion elementwise | flops 1179648 | bytes 7077888 | tf_op jit(solution)/shard_map/reshape | solution.py:853
  168.4 0.6 slice_bitcast_fusion.2
  169.0 0.0 copy-done.3
  169.0 1.1 copy.40
Async XLA Ops:
  155.0 2.2 %copy-start.1 = (bf16[16,256,384]{2,1,0:T(8,128)(2,1)S(1)}, bf16[16,256,384]{2,1,0:T(8,128)(2,1)}, u32[]{:S(2)}) copy-start(bf16[16,256,384]{2,1,0:T(8,128)(2,1)} %get-tuple-element.44) | copy-start | bytes 9437188
  157.3 2.5 %copy-start.6 = (f32[64,512]{1,0:T(8,128)S(1)}, f32[64,512]{1,0:T(8,128)}, u32[]{:S(2)}) copy-start(f32[64,512]{1,0:T(8,128)} %get-tuple-element.47) | copy-start | bytes 393220
  157.3 3.7 %copy-start.4 = (bf16[384,1536]{1,0:T(8,128)(2,1)S(1)}, bf16[384,1536]{1,0:T(8,128)(2,1)}, u32[]{:S(2)}) copy-start(bf16[384,1536]{1,0:T(8,128)(2,1)} %get-tuple-element.48) | copy-start | bytes 3538948
  159.7 3.5 %copy-start = (bf16[1536,384]{1,0:T(8,128)(2,1)S(1)}, bf16[1536,384]{1,0:T(8,128)(2,1)}, u32[]{:S(2)}) copy-start(bf16[1536,384]{1,0:T(8,128)(2,1)} %pw_far.3) | copy-start | bytes 3538948
  159.7 3.5 %copy-start.5 = (bf16[1536,384]{1,0:T(8,128)(2,1)S(1)}, bf16[1536,384]{1,0:T(8,128)(2,1)}, u32[]{:S(2)}) copy-start(bf16[1536,384]{1,0:T(8,128)(2,1)} %get-tuple-element.49) | copy-start | bytes 3538948
  163.3 1.8 %copy-start.7 = (f32[384]{0:T(512)S(1)}, f32[384]{0:T(512)}, u32[]{:S(2)}) copy-start(f32[384]{0:T(512)} %v3.3) | copy-start | bytes 4612
  163.3 1.8 %copy-start.8 = (f32[384]{0:T(512)S(1)}, f32[384]{0:T(512)}, u32[]{:S(2)}) copy-start(f32[384]{0:T(512)} %v4.3) | copy-start | bytes 4612
  163.3 2.5 %copy-start.2 = (bf16[1536,768]{1,0:T(8,128)(2,1)S(1)}, bf16[1536,768]{1,0:T(8,128)(2,1)}, u32[]{:S(2)}) copy-start(bf16[1536,768]{1,0:T(8,128)(2,1)} %get-tuple-element.50) | copy-start | bytes 7077892
  165.8 3.2 %copy-start.3 = (bf16[16,64,768]{2,1,0:T(8,128)(2,1)S(1)}, bf16[16,64,768]{2,1,0:T(8,128)(2,1)}, u32[]{:S(2)}) copy-start(bf16[16,64,768]{2,1,0:T(8,128)(2,1)} %get-tuple-element.33) | copy-start | bytes 4718596
